TPU v7x, 32 devices: a whole 2x2x4 slice. The times are simulated.
32 devices in a mesh: chan: 8 (over z, x), win: 4 (over y, core).
Axes of the slice: x: 2, y: 2, z: 4, core: 2. Of those that a mesh axis runs over, the one named last changes fastest.
Arguments:
- records: bfloat16 [10240, 102400], P('chan', 'win'), may hold values from -6 to 6
- offsets: int32 [32], P('win'), may hold values from 0 to 128
- src_index: int32 [4, 4], replicated, may hold values from 0 to 10239, as said below
- quality: int32 [10240], P('chan'), may hold values 0 or 1
Outputs:
- stacks: float32 [4, 196, 10240], P('win', None, 'chan')
Inputs may be any that keep to these rules, and one draw needn't show every extreme that they name: `src_index`: the 4 channels of one step are distinct and lie in one aligned block of 1280 channels; some step includes channel 0 and some other step the last channel.
All inputs are finite; a program needn't handle non-finite values. No bound on the sum of `quality` on one device may be relied on, other than what follows from the above.
Results may differ from a plain program's by a relative error of at most 0.0038.
Values may be sent and summed in bfloat16 or wider, within the bound.
No kernel may reach another device: no remote copies, remote signals or barrier semaphores. Data moves between devices by JAX's collectives and lax.ppermute only.
A program may use at most 320 MiB of HBM per device.

v0:
```python
import math

import jax
import jax.numpy as jnp
from jax import lax
from jax.sharding import PartitionSpec as P

L = 3072
LAGS = 49


EPSILON = 1e-06


def spread(value, axis, source):
    kept = jnp.where(lax.axis_index(axis) == source, value, 0).astype(value.dtype)
    return lax.psum(kept, axis)


def whiten(segment):
    values = segment.astype(jnp.float32)
    power = jnp.mean(values * values, axis=-1, keepdims=True)
    return (values / jnp.sqrt(power + EPSILON)).astype(jnp.bfloat16)


def lagged(source):
    half = (LAGS - 1) // 2
    length = source.shape[-1]
    widths = [(0, 0)] * (source.ndim - 1) + [(half, half)]
    padded = jnp.pad(source, widths)
    return jnp.stack(
        [padded[..., 2 * half - column : 2 * half - column + length] for column in range(LAGS)],
        axis=-2,
    )


def body(records, offsets, src_index, quality):
    channels = records.shape[0]
    seg_count = offsets.shape[0]
    stride = records.shape[1] // seg_count
    step_count = src_index.shape[0]
    src_count = src_index.shape[1]
    starts = jnp.arange(seg_count, dtype=jnp.int32) * stride + offsets

    def cut_segment(begin):
        return lax.dynamic_slice_in_dim(records, begin, L, 1)

    white = whiten(jax.vmap(cut_segment)(starts))
    owners = src_index[:, 0] // channels
    local_rows = src_index % channels
    received = []
    for number in range(step_count):
        candidate = jnp.take(white, local_rows[number], axis=1)
        received.append(spread(candidate, "chan", owners[number]))
    sources = jnp.stack(received)

    def step_term(source):
        shifted = lagged(source).reshape(seg_count, src_count * LAGS, L)
        return lax.dot_general(
            shifted, white, (((0, 2), (0, 2)), ((), ())), preferred_element_type=jnp.float32
        )

    terms = jnp.stack([step_term(sources[number]) for number in range(step_count)])
    summed = lax.psum_scatter(terms, "win", scatter_dimension=0, tiled=True)
    scale = 1.0 / math.sqrt(seg_count * lax.axis_size("win") * L)
    return summed * scale * quality.astype(jnp.float32)[None, None, :]


def solution(mesh):
    return jax.shard_map(
        body,
        mesh=mesh,
        in_specs=(P("chan", "win"), P("win"), P(), P("chan")),
        out_specs=P("win", None, "chan"),
        check_vma=False,
    )
```

profile of v0, /device:TPU:0, one launch (start us, length us, event | category | flops | bytes accessed | tf_op | source)
XLA Modules:
  0.0 759.8 jit_solution(15704916750470428453)
XLA Ops:
  9.5 97.7 %while.1 = (s32[]{:T(128)}, bf16[1280,25600]{1,0:T(8,128)(2,1)}, s32[8,2]{0,1:T(2,128)S(1)}, bf16[8,1280,3072]{2,1,0:T(8,128)(2,1)}, s32[]{:T(128)}) while((s32[]{:T(128)}, bf16[1280,25600]{1,0:T(8,128)(2,1)}, s32[8,2]{0,1:T(2,128)S(1)}, bf16[8,1280,3072]{2,1,0:T(8,128)(2,1)}, s32[]{:T(128)}) %tuple.32), condition=%wide.while_cond, body=%wide.while_body.sunk | while | flops 2 | bytes 15729753 | solution.py:46
  10.1 11.4 %bitcast_dynamic-update-slice_fusion.2 = bf16[8,1280,3072]{2,1,0:T(8,128)(2,1)} fusion(bf16[8,1280,3072]{2,1,0:T(8,128)(2,1)} %get-tuple-element.81, s32[]{:T(128)} %get-tuple-element.78, bf16[1280,25600]{1,0:T(8,128)(2,1)} %get-tuple-element.84, s32[]{:T(128)} %bitcast.440), kind=kLoop, calls=%fused_computation.4.clone.1 | loop fusion | bytes 15729664 | tf_op jit(solution)/shard_map/vmap()/gather
  22.2 11.5 %bitcast_dynamic-update-slice_fusion.2 = bf16[8,1280,3072]{2,1,0:T(8,128)(2,1)} fusion(bf16[8,1280,3072]{2,1,0:T(8,128)(2,1)} %get-tuple-element.81, s32[]{:T(128)} %get-tuple-element.78, bf16[1280,25600]{1,0:T(8,128)(2,1)} %get-tuple-element.84, s32[]{:T(128)} %bitcast.440), kind=kLoop, calls=%fused_computation.4.clone.1 | loop fusion | bytes 15729664 | tf_op jit(solution)/shard_map/vmap()/gather
  34.3 11.6 %bitcast_dynamic-update-slice_fusion.2 = bf16[8,1280,3072]{2,1,0:T(8,128)(2,1)} fusion(bf16[8,1280,3072]{2,1,0:T(8,128)(2,1)} %get-tuple-element.81, s32[]{:T(128)} %get-tuple-element.78, bf16[1280,25600]{1,0:T(8,128)(2,1)} %get-tuple-element.84, s32[]{:T(128)} %bitcast.440), kind=kLoop, calls=%fused_computation.4.clone.1 | loop fusion | bytes 15729664 | tf_op jit(solution)/shard_map/vmap()/gather
  46.5 11.7 %bitcast_dynamic-update-slice_fusion.2 = bf16[8,1280,3072]{2,1,0:T(8,128)(2,1)} fusion(bf16[8,1280,3072]{2,1,0:T(8,128)(2,1)} %get-tuple-element.81, s32[]{:T(128)} %get-tuple-element.78, bf16[1280,25600]{1,0:T(8,128)(2,1)} %get-tuple-element.84, s32[]{:T(128)} %bitcast.440), kind=kLoop, calls=%fused_computation.4.clone.1 | loop fusion | bytes 15729664 | tf_op jit(solution)/shard_map/vmap()/gather
  58.9 11.7 %bitcast_dynamic-update-slice_fusion.2 = bf16[8,1280,3072]{2,1,0:T(8,128)(2,1)} fusion(bf16[8,1280,3072]{2,1,0:T(8,128)(2,1)} %get-tuple-element.81, s32[]{:T(128)} %get-tuple-element.78, bf16[1280,25600]{1,0:T(8,128)(2,1)} %get-tuple-element.84, s32[]{:T(128)} %bitcast.440), kind=kLoop, calls=%fused_computation.4.clone.1 | loop fusion | bytes 15729664 | tf_op jit(solution)/shard_map/vmap()/gather
  71.3 11.6 %bitcast_dynamic-update-slice_fusion.2 = bf16[8,1280,3072]{2,1,0:T(8,128)(2,1)} fusion(bf16[8,1280,3072]{2,1,0:T(8,128)(2,1)} %get-tuple-element.81, s32[]{:T(128)} %get-tuple-element.78, bf16[1280,25600]{1,0:T(8,128)(2,1)} %get-tuple-element.84, s32[]{:T(128)} %bitcast.440), kind=kLoop, calls=%fused_computation.4.clone.1 | loop fusion | bytes 15729664 | tf_op jit(solution)/shard_map/vmap()/gather
  83.5 11.4 %bitcast_dynamic-update-slice_fusion.2 = bf16[8,1280,3072]{2,1,0:T(8,128)(2,1)} fusion(bf16[8,1280,3072]{2,1,0:T(8,128)(2,1)} %get-tuple-element.81, s32[]{:T(128)} %get-tuple-element.78, bf16[1280,25600]{1,0:T(8,128)(2,1)} %get-tuple-element.84, s32[]{:T(128)} %bitcast.440), kind=kLoop, calls=%fused_computation.4.clone.1 | loop fusion | bytes 15729664 | tf_op jit(solution)/shard_map/vmap()/gather
  95.5 11.7 %bitcast_dynamic-update-slice_fusion.2 = bf16[8,1280,3072]{2,1,0:T(8,128)(2,1)} fusion(bf16[8,1280,3072]{2,1,0:T(8,128)(2,1)} %get-tuple-element.81, s32[]{:T(128)} %get-tuple-element.78, bf16[1280,25600]{1,0:T(8,128)(2,1)} %get-tuple-element.84, s32[]{:T(128)} %bitcast.440), kind=kLoop, calls=%fused_computation.4.clone.1 | loop fusion | bytes 15729664 | tf_op jit(solution)/shard_map/vmap()/gather
  107.2 64.4 %fusion = f32[8,1280]{0,1:T(8,128)S(1)} fusion(bf16[8,1280,3072]{2,1,0:T(8,128)(2,1)} %get-tuple-element.13), kind=kLoop, calls=%fused_computation.8 | loop fusion | flops 94361600 | bytes 62955520 | tf_op jit(solution)/shard_map/reduce_sum | solution.py:22
  172.0 59.6 %fusion.1 = bf16[8,1280,3072]{2,0,1:T(8,128)(2,1)} fusion(f32[8,1280]{0,1:T(8,128)S(1)} %copy.41, bf16[8,1280,3072]{2,1,0:T(8,128)(2,1)} %get-tuple-element.13), kind=kLoop, calls=%fused_computation.9 | loop fusion | flops 94371840 | bytes 125870080 | tf_op jit(solution)/shard_map/convert_element_type | solution.py:23
  242.9 77.4 %all-reduce.8.cloned.1.call-done = (bf16[8,4,3072]{2,0,1:T(8,128)(2,1)}, bf16[8,4,3072]{2,0,1:T(8,128)(2,1)}, bf16[8,4,3072]{2,0,1:T(8,128)(2,1)}, bf16[8,4,3072]{2,0,1:T(8,128)(2,1)}) async-done(((bf16[8,4,3072]{2,0,1:T(8,128)(2,1)}, bf16[8,4,3072]{2,0,1:T(8,128)(2,1)}, bf16[8,4,3072]{2,0,1:T(8,128)(2,1)}, bf16[8,4,3072]{2,0,1:T(8,128)(2,1)}), (bf16[8,4,3072]{2,0,1:T(8,128)(2,1)}, ...) | async-done | bytes 786448 | tf_op jit(solution)/shard_map/psum | solution.py:17
  320.3 1.8 constant_dynamic-update-slice_fusion.48
  382.6 8.5 %copy.42 = bf16[8,4,49,3072]{3,0,2,1:T(8,128)(2,1)} copy(bf16[8,4,49,3072]{3,0,1,2:T(8,128)(2,1)} %constant_dynamic-update-slice_fusion) | data formatting | bytes 19267584 | tf_op jit(solution)/shard_map/stack | solution.py:31
  391.2 41.9 %fusion.14 = f32[1,196,1280]{2,1,0:T(8,128)S(1)} fusion(bf16[8,1280,3072]{2,0,1:T(8,128)(2,1)} %fusion.1, bf16[8,196,3072]{2,0,1:T(8,128)(2,1)} %bitcast.442), kind=kOutput, calls=%fused_computation.23 | convolution fusion | flops 12331253760 | bytes 73551872 | tf_op jit(solution)/shard_map/dot_general | solution.py:59
  472.2 8.5 %copy.45 = bf16[8,4,49,3072]{3,0,2,1:T(8,128)(2,1)} copy(bf16[8,4,49,3072]{3,0,1,2:T(8,128)(2,1)} %constant_dynamic-update-slice_fusion.49) | data formatting | bytes 19267584 | tf_op jit(solution)/shard_map/stack | solution.py:31
  480.7 42.1 %fusion.19 = f32[1,196,1280]{2,1,0:T(8,128)S(1)} fusion(bf16[8,1280,3072]{2,0,1:T(8,128)(2,1)} %fusion.1, bf16[8,196,3072]{2,0,1:T(8,128)(2,1)} %bitcast.443), kind=kOutput, calls=%fused_computation.24 | convolution fusion | flops 12331253760 | bytes 73551872 | tf_op jit(solution)/shard_map/dot_general | solution.py:59
  561.9 8.5 %copy.48 = bf16[8,4,49,3072]{3,0,2,1:T(8,128)(2,1)} copy(bf16[8,4,49,3072]{3,0,1,2:T(8,128)(2,1)} %constant_dynamic-update-slice_fusion.98) | data formatting | bytes 19267584 | tf_op jit(solution)/shard_map/stack | solution.py:31
  570.4 42.2 %fusion.24 = f32[1,196,1280]{2,1,0:T(8,128)S(1)} fusion(bf16[8,1280,3072]{2,0,1:T(8,128)(2,1)} %fusion.1, bf16[8,196,3072]{2,0,1:T(8,128)(2,1)} %bitcast.444), kind=kOutput, calls=%fused_computation.25 | convolution fusion | flops 12331253760 | bytes 73551872 | tf_op jit(solution)/shard_map/dot_general | solution.py:59
  651.8 8.4 %copy.51 = bf16[8,4,49,3072]{3,0,2,1:T(8,128)(2,1)} copy(bf16[8,4,49,3072]{3,0,1,2:T(8,128)(2,1)} %constant_dynamic-update-slice_fusion.147) | data formatting | bytes 19267584 | tf_op jit(solution)/shard_map/stack | solution.py:31
  660.2 42.5 %fusion.29 = f32[1,196,1280]{2,1,0:T(8,128)} fusion(bf16[8,1280,3072]{2,0,1:T(8,128)(2,1)} %fusion.1, bf16[8,196,3072]{2,0,1:T(8,128)(2,1)} %bitcast.441), kind=kOutput, calls=%fused_computation.26 | convolution fusion | flops 12331253760 | bytes 73551872 | tf_op jit(solution)/shard_map/dot_general | solution.py:59
  702.7 3.6 pad_maximum_fusion
  706.4 43.1 %reduce-scatter.2.cloned.1.call-done = f32[1,196,1280]{2,1,0:T(8,128)} async-done(((f32[4,196,1280]{2,1,0:T(8,128)}), f32[1,196,1280]{2,1,0:T(8,128)}) %reduce-scatter.2.cloned.1.call-update) | async-done | bytes 1003536 | tf_op jit(solution)/shard_map/reduce_scatter | solution.py:64
  750.7 2.0 copy.54
  (249 shorter events, 196.2 us)
Async XLA Ops:
  6.5 313.8 %all-reduce.8.cloned.1.call-start = ((), (), s32[]{:S(2)}) async-start(), calls=%async_computation.2 | async-start | bytes 1572864 | tf_op jit(solution)/shard_map/psum | solution.py:17
  242.3 507.2 %reduce-scatter.2.cloned.1.call-start = ((), (), s32[]{:S(2)}) async-start(), calls=%async_computation.1 | async-start | bytes 5120000 | tf_op jit(solution)/shard_map/reduce_scatter | solution.py:64
  320.3 43.1 %copy-start.3 = (bf16[8,4,3072]{2,0,1:T(8,128)(2,1)S(1)}, bf16[8,4,3072]{2,0,1:T(8,128)(2,1)}, u32[]{:S(2)}) copy-start(bf16[8,4,3072]{2,0,1:T(8,128)(2,1)} %get-tuple-element.25) | copy-start | bytes 589828
  391.2 41.9 %copy-start.2 = (bf16[8,4,3072]{2,0,1:T(8,128)(2,1)S(1)}, bf16[8,4,3072]{2,0,1:T(8,128)(2,1)}, u32[]{:S(2)}) copy-start(bf16[8,4,3072]{2,0,1:T(8,128)(2,1)} %get-tuple-element.24) | copy-start | bytes 589828
  480.7 42.1 %copy-start.1 = (bf16[8,4,3072]{2,0,1:T(8,128)(2,1)S(1)}, bf16[8,4,3072]{2,0,1:T(8,128)(2,1)}, u32[]{:S(2)}) copy-start(bf16[8,4,3072]{2,0,1:T(8,128)(2,1)} %get-tuple-element.23) | copy-start | bytes 589828
  570.4 42.2 %copy-start = (bf16[8,4,3072]{2,0,1:T(8,128)(2,1)S(1)}, bf16[8,4,3072]{2,0,1:T(8,128)(2,1)}, u32[]{:S(2)}) copy-start(bf16[8,4,3072]{2,0,1:T(8,128)(2,1)} %get-tuple-element.22) | copy-start | bytes 589828
  702.7 3.6 copy-start.4
Sparse Core Ops, SparseCore 0:
  242.4 77.8 all-reduce.7
  706.5 42.9 reduce-scatter.1
where the time goes:
time: 768 us; the launch traced here: 760 us
  local copies, waits for them, and re-layouts  320 us (42%)
  matrix products  169 us (22%)
  other arithmetic  134 us (17%)
  waiting for transfers between devices  121 us (16%)
  between operations  16.3 us (2%)
    unnamed x202, local copies, waits for them, and re-layouts  176 us
    dot_general x4, matrix products, step_term(): lax.dot_general(shifted, white, (((0, 2), (0, 2)), ((), ())), preferred_e...  169 us
    gather x24, local copies, waits for them, and re-layouts  97.6 us
    psum x1, waiting for transfers between devices, spread(): return lax.psum(kept, axis)  77.4 us
    reduce_sum x1, other arithmetic, whiten(): power = jnp.mean(values * values, axis=-1, keepdims=True)  64.4 us
    convert_element_type x1, other arithmetic, whiten(): return (values / jnp.sqrt(power + EPSILON)).astype(jnp.bfloat16)  59.6 us
    reduce_scatter x1, waiting for transfers between devices, body(): summed = lax.psum_scatter(terms, 'win', scatter_dimension=0, tiled=True)  43.1 us
    another operation x8, local copies, waits for them, and re-layouts, lagged(): jnp.stack([padded[..., 2 * half - column:2 * half - column + length] for...  37.3 us
  transfers between devices with their start and end apart: 2, of which 2 were waited for; matrix products, arithmetic and copies ran while one was open for 0% of the time, Pallas kernels for 0%

commit v1 on v0

v1 whole, which is shorter than its diff:
```python
import functools
import math

import jax
import jax.numpy as jnp
from jax import lax
from jax.experimental import pallas as pl
from jax.experimental.pallas import tpu as pltpu
from jax.sharding import PartitionSpec as P

L = 3072
LAGS = 49
HALF = (LAGS - 1) // 2
EVEN = HALF + 1
ODD = HALF
EPSILON = 1e-06
LANES = 128
TILES = L // LANES
PAIRS = TILES // 2
ROWS = 64
COLUMNS = 256


def lanes(rows, dtype=jnp.int32):
    return lax.broadcasted_iota(dtype, (rows, LANES), 1)


def source_kernel(offsets_ref, rows_ref, own_ref, out_ref):
    count = rows_ref.shape[0]
    seg_count = out_ref.shape[0]
    stride = rows_ref.shape[1] // seg_count
    lane = lanes(count)
    owned = own_ref[...] > 0

    def one(g, carry):
        off = offsets_ref[g]
        back = lax.rem(LANES - off, LANES)
        base = g * stride
        tiles = []
        for m in range(TILES + 1):
            start = pl.multiple_of(base + m * LANES, LANES)
            tiles.append(rows_ref[:, pl.ds(start, LANES)].astype(jnp.float32))
        cut = [jnp.where(lane < off, tiles[m + 1], tiles[m]) for m in range(TILES)]
        total = cut[0] * cut[0]
        for m in range(1, TILES):
            total = total + cut[m] * cut[m]
        power = jnp.sum(total, axis=1, keepdims=True) / L
        root = jnp.sqrt(power + EPSILON)
        for m in range(TILES):
            white = jnp.where(owned, pltpu.roll(cut[m], back, 1) / root, 0.0)
            out_ref[g, :, m * LANES : (m + 1) * LANES] = white.astype(jnp.bfloat16)
        return carry

    lax.fori_loop(0, seg_count, one, 0)


def phases(u_ref, seg, count):
    lane = lanes(count)
    even = lane % 2 == 0
    zero = jnp.zeros((count, LANES), jnp.float32)

    def tile(m):
        if m < 0 or m >= TILES:
            return zero
        return u_ref[seg, :, m * LANES : (m + 1) * LANES].astype(jnp.float32)

    plain, ahead, behind = [], [], []
    for p in range(-1, PAIRS + 1):
        low, high, before = tile(2 * p), tile(2 * p + 1), tile(2 * p - 1)
        low_on = pltpu.roll(low, 1, 1)
        high_on = pltpu.roll(high, 1, 1)
        before_on = pltpu.roll(before, 1, 1)
        plain.append(jnp.where(even, low, high_on))
        ahead.append(jnp.where(even, pltpu.roll(low, LANES - 1, 1) - low, high - high_on))
        late_low = jnp.where(lane == 0, before_on, low_on)
        late_high = jnp.where(lane == 0, low_on, high_on)
        behind.append(jnp.where(even, late_low - low, pltpu.roll(late_high, 1, 1) - high_on))
    return plain, ahead, behind


def build(tiles, lag_count, off, a_ref, count):
    lane = lanes(count)
    even = lane % 2 == 0
    shifted = []
    for p in range(PAIRS + 1):
        back = pltpu.roll(tiles[p], LANES - 1, 1)
        on = pltpu.roll(tiles[p + 1], 1, 1)
        shifted.append(jnp.where(even, back, on))
    now = jnp.concatenate(tiles[1 : PAIRS + 1], axis=0)
    early = jnp.concatenate(shifted[:PAIRS], axis=0)
    late = jnp.concatenate(shifted[1:], axis=0)
    wide = lanes(count * PAIRS)
    for index in range(lag_count):
        s = 2 * index - HALF
        if s > 0:
            z = jnp.where(wide >= LANES - s, early, now)
        elif s < 0:
            z = jnp.where(wide < -s, late, now)
        else:
            z = now
        z = pltpu.roll(z, lax.rem(off + (s + LANES), LANES), 1).astype(jnp.bfloat16)
        for p in range(PAIRS):
            a_ref[index * count : (index + 1) * count, p * LANES : (p + 1) * LANES] = z[
                p * count : (p + 1) * count
            ]


def prepare(x_ref, off, row, w_refs, at, sum_ref):
    lane = lanes(ROWS)
    early = lane < off
    even = lax.rem(lane + (LANES - off) % 2, 2) == 0
    total = jnp.zeros((ROWS, LANES), jnp.float32)
    first_ref, second_ref, both_ref = w_refs

    def tile(m):
        return x_ref[row : row + ROWS, m * LANES : (m + 1) * LANES]

    for p in range(PAIRS):
        a, b, c = tile(2 * p), tile(2 * p + 1), tile(2 * p + 2)
        low = jnp.where(early, b, a).astype(jnp.float32)
        high = jnp.where(early, c, b).astype(jnp.float32)
        total = total + low * low + high * high
        first = jnp.where(even, low, pltpu.roll(high, 1, 1))
        second = jnp.where(even, pltpu.roll(low, LANES - 1, 1), high)
        span = slice(p * LANES, (p + 1) * LANES)
        first_ref[at : at + ROWS, span] = first.astype(jnp.bfloat16)
        second_ref[at : at + ROWS, span] = second.astype(jnp.bfloat16)
        both_ref[at : at + ROWS, span] = (first + second).astype(jnp.bfloat16)
    sum_ref[at : at + ROWS, :] = total


def dot(a, b):
    return lax.dot_general(a, b, (((1,), (1,)), ((), ())), preferred_element_type=jnp.float32)


def stack_kernel(
    src_count, offsets_ref, win_ref, u_ref, x_ref, keep_ref, send_ref,
    a1, a2, a3, c1, c2, c3, w00, w01, w02, w10, w11, w12, s0, s1, stage,
):
    g = pl.program_id(0)
    last = pl.num_programs(0) - 1
    off = offsets_ref[g]
    channels = x_ref.shape[0]
    count = u_ref.shape[1]
    slots = (((w00, w01, w02), s0), ((w10, w11, w12), s1))
    blocks = [(c, min(COLUMNS, channels - c)) for c in range(0, channels, COLUMNS)]

    @pl.when(g == 0)
    def _():
        for c in (c1, c2, c3):
            c[...] = jnp.zeros_like(c)

    plain, ahead, behind = phases(u_ref, g, count)
    build(plain, EVEN, off, a1, count)
    build(ahead, EVEN, off, a2, count)
    build(behind, ODD, off, a3, count)

    def pieces(number):
        start, width = blocks[number]
        w_refs, sum_ref = slots[number % 2]
        return [
            functools.partial(prepare, x_ref, off, start + at, w_refs, at, sum_ref)
            for at in range(0, width, ROWS)
        ]

    for piece in pieces(0):
        piece()
    for number, (start, width) in enumerate(blocks):
        todo = pieces(number + 1) if number + 1 < len(blocks) else []
        (first, second, both), sum_ref = slots[number % 2]
        power = jnp.sum(jnp.transpose(sum_ref[:width, :]), axis=0, keepdims=True) / L
        gain = lax.rsqrt(power + EPSILON)
        for a, w, c in ((a1, both, c1), (a2, second, c2), (a3, first, c3)):
            term = dot(a[...], w[:width, :]) * gain
            for at in range(0, width, LANES):
                size = min(LANES, width - at)
                c[(start + at) // LANES, :, :size] += term[:, at : at + size]
            for piece in todo[:2]:
                piece()
            todo = todo[2:]

    @pl.when(g == last)
    def _():
        c2[...] += c1[...]
        c3[...] += c1[:, : ODD * count, :]
        for slot in range(4):
            step = win_ref[0] ^ slot
            out = send_ref if slot % 2 else keep_ref
            for start in range(0, channels, LANES):
                width = min(LANES, channels - start)
                evens, odds = c2.at[start // LANES], c3.at[start // LANES]
                for i in range(src_count):
                    row = step * src_count + i
                    here = i * LAGS
                    stage[pl.ds(here, EVEN, stride=2), :] = evens[pl.ds(row, EVEN, stride=count), :]
                    stage[pl.ds(here + 1, ODD, stride=2), :] = odds[pl.ds(row, ODD, stride=count), :]
                out[slot // 2, :, start : start + width] = stage[:, :width]


def exchange(value, axis, size):
    me = lax.axis_index(axis)

    def swap(v, bit):
        return lax.ppermute(v, axis, [(d, d ^ bit) for d in range(size)])

    half = value.shape[0] // 2
    low = me % 2 == 0
    one, two = value[:half], value[half:]
    mine = jnp.where(low, one, two) + swap(jnp.where(low, two, one), 1)
    bit = 2
    while bit < size:
        mine = mine + swap(mine, bit)
        bit *= 2
    other = swap(mine, 1)
    return jnp.concatenate([jnp.where(low, mine, other), jnp.where(low, other, mine)], axis=0)


def solution(mesh):
    chan = mesh.shape["chan"]
    win = mesh.shape["win"]

    def body(records, offsets, src_index, quality):
        channels, samples = records.shape
        seg_count = offsets.shape[0]
        stride = samples // seg_count
        step_count, src_count = src_index.shape
        count = step_count * src_count
        flat = src_index.reshape(-1)
        own = (flat // channels == lax.axis_index("chan")).astype(jnp.int32)[:, None]
        rows = jnp.take(records, flat % channels, axis=0)
        smem = pl.BlockSpec(memory_space=pltpu.SMEM)
        vmem = pl.BlockSpec(memory_space=pltpu.VMEM)
        sources = pl.pallas_call(
            source_kernel,
            out_shape=jax.ShapeDtypeStruct((seg_count, count, L), jnp.bfloat16),
            in_specs=[smem, vmem, vmem],
            out_specs=vmem,
            compiler_params=pltpu.CompilerParams(vmem_limit_bytes=32 * 2**20),
            name="sources",
        )(offsets, rows, own)
        sources = exchange(sources, "chan", chan)

        w = lax.axis_index("win").astype(jnp.int32).reshape(1)
        half = jax.ShapeDtypeStruct((2, src_count * LAGS, channels), jnp.float32)
        bf16 = functools.partial(pltpu.VMEM, dtype=jnp.bfloat16)
        f32 = functools.partial(pltpu.VMEM, dtype=jnp.float32)
        depth = L // 2
        groups = pl.cdiv(channels, LANES)
        keep, send = pl.pallas_call(
            functools.partial(stack_kernel, src_count),
            grid=(seg_count,),
            out_shape=(half, half),
            in_specs=[smem, smem, vmem, pl.BlockSpec((channels, stride), lambda g: (0, g))],
            out_specs=(vmem, vmem),
            scratch_shapes=[
                bf16((EVEN * count, depth)),
                bf16((EVEN * count, depth)),
                bf16((ODD * count, depth)),
                f32((groups, EVEN * count, LANES)),
                f32((groups, EVEN * count, LANES)),
                f32((groups, ODD * count, LANES)),
            ]
            + [bf16((COLUMNS, depth))] * 6
            + [f32((COLUMNS, LANES))] * 2
            + [f32((src_count * LAGS, LANES))],
            compiler_params=pltpu.CompilerParams(vmem_limit_bytes=56 * 2**20),
            cost_estimate=pl.CostEstimate(
                flops=2 * seg_count * (2 * EVEN + ODD) * count * depth * channels,
                bytes_accessed=records.size * 2,
                transcendentals=0,
            ),
            name="stacks",
        )(offsets, w, sources, records)

        def swap(v, bit):
            return lax.ppermute(v, "win", [(d, d ^ bit) for d in range(win)])

        pair = keep + swap(send, 1)
        total = pair[0] + swap(pair[1].astype(jnp.bfloat16), 2).astype(jnp.float32)
        scale = 1.0 / math.sqrt(seg_count * win * L)
        return (total * scale * quality.astype(jnp.float32)[None, :])[None]

    return jax.shard_map(
        body,
        mesh=mesh,
        in_specs=(P("chan", "win"), P("win"), P(), P("chan")),
        out_specs=P("win", None, "chan"),
        check_vma=False,
    )
```

time: 768 us -> 180 us (0.23); the launches traced: 760 us -> 180 us
  local copies, waits for them, and re-layouts: 320 us -> 8.35 us
  matrix products: 169 us -> 0 us
  other arithmetic: 134 us -> 3.33 us
  Pallas kernels: 0 us -> 98.4 us
  waiting for transfers between devices: 121 us -> 60 us
  between operations: 16.3 us -> 0.1 us
  starting transfers between devices: 0.63 us -> 9.53 us
    unnamed x202 -> x6, local copies, waits for them, and re-layouts: 176 us -> 0.01 us
    dot_general x4 -> x0, matrix products: 169 us -> none  [step_term(): lax.dot_general(shifted, white, (((0, 2), (0, 2)), ((), ())), preferred_e...]
    gather x28 -> x1, local copies, waits for them, and re-layouts: 103 us -> 3.23 us  [body(): rows = jnp.take(records, flat % channels, axis=0)]
    pallas_call x0 -> x2, Pallas kernels: none -> 98.4 us  [the longest x1 96.6 us: body(): pl.pallas_call(functools.partial(stack_kernel, src_count), grid=(seg_coun...]
    psum x1 -> x0, waiting for transfers between devices: 77.4 us -> none  [spread(): return lax.psum(kept, axis)]
    reduce_sum x1 -> x0, other arithmetic: 64.4 us -> none  [whiten(): power = jnp.mean(values * values, axis=-1, keepdims=True)]
    ppermute x0 -> x6, waiting for transfers between devices: none -> 60 us  [the longest x4 43 us: swap(): return lax.ppermute(v, axis, [(d, d ^ bit) for d in range(size)])]
    convert_element_type x1, other arithmetic: 59.6 us -> 0.01 us  [body(): (flat // channels == lax.axis_index('chan')).astype(jnp.int32)[:, None]]
  transfers between devices with their start and end apart: 2 -> 6, of which waited for: 2 -> 6; matrix products, arithmetic and copies ran while one was open for 0% -> 0% of each run, Pallas kernels for 0% -> 0%
where the time goes in v1:
time: 180 us
  Pallas kernels  98.4 us (55%)
  waiting for transfers between devices  60 us (33%)
  starting transfers between devices  9.53 us (5%)
  local copies, waits for them, and re-layouts  8.35 us (5%)
  other arithmetic  3.33 us (2%)
    pallas_call x1, Pallas kernels, body(): pl.pallas_call(functools.partial(stack_kernel, src_count), grid=(seg_coun...  96.6 us
    ppermute x4, waiting for transfers between devices, swap(): return lax.ppermute(v, axis, [(d, d ^ bit) for d in range(size)])  43 us
    ppermute x2, waiting for transfers between devices, swap(): return lax.ppermute(v, 'win', [(d, d ^ bit) for d in range(win)])  17 us
    ppermute x4, starting transfers between devices, swap(): return lax.ppermute(v, axis, [(d, d ^ bit) for d in range(size)])  8.65 us
  transfers between devices with their start and end apart: 6, of which 6 were waited for; matrix products, arithmetic and copies ran while one was open for 0% of the time, Pallas kernels for 0%

profile of v1, /device:TPU:0, one launch (start us, length us, event | category | flops | bytes accessed | tf_op | source)
XLA Modules:
  0.0 179.7 jit_solution(6898287230044701207)
XLA Ops:
  0.0 0.7 broadcast_divide_fusion
  0.9 0.7 sign_compare_fusion
  1.5 0.1 fusion.5
  1.8 3.2 %gather_fusion = bf16[16,25600]{1,0:T(8,128)(2,1)S(1)} fusion(bf16[1280,25600]{1,0:T(8,128)(2,1)} %x_ref.1, s32[1024]{0:T(1024)S(1)} %pad_clamp_fusion), kind=kCustom, calls=%fused_computation | custom fusion | bytes 1638464 | tf_op jit(solution)/shard_map/jit(_take)/gather | solution.py:230
  5.1 0.1 broadcast_select_fusion.rows_ref
  5.3 1.8 sources.1
  7.1 3.0 %collective-permute-start = (bf16[4,16,3072]{2,1,0:T(8,128)(2,1)S(1)}, bf16[4,16,3072]{2,1,0:T(8,128)(2,1)S(1)}, u32[]{:S(2)}, u32[]{:S(2)}) collective-permute-start(bf16[4,16,3072]{2,1,0:T(8,128)(2,1)S(1)} %broadcast_select_fusion.3), channel_id=1, source_target_pairs={{0,4},{4,0},{8,12},{12,8},{16,20},{20,16},{24,28},{28,24},{1,5},{5... | collective-permute-start | bytes 1179656 | tf_op jit(solution)/shard_map/ppermute | solution.py:204
  10.1 9.1 %collective-permute-done = bf16[4,16,3072]{2,1,0:T(8,128)(2,1)S(1)} collective-permute-done((bf16[4,16,3072]{2,1,0:T(8,128)(2,1)S(1)}, bf16[4,16,3072]{2,1,0:T(8,128)(2,1)S(1)}, u32[]{:S(2)}, u32[]{:S(2)}) %collective-permute-start) | collective-permute-done | bytes 393248 | tf_op jit(solution)/shard_map/ppermute | solution.py:204
  19.3 1.9 %collective-permute-start.1 = (bf16[4,16,3072]{2,1,0:T(8,128)(2,1)S(1)}, bf16[4,16,3072]{2,1,0:T(8,128)(2,1)S(1)}, u32[]{:S(2)}, u32[]{:S(2)}) collective-permute-start(bf16[4,16,3072]{2,1,0:T(8,128)(2,1)S(1)} %select_add_fusion), channel_id=1, source_target_pairs={{0,8},{4,12},{8,0},{12,4},{16,24},{20,28},{24,16},{28,20},{1,9},{5... | collective-permute-start | bytes 1179656 | tf_op jit(solution)/shard_map/ppermute | solution.py:204
  21.2 8.5 %collective-permute-done.1 = bf16[4,16,3072]{2,1,0:T(8,128)(2,1)S(1)} collective-permute-done((bf16[4,16,3072]{2,1,0:T(8,128)(2,1)S(1)}, bf16[4,16,3072]{2,1,0:T(8,128)(2,1)S(1)}, u32[]{:S(2)}, u32[]{:S(2)}) %collective-permute-start.1) | collective-permute-done | bytes 393248 | tf_op jit(solution)/shard_map/ppermute | solution.py:204
  29.7 0.1 add.65
  29.8 2.6 %collective-permute-start.2 = (bf16[4,16,3072]{2,1,0:T(8,128)(2,1)S(1)}, bf16[4,16,3072]{2,1,0:T(8,128)(2,1)S(1)}, u32[]{:S(2)}, u32[]{:S(2)}) collective-permute-start(bf16[4,16,3072]{2,1,0:T(8,128)(2,1)S(1)} %add.65), channel_id=1, source_target_pairs={{0,16},{4,20},{8,24},{12,28},{16,0},{20,4},{24,8},{28,12},{1,17},{... | collective-permute-start | bytes 1179656 | tf_op jit(solution)/shard_map/ppermute | solution.py:204
  32.3 16.2 %collective-permute-done.2 = bf16[4,16,3072]{2,1,0:T(8,128)(2,1)S(1)} collective-permute-done((bf16[4,16,3072]{2,1,0:T(8,128)(2,1)S(1)}, bf16[4,16,3072]{2,1,0:T(8,128)(2,1)S(1)}, u32[]{:S(2)}, u32[]{:S(2)}) %collective-permute-start.2) | collective-permute-done | bytes 393248 | tf_op jit(solution)/shard_map/ppermute | solution.py:204
  48.6 1.2 collective-permute-start.3
  49.8 9.2 %collective-permute-done.3 = bf16[4,16,3072]{2,1,0:T(8,128)(2,1)S(1)} collective-permute-done((bf16[4,16,3072]{2,1,0:T(8,128)(2,1)S(1)}, bf16[4,16,3072]{2,1,0:T(8,128)(2,1)S(1)}, u32[]{:S(2)}, u32[]{:S(2)}) %collective-permute-start.3) | collective-permute-done | bytes 393248 | tf_op jit(solution)/shard_map/ppermute | solution.py:204
  59.1 0.9 pad_maximum_fusion.u_ref
  60.0 96.6 %stacks.1 = (f32[2,196,1280]{2,1,0:T(8,128)}, f32[2,196,1280]{2,1,0:T(8,128)}) custom-call(s32[8]{0:T(128)} %offsets_ref.3, s32[1]{0:T(128)} %bitcast.win_ref, bf16[8,16,3072]{2,1,0:T(8,128)(2,1)} %pad_maximum_fusion.u_ref, bf16[1280,25600]{1,0:T(8,128)(2,1)} %x_ref.1), custom_call_target="tpu_custom_call" | custom-call | flops 37245419520 | bytes 65536000 | tf_op jit(solution)/shard_map/stacks/pallas_call | solution.py:249
  156.7 2.8 %copy.28 = f32[2,196,1280]{2,0,1:T(2,128)S(1)} copy(f32[2,196,1280]{2,1,0:T(8,128)} %get-tuple-element.8) | data formatting | bytes 4014080 | tf_op jit(solution)/shard_map/stacks/pallas_call | solution.py:249
  159.5 4.0 %collective-permute-done.4 = f32[2,196,1280]{2,0,1:T(2,128)S(1)} collective-permute-done((f32[2,196,1280]{2,0,1:T(2,128)S(1)}, f32[2,196,1280]{2,0,1:T(2,128)S(1)}, u32[]{:S(2)}, u32[]{:S(2)}) %collective-permute-start.4) | collective-permute-done | bytes 2007072 | tf_op jit(solution)/shard_map/ppermute | solution.py:276
  163.5 0.2 copy_add_fusion
  163.8 0.8 collective-permute-start.5
  164.7 13.0 %collective-permute-done.5 = bf16[196,1280]{1,0:T(8,128)(2,1)S(1)} collective-permute-done((bf16[196,1280]{1,0:T(8,128)(2,1)S(1)}, bf16[196,1280]{1,0:T(8,128)(2,1)S(1)}, u32[]{:S(2)}, u32[]{:S(2)}) %collective-permute-start.5) | collective-permute-done | bytes 501792 | tf_op jit(solution)/shard_map/ppermute | solution.py:276
  177.6 0.1 fusion.2
  177.7 2.0 %copy.30 = f32[1,196,1280]{2,0,1:T(1,128)} copy(f32[1,196,1280]{2,1,0:T(8,128)S(1)} %fusion.2) | data formatting | bytes 2007040 | tf_op jit(solution)/shard_map/broadcast_in_dim | solution.py:281
  (20 shorter events, 0.7 us)
Async XLA Ops:
  1.8 3.4 %copy-start = (s32[8]{0:T(128)S(1)}, s32[8]{0:T(128)}, u32[]{:S(2)}) copy-start(s32[8]{0:T(128)} %offsets_ref.3) | copy-start | bytes 100
  7.1 12.1 %collective-permute-start = (bf16[4,16,3072]{2,1,0:T(8,128)(2,1)S(1)}, bf16[4,16,3072]{2,1,0:T(8,128)(2,1)S(1)}, u32[]{:S(2)}, u32[]{:S(2)}) collective-permute-start(bf16[4,16,3072]{2,1,0:T(8,128)(2,1)S(1)} %broadcast_select_fusion.3), channel_id=1, source_target_pairs={{0,4},{4,0},{8,12},{12,8},{16,20},{20,16},{24,28},{28,24},{1,5},{5... | collective-permute-start | bytes 1179656 | tf_op jit(solution)/shard_map/ppermute | solution.py:204
  19.3 10.4 %collective-permute-start.1 = (bf16[4,16,3072]{2,1,0:T(8,128)(2,1)S(1)}, bf16[4,16,3072]{2,1,0:T(8,128)(2,1)S(1)}, u32[]{:S(2)}, u32[]{:S(2)}) collective-permute-start(bf16[4,16,3072]{2,1,0:T(8,128)(2,1)S(1)} %select_add_fusion), channel_id=1, source_target_pairs={{0,8},{4,12},{8,0},{12,4},{16,24},{20,28},{24,16},{28,20},{1,9},{5... | collective-permute-start | bytes 1179656 | tf_op jit(solution)/shard_map/ppermute | solution.py:204
  29.8 18.8 %collective-permute-start.2 = (bf16[4,16,3072]{2,1,0:T(8,128)(2,1)S(1)}, bf16[4,16,3072]{2,1,0:T(8,128)(2,1)S(1)}, u32[]{:S(2)}, u32[]{:S(2)}) collective-permute-start(bf16[4,16,3072]{2,1,0:T(8,128)(2,1)S(1)} %add.65), channel_id=1, source_target_pairs={{0,16},{4,20},{8,24},{12,28},{16,0},{20,4},{24,8},{28,12},{1,17},{... | collective-permute-start | bytes 1179656 | tf_op jit(solution)/shard_map/ppermute | solution.py:204
  48.6 10.4 %collective-permute-start.3 = (bf16[4,16,3072]{2,1,0:T(8,128)(2,1)S(1)}, bf16[4,16,3072]{2,1,0:T(8,128)(2,1)S(1)}, u32[]{:S(2)}, u32[]{:S(2)}) collective-permute-start(bf16[4,16,3072]{2,1,0:T(8,128)(2,1)S(1)} %add.66), channel_id=1, source_target_pairs={{0,4},{4,0},{8,12},{12,8},{16,20},{20,16},{24,28},{28,24},{1,5},{5... | collective-permute-start | bytes 1179656 | tf_op jit(solution)/shard_map/ppermute | solution.py:204
  156.7 6.9 %copy-start.1 = (f32[2,196,1280]{2,1,0:T(8,128)S(1)}, f32[2,196,1280]{2,1,0:T(8,128)}, u32[]{:S(2)}) copy-start(f32[2,196,1280]{2,1,0:T(8,128)} %get-tuple-element.7) | copy-start | bytes 6021124
  159.4 4.1 %collective-permute-start.4 = (f32[2,196,1280]{2,0,1:T(2,128)S(1)}, f32[2,196,1280]{2,0,1:T(2,128)S(1)}, u32[]{:S(2)}, u32[]{:S(2)}) collective-permute-start(f32[2,196,1280]{2,0,1:T(2,128)S(1)} %copy.28), channel_id=1, source_target_pairs={{0,1},{1,0},{2,3},{3,2},{4,5},{5,4},{6,7},{7,6},{8,9},{9,8},{10,11... | collective-permute-start | bytes 6021128 | tf_op jit(solution)/shard_map/ppermute | solution.py:276
  163.5 1.1 copy-start.2
  163.8 13.8 %collective-permute-start.5 = (bf16[196,1280]{1,0:T(8,128)(2,1)S(1)}, bf16[196,1280]{1,0:T(8,128)(2,1)S(1)}, u32[]{:S(2)}, u32[]{:S(2)}) collective-permute-start(bf16[196,1280]{1,0:T(8,128)(2,1)S(1)} %fusion.3), channel_id=1, source_target_pairs={{0,2},{1,3},{2,0},{3,1},{4,6},{5,7},{6,4},{7,5},{8,10},{9,11},{10,... | collective-permute-start | bytes 1505288 | tf_op jit(solution)/shard_map/ppermute | solution.py:276

commit v2 on v1

--- a/solution.py
+++ b/solution.py
@@ -18,7 +18,7 @@
 TILES = L // LANES
 PAIRS = TILES // 2
 ROWS = 64
-COLUMNS = 256
+COLUMNS = 512
 
 
 def lanes(rows, dtype=jnp.int32):
@@ -86,9 +86,9 @@
         back = pltpu.roll(tiles[p], LANES - 1, 1)
         on = pltpu.roll(tiles[p + 1], 1, 1)
         shifted.append(jnp.where(even, back, on))
-    now = jnp.concatenate(tiles[1 : PAIRS + 1], axis=0)
-    early = jnp.concatenate(shifted[:PAIRS], axis=0)
-    late = jnp.concatenate(shifted[1:], axis=0)
+    now = jnp.concatenate(tiles[1 : PAIRS + 1], axis=0).astype(jnp.bfloat16)
+    early = jnp.concatenate(shifted[:PAIRS], axis=0).astype(jnp.bfloat16)
+    late = jnp.concatenate(shifted[1:], axis=0).astype(jnp.bfloat16)
     wide = lanes(count * PAIRS)
     for index in range(lag_count):
         s = 2 * index - HALF
@@ -98,18 +98,37 @@
             z = jnp.where(wide < -s, late, now)
         else:
             z = now
-        z = pltpu.roll(z, lax.rem(off + (s + LANES), LANES), 1).astype(jnp.bfloat16)
+        z = pltpu.roll(z, lax.rem(off + (s + LANES), LANES), 1)
         for p in range(PAIRS):
             a_ref[index * count : (index + 1) * count, p * LANES : (p + 1) * LANES] = z[
                 p * count : (p + 1) * count
             ]
 
 
-def prepare(x_ref, off, row, w_refs, at, sum_ref):
+def power_kernel(offsets_ref, x_ref, gain_ref):
+    off = offsets_ref[pl.program_id(0)]
+    channels = x_ref.shape[0]
+    early = lanes(ROWS) < off
+    for row in range(0, channels, LANES):
+        sums = []
+        for at in range(row, min(row + LANES, channels), ROWS):
+            total = jnp.zeros((ROWS, LANES), jnp.float32)
+            now = x_ref[at : at + ROWS, :LANES]
+            for m in range(TILES):
+                later = x_ref[at : at + ROWS, (m + 1) * LANES : (m + 2) * LANES]
+                cut = jnp.where(early, later, now).astype(jnp.float32)
+                total = total + cut * cut
+                now = later
+            sums.append(total)
+        across = jnp.concatenate(sums, axis=0)
+        power = jnp.sum(jnp.transpose(across), axis=0, keepdims=True) / L
+        gain_ref[0, :, row : row + across.shape[0]] = lax.rsqrt(power + EPSILON)
+
+
+def prepare(x_ref, off, row, w_refs, at):
     lane = lanes(ROWS)
     early = lane < off
-    even = lax.rem(lane + (LANES - off) % 2, 2) == 0
-    total = jnp.zeros((ROWS, LANES), jnp.float32)
+    even = lax.rem(lane + off, 2) == 0
     first_ref, second_ref, both_ref = w_refs
 
     def tile(m):
@@ -117,16 +136,14 @@
 
     for p in range(PAIRS):
         a, b, c = tile(2 * p), tile(2 * p + 1), tile(2 * p + 2)
-        low = jnp.where(early, b, a).astype(jnp.float32)
-        high = jnp.where(early, c, b).astype(jnp.float32)
-        total = total + low * low + high * high
+        low = jnp.where(early, b, a)
+        high = jnp.where(early, c, b)
         first = jnp.where(even, low, pltpu.roll(high, 1, 1))
         second = jnp.where(even, pltpu.roll(low, LANES - 1, 1), high)
         span = slice(p * LANES, (p + 1) * LANES)
-        first_ref[at : at + ROWS, span] = first.astype(jnp.bfloat16)
-        second_ref[at : at + ROWS, span] = second.astype(jnp.bfloat16)
-        both_ref[at : at + ROWS, span] = (first + second).astype(jnp.bfloat16)
-    sum_ref[at : at + ROWS, :] = total
+        first_ref[at : at + ROWS, span] = first
+        second_ref[at : at + ROWS, span] = second
+        both_ref[at : at + ROWS, span] = first + second
 
 
 def dot(a, b):
@@ -134,15 +151,15 @@
 
 
 def stack_kernel(
-    src_count, offsets_ref, win_ref, u_ref, x_ref, keep_ref, send_ref,
-    a1, a2, a3, c1, c2, c3, w00, w01, w02, w10, w11, w12, s0, s1, stage,
+    src_count, offsets_ref, win_ref, u_ref, gain_ref, x_ref, keep_ref, send_ref,
+    a1, a2, a3, c1, c2, c3, w00, w01, w02, w10, w11, w12, stage,
 ):
     g = pl.program_id(0)
     last = pl.num_programs(0) - 1
     off = offsets_ref[g]
     channels = x_ref.shape[0]
     count = u_ref.shape[1]
-    slots = (((w00, w01, w02), s0), ((w10, w11, w12), s1))
+    slots = ((w00, w01, w02), (w10, w11, w12))
     blocks = [(c, min(COLUMNS, channels - c)) for c in range(0, channels, COLUMNS)]
 
     @pl.when(g == 0)
@@ -157,9 +174,8 @@
 
     def pieces(number):
         start, width = blocks[number]
-        w_refs, sum_ref = slots[number % 2]
         return [
-            functools.partial(prepare, x_ref, off, start + at, w_refs, at, sum_ref)
+            functools.partial(prepare, x_ref, off, start + at, slots[number % 2], at)
             for at in range(0, width, ROWS)
         ]
 
@@ -167,17 +183,17 @@
         piece()
     for number, (start, width) in enumerate(blocks):
         todo = pieces(number + 1) if number + 1 < len(blocks) else []
-        (first, second, both), sum_ref = slots[number % 2]
-        power = jnp.sum(jnp.transpose(sum_ref[:width, :]), axis=0, keepdims=True) / L
-        gain = lax.rsqrt(power + EPSILON)
+        first, second, both = slots[number % 2]
+        gain = gain_ref[g, :, start : start + width]
+        share = pl.cdiv(len(todo), 3)
         for a, w, c in ((a1, both, c1), (a2, second, c2), (a3, first, c3)):
             term = dot(a[...], w[:width, :]) * gain
             for at in range(0, width, LANES):
                 size = min(LANES, width - at)
                 c[(start + at) // LANES, :, :size] += term[:, at : at + size]
-            for piece in todo[:2]:
+            for piece in todo[:share]:
                 piece()
-            todo = todo[2:]
+            todo = todo[share:]
 
     @pl.when(g == last)
     def _():
@@ -239,6 +255,19 @@
             name="sources",
         )(offsets, rows, own)
         sources = exchange(sources, "chan", chan)
+        segment = pl.BlockSpec((channels, stride), lambda g: (0, g))
+        gain = pl.pallas_call(
+            power_kernel,
+            grid=(seg_count,),
+            out_shape=jax.ShapeDtypeStruct((seg_count, 1, channels), jnp.float32),
+            in_specs=[smem, segment],
+            out_specs=pl.BlockSpec((1, 1, channels), lambda g: (g, 0, 0)),
+            compiler_params=pltpu.CompilerParams(vmem_limit_bytes=32 * 2**20),
+            cost_estimate=pl.CostEstimate(
+                flops=2 * records.size, bytes_accessed=2 * records.size, transcendentals=0
+            ),
+            name="power",
+        )(offsets, records)
 
         w = lax.axis_index("win").astype(jnp.int32).reshape(1)
         half = jax.ShapeDtypeStruct((2, src_count * LAGS, channels), jnp.float32)
@@ -250,7 +279,7 @@
             functools.partial(stack_kernel, src_count),
             grid=(seg_count,),
             out_shape=(half, half),
-            in_specs=[smem, smem, vmem, pl.BlockSpec((channels, stride), lambda g: (0, g))],
+            in_specs=[smem, smem, vmem, vmem, segment],
             out_specs=(vmem, vmem),
             scratch_shapes=[
                 bf16((EVEN * count, depth)),
@@ -261,7 +290,6 @@
                 f32((groups, ODD * count, LANES)),
             ]
             + [bf16((COLUMNS, depth))] * 6
-            + [f32((COLUMNS, LANES))] * 2
             + [f32((src_count * LAGS, LANES))],
             compiler_params=pltpu.CompilerParams(vmem_limit_bytes=56 * 2**20),
             cost_estimate=pl.CostEstimate(
@@ -270,7 +298,7 @@
                 transcendentals=0,
             ),
             name="stacks",
-        )(offsets, w, sources, records)
+        )(offsets, w, sources, gain, records)
 
         def swap(v, bit):
             return lax.ppermute(v, "win", [(d, d ^ bit) for d in range(win)])

time: 180 us -> 165 us (0.917)
  waiting for transfers between devices: 60 us -> 50 us
  Pallas kernels: 98.4 us -> 92.2 us
    pallas_call x1, Pallas kernels: 96.6 us -> 65.4 us  [body(): pl.pallas_call(functools.partial(stack_kernel, src_count), grid=(seg_coun...]
    pallas_call x0 -> x1, Pallas kernels: none -> 25 us  [body(): pl.pallas_call(power_kernel, grid=(seg_count,), out_shape=jax.ShapeDtypeS...]
    ppermute x4, waiting for transfers between devices: 43 us -> 33.8 us  [swap(): return lax.ppermute(v, axis, [(d, d ^ bit) for d in range(size)])]
  transfers between devices with their start and end apart: 6 -> 6, of which waited for: 6 -> 5; matrix products, arithmetic and copies ran while one was open for 0% -> 0% of each run, Pallas kernels for 0% -> 15%
where the time goes in v2:
time: 165 us
  Pallas kernels  92.2 us (56%)
  waiting for transfers between devices  50 us (30%)
  starting transfers between devices  10.3 us (6%)
  local copies, waits for them, and re-layouts  8.96 us (5%)
  other arithmetic  3.33 us (2%)
    pallas_call x1, Pallas kernels, body(): pl.pallas_call(functools.partial(stack_kernel, src_count), grid=(seg_coun...  65.4 us
    ppermute x4, waiting for transfers between devices, swap(): return lax.ppermute(v, axis, [(d, d ^ bit) for d in range(size)])  33.8 us
    pallas_call x1, Pallas kernels, body(): pl.pallas_call(power_kernel, grid=(seg_count,), out_shape=jax.ShapeDtypeS...  25 us
    ppermute x2, waiting for transfers between devices, swap(): return lax.ppermute(v, 'win', [(d, d ^ bit) for d in range(win)])  16.2 us
    ppermute x4, starting transfers between devices, swap(): return lax.ppermute(v, axis, [(d, d ^ bit) for d in range(size)])  8.65 us
  transfers between devices with their start and end apart: 6, of which 5 were waited for; matrix products, arithmetic and copies ran while one was open for 0% of the time, Pallas kernels for 15%

profile of v2, /device:TPU:0, one launch (start us, length us, event | category | flops | bytes accessed | tf_op | source)
XLA Modules:
  0.0 164.9 jit_solution(2691853170485045597)
XLA Ops:
  0.0 0.7 broadcast_divide_fusion
  0.9 0.7 sign_compare_fusion
  1.5 0.1 fusion.5
  1.8 3.2 %gather_fusion = bf16[16,25600]{1,0:T(8,128)(2,1)S(1)} fusion(bf16[1280,25600]{1,0:T(8,128)(2,1)} %x_ref.3, s32[1024]{0:T(1024)S(1)} %pad_clamp_fusion), kind=kCustom, calls=%fused_computation | custom fusion | bytes 1638464 | tf_op jit(solution)/shard_map/jit(_take)/gather | solution.py:246
  5.1 0.1 broadcast_select_fusion.rows_ref
  5.3 1.8 %sources.1 = bf16[8,16,3072]{2,1,0:T(8,128)(2,1)S(1)} custom-call(s32[8]{0:T(128)S(1)} %copy-done.1, bf16[16,25600]{1,0:T(8,128)(2,1)S(1)} %broadcast_select_fusion.rows_ref, s32[16,1]{1,0:T(8,128)S(1)} %fusion.6.own_ref), custom_call_target="tpu_custom_call" | custom-call | tf_op jit(solution)/shard_map/sources/pallas_call | solution.py:249
  7.1 3.0 %collective-permute-start = (bf16[4,16,3072]{2,1,0:T(8,128)(2,1)S(1)}, bf16[4,16,3072]{2,1,0:T(8,128)(2,1)S(1)}, u32[]{:S(2)}, u32[]{:S(2)}) collective-permute-start(bf16[4,16,3072]{2,1,0:T(8,128)(2,1)S(1)} %broadcast_select_fusion.3), channel_id=1, source_target_pairs={{0,4},{4,0},{8,12},{12,8},{16,20},{20,16},{24,28},{28,24},{1,5},{5... | collective-permute-start | bytes 1179656 | tf_op jit(solution)/shard_map/ppermute | solution.py:220
  10.1 9.1 %collective-permute-done = bf16[4,16,3072]{2,1,0:T(8,128)(2,1)S(1)} collective-permute-done((bf16[4,16,3072]{2,1,0:T(8,128)(2,1)S(1)}, bf16[4,16,3072]{2,1,0:T(8,128)(2,1)S(1)}, u32[]{:S(2)}, u32[]{:S(2)}) %collective-permute-start) | collective-permute-done | bytes 393248 | tf_op jit(solution)/shard_map/ppermute | solution.py:220
  19.3 1.9 %collective-permute-start.1 = (bf16[4,16,3072]{2,1,0:T(8,128)(2,1)S(1)}, bf16[4,16,3072]{2,1,0:T(8,128)(2,1)S(1)}, u32[]{:S(2)}, u32[]{:S(2)}) collective-permute-start(bf16[4,16,3072]{2,1,0:T(8,128)(2,1)S(1)} %select_add_fusion), channel_id=1, source_target_pairs={{0,8},{4,12},{8,0},{12,4},{16,24},{20,28},{24,16},{28,20},{1,9},{5... | collective-permute-start | bytes 1179656 | tf_op jit(solution)/shard_map/ppermute | solution.py:220
  21.2 8.5 %collective-permute-done.1 = bf16[4,16,3072]{2,1,0:T(8,128)(2,1)S(1)} collective-permute-done((bf16[4,16,3072]{2,1,0:T(8,128)(2,1)S(1)}, bf16[4,16,3072]{2,1,0:T(8,128)(2,1)S(1)}, u32[]{:S(2)}, u32[]{:S(2)}) %collective-permute-start.1) | collective-permute-done | bytes 393248 | tf_op jit(solution)/shard_map/ppermute | solution.py:220
  29.8 2.6 %collective-permute-start.2 = (bf16[4,16,3072]{2,1,0:T(8,128)(2,1)S(1)}, bf16[4,16,3072]{2,1,0:T(8,128)(2,1)S(1)}, u32[]{:S(2)}, u32[]{:S(2)}) collective-permute-start(bf16[4,16,3072]{2,1,0:T(8,128)(2,1)S(1)} %add.65), channel_id=1, source_target_pairs={{0,16},{4,20},{8,24},{12,28},{16,0},{20,4},{24,8},{28,12},{1,17},{... | collective-permute-start | bytes 1179656 | tf_op jit(solution)/shard_map/ppermute | solution.py:220
  32.3 16.2 %collective-permute-done.2 = bf16[4,16,3072]{2,1,0:T(8,128)(2,1)S(1)} collective-permute-done((bf16[4,16,3072]{2,1,0:T(8,128)(2,1)S(1)}, bf16[4,16,3072]{2,1,0:T(8,128)(2,1)S(1)}, u32[]{:S(2)}, u32[]{:S(2)}) %collective-permute-start.2) | collective-permute-done | bytes 393248 | tf_op jit(solution)/shard_map/ppermute | solution.py:220
  48.6 1.2 collective-permute-start.3
  49.8 25.0 %power.1.gain_ref = f32[8,1,1280]{2,1,0:T(1,128)S(1)} custom-call(s32[8]{0:T(128)S(1)} %copy-done.1, bf16[1280,25600]{1,0:T(8,128)(2,1)} %x_ref.3), custom_call_target="tpu_custom_call" | custom-call | flops 65536000 | bytes 65536000 | tf_op jit(solution)/shard_map/power/pallas_call | solution.py:259
  74.9 0.6 copy-done
  75.5 0.9 pad_maximum_fusion.u_ref
  76.5 65.4 %stacks.1 = (f32[2,196,1280]{2,1,0:T(8,128)}, f32[2,196,1280]{2,1,0:T(8,128)}) custom-call(s32[8]{0:T(128)} %offsets_ref.5, s32[1]{0:T(128)} %bitcast.win_ref, bf16[8,16,3072]{2,1,0:T(8,128)(2,1)} %pad_maximum_fusion.u_ref, f32[8,1,1280]{2,1,0:T(1,128)} %copy-done, bf16[1280,25600]{1,0:T(8,128)(2,1)} %x_ref.3), custom_call_target="tpu_custom_call" | custom-call | flops 37245419520 | bytes 65536000 | tf_op jit(solution)/shard_map/stacks/pallas_call | solution.py:278
  141.9 2.8 %copy.28 = f32[2,196,1280]{2,0,1:T(2,128)S(1)} copy(f32[2,196,1280]{2,1,0:T(8,128)} %get-tuple-element.8) | data formatting | bytes 4014080 | tf_op jit(solution)/shard_map/stacks/pallas_call | solution.py:278
  144.7 4.0 %collective-permute-done.4 = f32[2,196,1280]{2,0,1:T(2,128)S(1)} collective-permute-done((f32[2,196,1280]{2,0,1:T(2,128)S(1)}, f32[2,196,1280]{2,0,1:T(2,128)S(1)}, u32[]{:S(2)}, u32[]{:S(2)}) %collective-permute-start.4) | collective-permute-done | bytes 2007072 | tf_op jit(solution)/shard_map/ppermute | solution.py:304
  148.7 0.2 copy_add_fusion
  149.0 1.6 collective-permute-start.5
  150.6 12.2 %collective-permute-done.5 = bf16[196,1280]{1,0:T(8,128)(2,1)S(1)} collective-permute-done((bf16[196,1280]{1,0:T(8,128)(2,1)S(1)}, bf16[196,1280]{1,0:T(8,128)(2,1)S(1)}, u32[]{:S(2)}, u32[]{:S(2)}) %collective-permute-start.5) | collective-permute-done | bytes 501792 | tf_op jit(solution)/shard_map/ppermute | solution.py:304
  162.8 0.1 fusion.2
  162.9 2.0 %copy.30 = f32[1,196,1280]{2,0,1:T(1,128)} copy(f32[1,196,1280]{2,1,0:T(8,128)S(1)} %fusion.2) | data formatting | bytes 2007040 | tf_op jit(solution)/shard_map/broadcast_in_dim | solution.py:309
  (23 shorter events, 0.8 us)
Async XLA Ops:
  1.8 3.4 %copy-start.1 = (s32[8]{0:T(128)S(1)}, s32[8]{0:T(128)}, u32[]{:S(2)}) copy-start(s32[8]{0:T(128)} %offsets_ref.5) | copy-start | bytes 100
  7.1 12.1 %collective-permute-start = (bf16[4,16,3072]{2,1,0:T(8,128)(2,1)S(1)}, bf16[4,16,3072]{2,1,0:T(8,128)(2,1)S(1)}, u32[]{:S(2)}, u32[]{:S(2)}) collective-permute-start(bf16[4,16,3072]{2,1,0:T(8,128)(2,1)S(1)} %broadcast_select_fusion.3), channel_id=1, source_target_pairs={{0,4},{4,0},{8,12},{12,8},{16,20},{20,16},{24,28},{28,24},{1,5},{5... | collective-permute-start | bytes 1179656 | tf_op jit(solution)/shard_map/ppermute | solution.py:220
  19.3 10.4 %collective-permute-start.1 = (bf16[4,16,3072]{2,1,0:T(8,128)(2,1)S(1)}, bf16[4,16,3072]{2,1,0:T(8,128)(2,1)S(1)}, u32[]{:S(2)}, u32[]{:S(2)}) collective-permute-start(bf16[4,16,3072]{2,1,0:T(8,128)(2,1)S(1)} %select_add_fusion), channel_id=1, source_target_pairs={{0,8},{4,12},{8,0},{12,4},{16,24},{20,28},{24,16},{28,20},{1,9},{5... | collective-permute-start | bytes 1179656 | tf_op jit(solution)/shard_map/ppermute | solution.py:220
  29.8 18.8 %collective-permute-start.2 = (bf16[4,16,3072]{2,1,0:T(8,128)(2,1)S(1)}, bf16[4,16,3072]{2,1,0:T(8,128)(2,1)S(1)}, u32[]{:S(2)}, u32[]{:S(2)}) collective-permute-start(bf16[4,16,3072]{2,1,0:T(8,128)(2,1)S(1)} %add.65), channel_id=1, source_target_pairs={{0,16},{4,20},{8,24},{12,28},{16,0},{20,4},{24,8},{28,12},{1,17},{... | collective-permute-start | bytes 1179656 | tf_op jit(solution)/shard_map/ppermute | solution.py:220
  48.6 26.8 %collective-permute-start.3 = (bf16[4,16,3072]{2,1,0:T(8,128)(2,1)S(1)}, bf16[4,16,3072]{2,1,0:T(8,128)(2,1)S(1)}, u32[]{:S(2)}, u32[]{:S(2)}) collective-permute-start(bf16[4,16,3072]{2,1,0:T(8,128)(2,1)S(1)} %add.66), channel_id=1, source_target_pairs={{0,4},{4,0},{8,12},{12,8},{16,20},{20,16},{24,28},{28,24},{1,5},{5... | collective-permute-start | bytes 1179656 | tf_op jit(solution)/shard_map/ppermute | solution.py:220
  74.8 0.6 copy-start
  141.9 6.9 %copy-start.2 = (f32[2,196,1280]{2,1,0:T(8,128)S(1)}, f32[2,196,1280]{2,1,0:T(8,128)}, u32[]{:S(2)}) copy-start(f32[2,196,1280]{2,1,0:T(8,128)} %get-tuple-element.7) | copy-start | bytes 6021124
  144.6 4.1 %collective-permute-start.4 = (f32[2,196,1280]{2,0,1:T(2,128)S(1)}, f32[2,196,1280]{2,0,1:T(2,128)S(1)}, u32[]{:S(2)}, u32[]{:S(2)}) collective-permute-start(f32[2,196,1280]{2,0,1:T(2,128)S(1)} %copy.28), channel_id=1, source_target_pairs={{0,1},{1,0},{2,3},{3,2},{4,5},{5,4},{6,7},{7,6},{8,9},{9,8},{10,11... | collective-permute-start | bytes 6021128 | tf_op jit(solution)/shard_map/ppermute | solution.py:304
  148.7 1.9 %copy-start.3 = (s32[1280]{0:T(1024)S(1)}, s32[1280]{0:T(1024)}, u32[]{:S(2)}) copy-start(s32[1280]{0:T(1024)} %param.7) | copy-start | bytes 15364
  149.0 13.8 %collective-permute-start.5 = (bf16[196,1280]{1,0:T(8,128)(2,1)S(1)}, bf16[196,1280]{1,0:T(8,128)(2,1)S(1)}, u32[]{:S(2)}, u32[]{:S(2)}) collective-permute-start(bf16[196,1280]{1,0:T(8,128)(2,1)S(1)} %fusion.3), channel_id=1, source_target_pairs={{0,2},{1,3},{2,0},{3,1},{4,6},{5,7},{6,4},{7,5},{8,10},{9,11},{10,... | collective-permute-start | bytes 1505288 | tf_op jit(solution)/shard_map/ppermute | solution.py:304

commit v3 on v2

v3 whole, which is shorter than its diff:
```python
import functools
import math

import jax
import jax.numpy as jnp
from jax import lax
from jax.experimental import pallas as pl
from jax.experimental.pallas import tpu as pltpu
from jax.sharding import PartitionSpec as P

L = 3072
LAGS = 49
HALF = (LAGS - 1) // 2
EVEN = HALF + 1
ODD = HALF
EPSILON = 1e-06
LANES = 128
TILES = L // LANES
PAIRS = TILES // 2
ROWS = 64
UNIT = 256


def lanes(rows, dtype=jnp.int32):
    return lax.broadcasted_iota(dtype, (rows, LANES), 1)


def source_kernel(offsets_ref, rows_ref, own_ref, out_ref):
    count = rows_ref.shape[0]
    seg_count = out_ref.shape[0]
    stride = rows_ref.shape[1] // seg_count
    lane = lanes(count)
    owned = own_ref[...] > 0

    def one(g, carry):
        off = offsets_ref[g]
        back = lax.rem(LANES - off, LANES)
        base = g * stride
        tiles = []
        for m in range(TILES + 1):
            start = pl.multiple_of(base + m * LANES, LANES)
            tiles.append(rows_ref[:, pl.ds(start, LANES)].astype(jnp.float32))
        cut = [jnp.where(lane < off, tiles[m + 1], tiles[m]) for m in range(TILES)]
        total = cut[0] * cut[0]
        for m in range(1, TILES):
            total = total + cut[m] * cut[m]
        power = jnp.sum(total, axis=1, keepdims=True) / L
        root = jnp.sqrt(power + EPSILON)
        for m in range(TILES):
            white = jnp.where(owned, pltpu.roll(cut[m], back, 1) / root, 0.0)
            out_ref[g, :, m * LANES : (m + 1) * LANES] = white.astype(jnp.bfloat16)
        return carry

    lax.fori_loop(0, seg_count, one, 0)


def phases(u_ref, seg, count):
    lane = lanes(count)
    even = lane % 2 == 0
    zero = jnp.zeros((count, LANES), jnp.float32)

    def tile(m):
        if m < 0 or m >= TILES:
            return zero
        return u_ref[seg, :, m * LANES : (m + 1) * LANES].astype(jnp.float32)

    plain, ahead, behind = [], [], []
    for p in range(-1, PAIRS + 1):
        low, high, before = tile(2 * p), tile(2 * p + 1), tile(2 * p - 1)
        low_on = pltpu.roll(low, 1, 1)
        high_on = pltpu.roll(high, 1, 1)
        before_on = pltpu.roll(before, 1, 1)
        plain.append(jnp.where(even, low, high_on))
        ahead.append(jnp.where(even, pltpu.roll(low, LANES - 1, 1) - low, high - high_on))
        late_low = jnp.where(lane == 0, before_on, low_on)
        late_high = jnp.where(lane == 0, low_on, high_on)
        behind.append(jnp.where(even, late_low - low, pltpu.roll(late_high, 1, 1) - high_on))
    return plain, ahead, behind


def builders(u_ref, seg, off, a_refs, count):
    lane = lanes(count)
    even = lane % 2 == 0
    wide = lanes(count * PAIRS)
    held = []

    def start():
        for tiles in phases(u_ref, seg, count):
            shifted = []
            for p in range(PAIRS + 1):
                back = pltpu.roll(tiles[p], LANES - 1, 1)
                on = pltpu.roll(tiles[p + 1], 1, 1)
                shifted.append(jnp.where(even, back, on))
            held.append(
                [
                    jnp.concatenate(part, axis=0).astype(jnp.bfloat16)
                    for part in (tiles[1 : PAIRS + 1], shifted[:PAIRS], shifted[1:])
                ]
            )

    def one(which, index):
        now, early, late = held[which]
        s = 2 * index - HALF
        if s > 0:
            z = jnp.where(wide >= LANES - s, early, now)
        elif s < 0:
            z = jnp.where(wide < -s, late, now)
        else:
            z = now
        z = pltpu.roll(z, lax.rem(off + (s + LANES), LANES), 1)
        for p in range(PAIRS):
            a_refs[which][index * count : (index + 1) * count, p * LANES : (p + 1) * LANES] = z[
                p * count : (p + 1) * count
            ]

    work = [start]
    for which, lag_count in enumerate((EVEN, EVEN, ODD)):
        work += [functools.partial(one, which, index) for index in range(lag_count)]
    return work


def power_kernel(begin, offsets_ref, x_ref, gain_ref):
    off = offsets_ref[begin + pl.program_id(0)]
    channels = x_ref.shape[0]
    early = lanes(ROWS) < off

    def square(at, m):
        value = x_ref[at : at + ROWS, m * LANES : (m + 1) * LANES].astype(jnp.float32)
        return value * value

    for row in range(0, channels, LANES):
        sums = []
        for at in range(row, min(row + LANES, channels), ROWS):
            total = jnp.where(early, square(at, TILES), square(at, 0))
            for m in range(1, TILES):
                total = total + square(at, m)
            sums.append(total)
        across = jnp.concatenate(sums, axis=0)
        power = jnp.sum(jnp.transpose(across), axis=0, keepdims=True) / L
        gain_ref[0, :, row : row + across.shape[0]] = lax.rsqrt(power + EPSILON)


def prepare(x_ref, base, off, row, w_refs, at):
    lane = lanes(ROWS)
    early = lane < off
    even = lax.rem(lane + off, 2) == 0
    first_ref, second_ref, both_ref = w_refs

    def tile(m):
        return x_ref[row : row + ROWS, base + m * LANES : base + (m + 1) * LANES]

    for p in range(PAIRS):
        a, b, c = tile(2 * p), tile(2 * p + 1), tile(2 * p + 2)
        low = jnp.where(early, b, a)
        high = jnp.where(early, c, b)
        first = jnp.where(even, low, pltpu.roll(high, 1, 1))
        second = jnp.where(even, pltpu.roll(low, LANES - 1, 1), high)
        span = slice(p * LANES, (p + 1) * LANES)
        first_ref[at : at + ROWS, span] = first
        second_ref[at : at + ROWS, span] = second
        both_ref[at : at + ROWS, span] = first + second


def dot(a, b):
    return lax.dot_general(a, b, (((1,), (1,)), ((), ())), preferred_element_type=jnp.float32)


def stack_kernel(src_count, blocks, begin, leads, *refs):
    refs = list(refs)

    def take(number):
        taken = refs[:number]
        del refs[:number]
        return taken

    units = sum(len(block) for block in blocks)
    offsets_ref, win_ref, gain_ref = take(3)
    if leads:
        (u_ref,) = take(1)
    else:
        shared = take(3)
    x_refs = take(units)
    keep_ref, send_ref = take(2)
    if leads:
        shared = take(3)
        a_slots = (take(3), take(3))
    c1, c2, c3 = take(3)
    w_slots = (take(3), take(3))
    (stage,) = take(1)
    if leads:
        (sems,) = take(1)

    n = pl.program_id(0)
    last = pl.num_programs(0) - 1
    unit, stride = x_refs[0].shape[0], x_refs[0].shape[1] // 2
    per_unit = pl.cdiv(unit, LANES)
    count = c1.shape[1] // EVEN
    offs = (offsets_ref[2 * n], offsets_ref[2 * n + 1])

    @pl.when(n == 0)
    def _():
        for c in (c1, c2, c3):
            c[...] = jnp.zeros_like(c)
        if leads:
            for piece in builders(u_ref, 0, offs[0], a_slots[0], count):
                piece()

    places = [(half, block) for half in (0, 1) for block in range(len(blocks))]

    def pieces(k):
        half, block = places[k]
        work = []
        for at, number in enumerate(blocks[block]):
            for row in range(0, unit, ROWS):
                work.append(
                    functools.partial(
                        prepare, x_refs[number], half * stride, offs[half], row,
                        w_slots[k % 2], at * unit + row,
                    )
                )
        return work

    def copies(half):
        return [
            pltpu.make_async_copy(a, out.at[2 * n + half], sems.at[i])
            for i, (a, out) in enumerate(zip(a_slots[half], shared))
        ]

    for piece in pieces(0):
        piece()
    built = []
    for k, (half, block) in enumerate(places):
        if leads and block == 0:
            for copy in copies(half):
                copy.start()
            later = 2 * n + 1 if half == 0 else lax.rem(2 * n + 2, 2 * last + 2)
            built = builders(u_ref, later, offsets_ref[later], a_slots[1 - half], count)
        slots_left = 3 * (len(blocks) - block)
        todo = pieces(k + 1) if k + 1 < len(places) else []
        first, second, both = w_slots[k % 2]
        width = unit * len(blocks[block])
        start = blocks[block][0] * unit
        gain = gain_ref[2 * n + half, :, begin + start : begin + start + width]
        operands = a_slots[half] if leads else [a.at[half] for a in shared]
        for i, (a, w, c) in enumerate(zip(operands, (both, second, first), (c1, c2, c3))):
            term = dot(a[...], w[:width, :]) * gain
            for at, number in enumerate(blocks[block]):
                for lane in range(0, unit, LANES):
                    size = min(LANES, unit - lane)
                    here = at * unit + lane
                    c[number * per_unit + lane // LANES, :, :size] += term[:, here : here + size]
            share = pl.cdiv(len(todo), 3 - i)
            built_share = pl.cdiv(len(built), slots_left - i)
            for piece in todo[:share] + built[:built_share]:
                piece()
            todo, built = todo[share:], built[built_share:]
        if leads and block == len(blocks) - 1:
            for copy in copies(half):
                copy.wait()

    @pl.when(n == last)
    def _():
        c2[...] += c1[...]
        c3[...] += c1[:, : ODD * count, :]
        for slot in range(4):
            step = win_ref[0] ^ slot
            out = send_ref if slot % 2 else keep_ref
            for group in range(units * per_unit):
                start = group // per_unit * unit + group % per_unit * LANES
                width = min(LANES, unit - group % per_unit * LANES)
                evens, odds = c2.at[group], c3.at[group]
                for i in range(src_count):
                    row = step * src_count + i
                    here = i * LAGS
                    stage[pl.ds(here, EVEN, stride=2), :] = evens[pl.ds(row, EVEN, stride=count), :]
                    stage[pl.ds(here + 1, ODD, stride=2), :] = odds[pl.ds(row, ODD, stride=count), :]
                out[slot // 2, :, start : start + width] = stage[:, :width]


def exchange(value, axis, size, offsets, works):
    me = lax.axis_index(axis)

    def swap(v, bit):
        return lax.ppermute(v, axis, [(d, d ^ bit) for d in range(size)])

    def scatter(v, bit):
        low = me & bit == 0
        half = v.shape[0] // 2
        one, two = v[:half], v[half:]
        return jnp.where(low, one, two) + swap(jnp.where(low, two, one), bit)

    def whole(v, bit):
        return v + swap(v, bit)

    def gather(v, bit):
        low = me & bit == 0
        other = swap(v, bit)
        return jnp.concatenate([jnp.where(low, v, other), jnp.where(low, other, v)], axis=0)

    bits = [1 << b for b in range(2, size.bit_length() - 1)]
    plans = [
        [(scatter, p), (scatter, q)] + [(whole, b) for b in bits] + [(gather, q), (gather, p)]
        for p, q in ((1, 2), (2, 1))
    ]
    half = value.shape[0] // 2
    values = [value[:half], value[half:]]
    results = []
    works = list(works)
    for index, steps in enumerate(zip(*plans)):
        values = [step(v, bit) for v, (step, bit) in zip(values, steps)]
        left = len(plans[0]) - index
        share = pl.cdiv(len(works), left)
        now = [work(offsets) for work in works[:share]]
        works = works[share:]
        if works:
            values, now, offsets = lax.optimization_barrier((values, now, offsets))
        results += now
    return jnp.concatenate(values, axis=0), results


def solution(mesh):
    chan = mesh.shape["chan"]
    win = mesh.shape["win"]

    def body(records, offsets, src_index, quality):
        channels, samples = records.shape
        seg_count = offsets.shape[0]
        stride = samples // seg_count
        step_count, src_count = src_index.shape
        count = step_count * src_count
        flat = src_index.reshape(-1)
        own = (lax.div(flat, channels) == lax.axis_index("chan")).astype(jnp.int32)[:, None]
        rows = jnp.take(records, lax.rem(flat, channels), axis=0, mode="clip")
        smem = pl.BlockSpec(memory_space=pltpu.SMEM)
        vmem = pl.BlockSpec(memory_space=pltpu.VMEM)
        sources = pl.pallas_call(
            source_kernel,
            out_shape=jax.ShapeDtypeStruct((seg_count, count, L), jnp.bfloat16),
            in_specs=[smem, vmem, vmem],
            out_specs=vmem,
            compiler_params=pltpu.CompilerParams(vmem_limit_bytes=32 * 2**20),
            name="sources",
        )(offsets, rows, own)

        def power(begin, number):
            return lambda starts: pl.pallas_call(
                functools.partial(power_kernel, begin),
                grid=(number,),
                out_shape=jax.ShapeDtypeStruct((number, 1, channels), jnp.float32),
                in_specs=[smem, pl.BlockSpec((channels, stride), lambda g: (0, begin + g))],
                out_specs=pl.BlockSpec((1, 1, channels), lambda g: (g, 0, 0)),
                compiler_params=pltpu.CompilerParams(vmem_limit_bytes=32 * 2**20),
                cost_estimate=pl.CostEstimate(
                    flops=2 * number * channels * stride,
                    bytes_accessed=2 * number * channels * stride,
                    transcendentals=0,
                ),
                name="power",
            )(starts, records)

        cuts = [0, 2, 3, 5, 6, seg_count]
        works = [power(a, b - a) for a, b in zip(cuts, cuts[1:])]
        sources, gains = exchange(sources, "chan", chan, offsets, works)
        gain = jnp.concatenate(gains, axis=0)

        w = lax.axis_index("win").astype(jnp.int32).reshape(1)
        bf16 = functools.partial(pltpu.VMEM, dtype=jnp.bfloat16)
        f32 = functools.partial(pltpu.VMEM, dtype=jnp.float32)
        depth = L // 2
        unit = UNIT if channels % UNIT == 0 else math.gcd(channels, ROWS)
        units = channels // unit
        lead = pl.cdiv(3 * units, 5)
        row_counts = (EVEN * count, EVEN * count, ODD * count)
        a_shapes = [jax.ShapeDtypeStruct((seg_count, r, depth), jnp.bfloat16) for r in row_counts]

        def stacks(blocks, begin, leads, operands):
            number = sum(len(block) for block in blocks)
            wide = number * unit
            half = jax.ShapeDtypeStruct((2, src_count * LAGS, wide), jnp.float32)
            sizes = [
                max([len(b) for b in (blocks + blocks)[parity::2]]) * unit for parity in (0, 1)
            ]

            def place(index):
                return pl.BlockSpec((unit, 2 * stride), lambda n: (begin // unit + index, n))

            any_space = pl.BlockSpec(memory_space=pl.ANY)
            given = (
                [vmem]
                if leads
                else [pl.BlockSpec((2, r, depth), lambda n: (n, 0, 0)) for r in row_counts]
            )
            return pl.pallas_call(
                functools.partial(stack_kernel, src_count, blocks, begin, leads),
                grid=(seg_count // 2,),
                out_shape=[half, half] + (a_shapes if leads else []),
                in_specs=[smem, smem, vmem] + given + [place(i) for i in range(number)],
                out_specs=[vmem, vmem] + ([any_space] * 3 if leads else []),
                scratch_shapes=([bf16((r, depth)) for r in row_counts] * 2 if leads else [])
                + [f32((number * pl.cdiv(unit, LANES), r, LANES)) for r in row_counts]
                + [bf16((size, depth)) for size in sizes for _ in range(3)]
                + [f32((src_count * LAGS, LANES))]
                + ([pltpu.SemaphoreType.DMA((3,))] if leads else []),
                compiler_params=pltpu.CompilerParams(vmem_limit_bytes=58 * 2**20),
                cost_estimate=pl.CostEstimate(
                    flops=2 * seg_count * sum(row_counts) * depth * wide,
                    bytes_accessed=2 * wide * samples,
                    transcendentals=0,
                ),
                name="stacks",
            )(offsets, w, gain, *operands, *([records] * number))

        def swap(v, bit):
            return lax.ppermute(v, "win", [(d, d ^ bit) for d in range(win)])

        def combine(keep, send):
            pair = keep + swap(send, 1)
            return pair[0] + swap(pair[1].astype(jnp.bfloat16), 2).astype(jnp.float32)

        rest = units - lead
        lead_blocks = [[0], list(range(1, lead))] if lead > 1 else [[0]]
        keep, send, *operands = stacks(lead_blocks, 0, True, [sources])
        totals = [combine(keep, send)]
        if rest:
            keep, send = stacks([list(range(rest))], lead * unit, False, operands)
            totals.append(combine(keep, send))
        total = jnp.concatenate(totals, axis=1)
        scale = 1.0 / math.sqrt(seg_count * win * L)
        return (total * scale * quality.astype(jnp.float32)[None, :])[None]

    return jax.shard_map(
        body,
        mesh=mesh,
        in_specs=(P("chan", "win"), P("win"), P(), P("chan")),
        out_specs=P("win", None, "chan"),
        check_vma=False,
    )
```

time: 165 us -> 164 us (level)
  waiting for transfers between devices: 50 us -> 11.4 us
  Pallas kernels: 92.2 us -> 124 us
  starting transfers between devices: 10.3 us -> 16.5 us
    ppermute x4 -> x10, waiting for transfers between devices: 33.8 us -> 0.05 us  [swap(): return lax.ppermute(v, axis, [(d, d ^ bit) for d in range(size)])]
    pallas_call x2 -> x7, Pallas kernels: 90.4 us -> 122 us  [the longest x2 89.3 us: stacks(): pl.pallas_call(functools.partial(stack_kernel, src_count, blocks, begin,...]
    ppermute x2 -> x4, waiting for transfers between devices: 16.2 us -> 11.3 us  [swap(): return lax.ppermute(v, 'win', [(d, d ^ bit) for d in range(win)])]
    ppermute x4 -> x10, starting transfers between devices: 8.65 us -> 12.6 us  [swap(): return lax.ppermute(v, axis, [(d, d ^ bit) for d in range(size)])]
    ppermute x2 -> x4, starting transfers between devices: 1.66 us -> 3.92 us  [swap(): return lax.ppermute(v, 'win', [(d, d ^ bit) for d in range(win)])]
    broadcast_in_dim x1 -> x0, local copies, waits for them, and re-layouts: 1.98 us -> none  [body(): return (total * scale * quality.astype(jnp.float32)[None, :])[None]]
    mul x0 -> x1, local copies, waits for them, and re-layouts: none -> 1.98 us  [body(): return (total * scale * quality.astype(jnp.float32)[None, :])[None]]
  transfers between devices with their start and end apart: 6 -> 14, of which waited for: 5 -> 3; matrix products, arithmetic and copies ran while one was open for 0% -> 1% of each run, Pallas kernels for 15% -> 20%
where the time goes in v3:
time: 164 us
  Pallas kernels  124 us (76%)
  starting transfers between devices  16.5 us (10%)
  waiting for transfers between devices  11.4 us (7%)
  local copies, waits for them, and re-layouts  7.98 us (5%)
  other arithmetic  3.31 us (2%)
    pallas_call x2, Pallas kernels, stacks(): pl.pallas_call(functools.partial(stack_kernel, src_count, blocks, begin,...  89.3 us
    pallas_call x5, Pallas kernels, power(): pl.pallas_call(functools.partial(power_kernel, begin), grid=(number,), ou...  32.9 us
    ppermute x10, starting transfers between devices, swap(): return lax.ppermute(v, axis, [(d, d ^ bit) for d in range(size)])  12.6 us
    ppermute x4, waiting for transfers between devices, swap(): return lax.ppermute(v, 'win', [(d, d ^ bit) for d in range(win)])  11.3 us
    ppermute x4, starting transfers between devices, swap(): return lax.ppermute(v, 'win', [(d, d ^ bit) for d in range(win)])  3.92 us
  transfers between devices with their start and end apart: 14, of which 3 were waited for; matrix products, arithmetic and copies ran while one was open for 1% of the time, Pallas kernels for 20%

profile of v3, /device:TPU:0, one launch (start us, length us, event | category | flops | bytes accessed | tf_op | source)
XLA Modules:
  0.0 163.6 jit_solution(1774002948729131631)
XLA Ops:
  0.0 0.7 broadcast_remainder_fusion
  0.7 0.7 fusion.6
  1.6 3.2 %gather_fusion = bf16[16,25600]{1,0:T(8,128)(2,1)S(1)} fusion(bf16[1280,25600]{1,0:T(8,128)(2,1)} %refs_7_.1, s32[1024]{0:T(1024)S(1)} %pad_clamp_fusion), kind=kCustom, calls=%fused_computation | custom fusion | bytes 1638464 | tf_op jit(solution)/shard_map/jit(_take)/gather | solution.py:333
  4.8 1.8 %sources.1 = bf16[8,16,3072]{2,1,0:T(8,128)(2,1)S(1)} custom-call(s32[8]{0:T(128)S(1)} %copy-done, bf16[16,25600]{1,0:T(8,128)(2,1)S(1)} %gather_fusion, s32[16,1]{1,0:T(8,128)S(1)} %reshape.101.own_ref), custom_call_target="tpu_custom_call" | custom-call | tf_op jit(solution)/shard_map/sources/pallas_call | solution.py:336
  6.6 3.0 %collective-permute-start = (bf16[2,16,3072]{2,1,0:T(8,128)(2,1)S(1)}, bf16[2,16,3072]{2,1,0:T(8,128)(2,1)S(1)}, u32[]{:S(2)}, u32[]{:S(2)}) collective-permute-start(bf16[2,16,3072]{2,1,0:T(8,128)(2,1)S(1)} %get-tuple-element.54), channel_id=1, source_target_pairs={{0,4},{4,0},{8,12},{12,8},{16,20},{20,16},{24,28},{28,24},{1,5},{5... | collective-permute-start | bytes 589832 | tf_op jit(solution)/shard_map/ppermute | solution.py:284
  9.7 1.6 collective-permute-start.1
  11.2 7.6 %power.5 = f32[2,1,1280]{2,1,0:T(1,128)S(1)} custom-call(s32[8]{0:T(128)S(1)} %copy-done, bf16[1280,25600]{1,0:T(8,128)(2,1)} %refs_7_.1), custom_call_target="tpu_custom_call" | custom-call | flops 16384000 | bytes 16384000 | tf_op jit(solution)/shard_map/power/pallas_call | solution.py:346
  19.7 5.0 %power.6 = f32[1,1,1280]{2,1,0:T(1,128)S(1)} custom-call(s32[8]{0:T(128)S(1)} %copy-done, bf16[1280,25600]{1,0:T(8,128)(2,1)} %refs_7_.1), custom_call_target="tpu_custom_call" | custom-call | flops 8192000 | bytes 8192000 | tf_op jit(solution)/shard_map/power/pallas_call | solution.py:346
  24.8 3.1 %collective-permute-start.5 = (bf16[1,16,3072]{2,1,0:T(8,128)(2,1)S(1)}, bf16[1,16,3072]{2,1,0:T(8,128)(2,1)S(1)}, u32[]{:S(2)}, u32[]{:S(2)}) collective-permute-start(bf16[1,16,3072]{2,1,0:T(8,128)(2,1)S(1)} %select_add_fusion.2), channel_id=1, source_target_pairs={{0,16},{4,20},{8,24},{12,28},{16,0},{20,4},{24,8},{28,12},{1,17},{... | collective-permute-start | bytes 294920 | tf_op jit(solution)/shard_map/ppermute | solution.py:284
  27.9 7.8 %power.7 = f32[2,1,1280]{2,1,0:T(1,128)S(1)} custom-call(s32[8]{0:T(128)S(1)} %copy-done, bf16[1280,25600]{1,0:T(8,128)(2,1)} %refs_7_.1), custom_call_target="tpu_custom_call" | custom-call | flops 16384000 | bytes 16384000 | tf_op jit(solution)/shard_map/power/pallas_call | solution.py:346
  35.9 1.8 %collective-permute-start.7 = (bf16[1,16,3072]{2,1,0:T(8,128)(2,1)S(1)}, bf16[1,16,3072]{2,1,0:T(8,128)(2,1)S(1)}, u32[]{:S(2)}, u32[]{:S(2)}) collective-permute-start(bf16[1,16,3072]{2,1,0:T(8,128)(2,1)S(1)} %add.35), channel_id=1, source_target_pairs={{0,4},{4,0},{8,12},{12,8},{16,20},{20,16},{24,28},{28,24},{1,5},{5... | collective-permute-start | bytes 294920 | tf_op jit(solution)/shard_map/ppermute | solution.py:284
  37.7 1.6 collective-permute-start.6
  39.3 5.0 %power.8 = f32[1,1,1280]{2,1,0:T(1,128)S(1)} custom-call(s32[8]{0:T(128)S(1)} %copy-done, bf16[1280,25600]{1,0:T(8,128)(2,1)} %refs_7_.1), custom_call_target="tpu_custom_call" | custom-call | flops 8192000 | bytes 8192000 | tf_op jit(solution)/shard_map/power/pallas_call | solution.py:346
  45.2 7.4 %power.9 = f32[2,1,1280]{2,1,0:T(1,128)S(1)} custom-call(s32[8]{0:T(128)S(1)} %copy-done, bf16[1280,25600]{1,0:T(8,128)(2,1)} %refs_7_.1), custom_call_target="tpu_custom_call" | custom-call | flops 16384000 | bytes 16384000 | tf_op jit(solution)/shard_map/power/pallas_call | solution.py:346
  52.8 1.0 pad_maximum_fusion.refs_3_
  53.8 60.1 %stacks.2 = (f32[2,196,768]{2,1,0:T(8,128)}, f32[2,196,768]{2,1,0:T(8,128)}, bf16[8,400,1536]{2,1,0:T(8,128)(2,1)}, bf16[8,400,1536]{2,1,0:T(8,128)(2,1)}, bf16[8,384,1536]{2,1,0:T(8,128)(2,1)}) custom-call(s32[8]{0:T(128)} %refs_0_.3, s32[1]{0:T(128)} %bitcast.refs_1_, f32[8,1,1280]{2,1,0:T(1,128)} %copy-done.4, ...), custom_call_target="tpu_custom_call" | custom-call | flops 22347251712 | bytes 39321600 | tf_op jit(solution)/shard_map/stacks/pallas_call | solution.py:393
  113.9 29.2 %stacks.3 = (f32[2,196,512]{2,1,0:T(8,128)}, f32[2,196,512]{2,1,0:T(8,128)}) custom-call(s32[8]{0:T(128)} %refs_0_.3, s32[1]{0:T(128)} %bitcast.refs_1_, f32[8,1,1280]{2,1,0:T(1,128)} %copy-done.4, bf16[8,400,1536]{2,1,0:T(8,128)(2,1)} %get-tuple-element.46.refs_3_, bf16[8,400,1536]{2,1,0:T(8,128)(2,1)} %get-tuple-element.47.refs_4_, ...), custom_call_target="tpu_custom_call" | custom-call | flops 14898167808 | bytes 26214400 | tf_op jit(solution)/shard_map/stacks/pallas_call | solution.py:393
  143.1 1.9 %copy.10 = f32[2,196,512]{2,0,1:T(2,128)S(1)} copy(f32[2,196,512]{2,1,0:T(8,128)} %get-tuple-element.50) | data formatting | bytes 1605632 | tf_op jit(solution)/shard_map/stacks/pallas_call | solution.py:393
  146.3 1.1 collective-permute-done.12
  147.6 1.8 %collective-permute-start.13 = (bf16[196,512]{1,0:T(8,128)(2,1)S(1)}, bf16[196,512]{1,0:T(8,128)(2,1)S(1)}, u32[]{:S(2)}, u32[]{:S(2)}) collective-permute-start(bf16[196,512]{1,0:T(8,128)(2,1)S(1)} %fusion.5), channel_id=1, source_target_pairs={{0,2},{1,3},{2,0},{3,1},{4,6},{5,7},{6,4},{7,5},{8,10},{9,11},{10,... | collective-permute-start | bytes 602120 | tf_op jit(solution)/shard_map/ppermute | solution.py:414
  149.7 1.5 collective-permute-start.11
  151.1 4.5 %collective-permute-done.13 = bf16[196,512]{1,0:T(8,128)(2,1)S(1)} collective-permute-done((bf16[196,512]{1,0:T(8,128)(2,1)S(1)}, bf16[196,512]{1,0:T(8,128)(2,1)S(1)}, u32[]{:S(2)}, u32[]{:S(2)}) %collective-permute-start.13) | collective-permute-done | bytes 200736 | tf_op jit(solution)/shard_map/ppermute | solution.py:414
  155.7 5.7 %collective-permute-done.11 = bf16[196,768]{1,0:T(8,128)(2,1)S(1)} collective-permute-done((bf16[196,768]{1,0:T(8,128)(2,1)S(1)}, bf16[196,768]{1,0:T(8,128)(2,1)S(1)}, u32[]{:S(2)}, u32[]{:S(2)}) %collective-permute-start.11) | collective-permute-done | bytes 301088 | tf_op jit(solution)/shard_map/ppermute | solution.py:414
  161.6 2.0 %copy.12 = f32[1,196,1280]{2,0,1:T(1,128)} copy(f32[1,196,1280]{2,1,0:T(8,128)S(1)} %maximum_multiply_fusion) | data formatting | bytes 2007040 | tf_op jit(solution)/shard_map/mul | solution.py:429
  (60 shorter events, 4.1 us)
Async XLA Ops:
  1.6 3.2 %copy-start = (s32[8]{0:T(128)S(1)}, s32[8]{0:T(128)}, u32[]{:S(2)}) copy-start(s32[8]{0:T(128)} %refs_0_.3) | copy-start | bytes 100
  6.6 12.2 %collective-permute-start = (bf16[2,16,3072]{2,1,0:T(8,128)(2,1)S(1)}, bf16[2,16,3072]{2,1,0:T(8,128)(2,1)S(1)}, u32[]{:S(2)}, u32[]{:S(2)}) collective-permute-start(bf16[2,16,3072]{2,1,0:T(8,128)(2,1)S(1)} %get-tuple-element.54), channel_id=1, source_target_pairs={{0,4},{4,0},{8,12},{12,8},{16,20},{20,16},{24,28},{28,24},{1,5},{5... | collective-permute-start | bytes 589832 | tf_op jit(solution)/shard_map/ppermute | solution.py:284
  9.7 9.2 %collective-permute-start.1 = (bf16[2,16,3072]{2,1,0:T(8,128)(2,1)S(1)}, bf16[2,16,3072]{2,1,0:T(8,128)(2,1)S(1)}, u32[]{:S(2)}, u32[]{:S(2)}) collective-permute-start(bf16[2,16,3072]{2,1,0:T(8,128)(2,1)S(1)} %get-tuple-element.53), channel_id=1, source_target_pairs={{0,8},{4,12},{8,0},{12,4},{16,24},{20,28},{24,16},{28,20},{1,9},{5... | collective-permute-start | bytes 589832 | tf_op jit(solution)/shard_map/ppermute | solution.py:284
  19.0 5.7 %collective-permute-start.3 = (bf16[1,16,3072]{2,1,0:T(8,128)(2,1)S(1)}, bf16[1,16,3072]{2,1,0:T(8,128)(2,1)S(1)}, u32[]{:S(2)}, u32[]{:S(2)}) collective-permute-start(bf16[1,16,3072]{2,1,0:T(8,128)(2,1)S(1)} %broadcast_select_fusion.8), channel_id=1, source_target_pairs={{0,4},{4,0},{8,12},{12,8},{16,20},{20,16},{24,28},{28,24},{1,5},{5... | collective-permute-start | bytes 294920 | tf_op jit(solution)/shard_map/ppermute | solution.py:284
  19.6 5.2 %collective-permute-start.2 = (bf16[1,16,3072]{2,1,0:T(8,128)(2,1)S(1)}, bf16[1,16,3072]{2,1,0:T(8,128)(2,1)S(1)}, u32[]{:S(2)}, u32[]{:S(2)}) collective-permute-start(bf16[1,16,3072]{2,1,0:T(8,128)(2,1)S(1)} %broadcast_select_fusion.11), channel_id=1, source_target_pairs={{0,8},{4,12},{8,0},{12,4},{16,24},{20,28},{24,16},{28,20},{1,9},{5... | collective-permute-start | bytes 294920 | tf_op jit(solution)/shard_map/ppermute | solution.py:284
  24.8 11.0 %collective-permute-start.5 = (bf16[1,16,3072]{2,1,0:T(8,128)(2,1)S(1)}, bf16[1,16,3072]{2,1,0:T(8,128)(2,1)S(1)}, u32[]{:S(2)}, u32[]{:S(2)}) collective-permute-start(bf16[1,16,3072]{2,1,0:T(8,128)(2,1)S(1)} %select_add_fusion.2), channel_id=1, source_target_pairs={{0,16},{4,20},{8,24},{12,28},{16,0},{20,4},{24,8},{28,12},{1,17},{... | collective-permute-start | bytes 294920 | tf_op jit(solution)/shard_map/ppermute | solution.py:284
  27.8 8.0 %collective-permute-start.4 = (bf16[1,16,3072]{2,1,0:T(8,128)(2,1)S(1)}, bf16[1,16,3072]{2,1,0:T(8,128)(2,1)S(1)}, u32[]{:S(2)}, u32[]{:S(2)}) collective-permute-start(bf16[1,16,3072]{2,1,0:T(8,128)(2,1)S(1)} %select_add_fusion.3), channel_id=1, source_target_pairs={{0,16},{4,20},{8,24},{12,28},{16,0},{20,4},{24,8},{28,12},{1,17},{... | collective-permute-start | bytes 294920 | tf_op jit(solution)/shard_map/ppermute | solution.py:284
  35.9 8.4 %collective-permute-start.7 = (bf16[1,16,3072]{2,1,0:T(8,128)(2,1)S(1)}, bf16[1,16,3072]{2,1,0:T(8,128)(2,1)S(1)}, u32[]{:S(2)}, u32[]{:S(2)}) collective-permute-start(bf16[1,16,3072]{2,1,0:T(8,128)(2,1)S(1)} %add.35), channel_id=1, source_target_pairs={{0,4},{4,0},{8,12},{12,8},{16,20},{20,16},{24,28},{28,24},{1,5},{5... | collective-permute-start | bytes 294920 | tf_op jit(solution)/shard_map/ppermute | solution.py:284
  37.7 6.6 %collective-permute-start.6 = (bf16[1,16,3072]{2,1,0:T(8,128)(2,1)S(1)}, bf16[1,16,3072]{2,1,0:T(8,128)(2,1)S(1)}, u32[]{:S(2)}, u32[]{:S(2)}) collective-permute-start(bf16[1,16,3072]{2,1,0:T(8,128)(2,1)S(1)} %add.34), channel_id=1, source_target_pairs={{0,8},{4,12},{8,0},{12,4},{16,24},{20,28},{24,16},{28,20},{1,9},{5... | collective-permute-start | bytes 294920 | tf_op jit(solution)/shard_map/ppermute | solution.py:284
  44.4 8.3 %collective-permute-start.8 = (bf16[2,16,3072]{2,1,0:T(8,128)(2,1)S(1)}, bf16[2,16,3072]{2,1,0:T(8,128)(2,1)S(1)}, u32[]{:S(2)}, u32[]{:S(2)}) collective-permute-start(bf16[2,16,3072]{2,1,0:T(8,128)(2,1)S(1)} %get-tuple-element.42), channel_id=1, source_target_pairs={{0,4},{4,0},{8,12},{12,8},{16,20},{20,16},{24,28},{28,24},{1,5},{5... | collective-permute-start | bytes 589832 | tf_op jit(solution)/shard_map/ppermute | solution.py:284
  45.0 7.8 %collective-permute-start.9 = (bf16[2,16,3072]{2,1,0:T(8,128)(2,1)S(1)}, bf16[2,16,3072]{2,1,0:T(8,128)(2,1)S(1)}, u32[]{:S(2)}, u32[]{:S(2)}) collective-permute-start(bf16[2,16,3072]{2,1,0:T(8,128)(2,1)S(1)} %get-tuple-element.43), channel_id=1, source_target_pairs={{0,8},{4,12},{8,0},{12,4},{16,24},{20,28},{24,16},{28,20},{1,9},{5... | collective-permute-start | bytes 589832 | tf_op jit(solution)/shard_map/ppermute | solution.py:284
  52.7 1.1 copy-start.4
  143.1 2.0 %copy-start.2 = (f32[2,196,768]{2,1,0:T(8,128)S(1)}, f32[2,196,768]{2,1,0:T(8,128)}, u32[]{:S(2)}) copy-start(f32[2,196,768]{2,1,0:T(8,128)} %get-tuple-element.45) | copy-start | bytes 3612676
  145.0 2.4 %copy-start.3 = (f32[2,196,512]{2,1,0:T(8,128)S(1)}, f32[2,196,512]{2,1,0:T(8,128)}, u32[]{:S(2)}) copy-start(f32[2,196,512]{2,1,0:T(8,128)} %get-tuple-element.49) | copy-start | bytes 2408452
  145.0 2.4 %collective-permute-start.12 = (f32[2,196,512]{2,0,1:T(2,128)S(1)}, f32[2,196,512]{2,0,1:T(2,128)S(1)}, u32[]{:S(2)}, u32[]{:S(2)}) collective-permute-start(f32[2,196,512]{2,0,1:T(2,128)S(1)} %copy.10), channel_id=1, source_target_pairs={{0,1},{1,0},{2,3},{3,2},{4,5},{5,4},{6,7},{7,6},{8,9},{9,8},{10,11... | collective-permute-start | bytes 2408456 | tf_op jit(solution)/shard_map/ppermute | solution.py:414
  145.7 3.7 %collective-permute-start.10 = (f32[2,196,768]{2,0,1:T(2,128)S(1)}, f32[2,196,768]{2,0,1:T(2,128)S(1)}, u32[]{:S(2)}, u32[]{:S(2)}) collective-permute-start(f32[2,196,768]{2,0,1:T(2,128)S(1)} %copy.8), channel_id=1, source_target_pairs={{0,1},{1,0},{2,3},{3,2},{4,5},{5,4},{6,7},{7,6},{8,9},{9,8},{10,11... | collective-permute-start | bytes 3612680 | tf_op jit(solution)/shard_map/ppermute | solution.py:414
  147.4 2.1 %copy-start.1 = (f32[2,196,768]{2,1,0:T(8,128)S(1)}, f32[2,196,768]{2,1,0:T(8,128)}, u32[]{:S(2)}) copy-start(f32[2,196,768]{2,1,0:T(8,128)} %get-tuple-element.44) | copy-start | bytes 3612676
  147.6 8.0 %collective-permute-start.13 = (bf16[196,512]{1,0:T(8,128)(2,1)S(1)}, bf16[196,512]{1,0:T(8,128)(2,1)S(1)}, u32[]{:S(2)}, u32[]{:S(2)}) collective-permute-start(bf16[196,512]{1,0:T(8,128)(2,1)S(1)} %fusion.5), channel_id=1, source_target_pairs={{0,2},{1,3},{2,0},{3,1},{4,6},{5,7},{6,4},{7,5},{8,10},{9,11},{10,... | collective-permute-start | bytes 602120 | tf_op jit(solution)/shard_map/ppermute | solution.py:414
  149.5 1.7 %copy-start.5 = (s32[1280]{0:T(1024)S(1)}, s32[1280]{0:T(1024)}, u32[]{:S(2)}) copy-start(s32[1280]{0:T(1024)} %param.7) | copy-start | bytes 15364
  149.7 11.8 %collective-permute-start.11 = (bf16[196,768]{1,0:T(8,128)(2,1)S(1)}, bf16[196,768]{1,0:T(8,128)(2,1)S(1)}, u32[]{:S(2)}, u32[]{:S(2)}) collective-permute-start(bf16[196,768]{1,0:T(8,128)(2,1)S(1)} %fusion.4), channel_id=1, source_target_pairs={{0,2},{1,3},{2,0},{3,1},{4,6},{5,7},{6,4},{7,5},{8,10},{9,11},{10,... | collective-permute-start | bytes 903176 | tf_op jit(solution)/shard_map/ppermute | solution.py:414

commit v4 on v3

v4 whole, which is shorter than its diff:
```python
import functools
import math

import jax
import jax.numpy as jnp
from jax import lax
from jax.experimental import pallas as pl
from jax.experimental.pallas import tpu as pltpu
from jax.sharding import PartitionSpec as P

L = 3072
LAGS = 49
HALF = (LAGS - 1) // 2
EVEN = HALF + 1
ODD = HALF
EPSILON = 1e-06
LANES = 128
TILES = L // LANES
PAIRS = TILES // 2
ROWS = 64
COLUMNS = 512


def lanes(rows, dtype=jnp.int32):
    return lax.broadcasted_iota(dtype, (rows, LANES), 1)


def source_kernel(offsets_ref, rows_ref, own_ref, out_ref):
    count = rows_ref.shape[0]
    seg_count = out_ref.shape[0]
    stride = rows_ref.shape[1] // seg_count
    lane = lanes(count)
    owned = own_ref[...] > 0

    def one(g, carry):
        off = offsets_ref[g]
        back = lax.rem(LANES - off, LANES)
        base = g * stride
        tiles = []
        for m in range(TILES + 1):
            start = pl.multiple_of(base + m * LANES, LANES)
            tiles.append(rows_ref[:, pl.ds(start, LANES)].astype(jnp.float32))
        cut = [jnp.where(lane < off, tiles[m + 1], tiles[m]) for m in range(TILES)]
        total = cut[0] * cut[0]
        for m in range(1, TILES):
            total = total + cut[m] * cut[m]
        power = jnp.sum(total, axis=1, keepdims=True) / L
        root = jnp.sqrt(power + EPSILON)
        for m in range(TILES):
            white = jnp.where(owned, pltpu.roll(cut[m], back, 1) / root, 0.0)
            out_ref[g, :, m * LANES : (m + 1) * LANES] = white.astype(jnp.bfloat16)
        return carry

    lax.fori_loop(0, seg_count, one, 0)


def phases(u_ref, seg, count):
    lane = lanes(count)
    even = lane % 2 == 0
    zero = jnp.zeros((count, LANES), jnp.float32)

    def tile(m):
        if m < 0 or m >= TILES:
            return zero
        return u_ref[seg, :, m * LANES : (m + 1) * LANES].astype(jnp.float32)

    plain, ahead, behind = [], [], []
    for p in range(-1, PAIRS + 1):
        low, high, before = tile(2 * p), tile(2 * p + 1), tile(2 * p - 1)
        low_on = pltpu.roll(low, 1, 1)
        high_on = pltpu.roll(high, 1, 1)
        before_on = pltpu.roll(before, 1, 1)
        plain.append(jnp.where(even, low, high_on))
        ahead.append(jnp.where(even, pltpu.roll(low, LANES - 1, 1) - low, high - high_on))
        late_low = jnp.where(lane == 0, before_on, low_on)
        late_high = jnp.where(lane == 0, low_on, high_on)
        behind.append(jnp.where(even, late_low - low, pltpu.roll(late_high, 1, 1) - high_on))
    return plain, ahead, behind


def builders(u_ref, seg, off, a_refs, count):
    lane = lanes(count)
    even = lane % 2 == 0
    wide = lanes(count * PAIRS)
    held = []

    def start():
        for tiles in phases(u_ref, seg, count):
            shifted = []
            for p in range(PAIRS + 1):
                back = pltpu.roll(tiles[p], LANES - 1, 1)
                on = pltpu.roll(tiles[p + 1], 1, 1)
                shifted.append(jnp.where(even, back, on))
            held.append(
                [
                    jnp.concatenate(part, axis=0).astype(jnp.bfloat16)
                    for part in (tiles[1 : PAIRS + 1], shifted[:PAIRS], shifted[1:])
                ]
            )

    def one(which, index):
        now, early, late = held[which]
        s = 2 * index - HALF
        if s > 0:
            z = jnp.where(wide >= LANES - s, early, now)
        elif s < 0:
            z = jnp.where(wide < -s, late, now)
        else:
            z = now
        z = pltpu.roll(z, lax.rem(off + (s + LANES), LANES), 1)
        a_refs[which][:, index * count : (index + 1) * count, :] = z.reshape(PAIRS, count, LANES)

    work = [start]
    for which, lag_count in enumerate((EVEN, EVEN, ODD)):
        work += [functools.partial(one, which, index) for index in range(lag_count)]
    return work


def power_kernel(begin, offsets_ref, *refs):
    x_refs, gain_ref = refs[:-1], refs[-1]
    off = offsets_ref[begin + pl.program_id(0)]
    channels = x_refs[0].shape[0]
    early = lanes(ROWS) < off

    def square(at, m):
        value = x_refs[m][at : at + ROWS, :].astype(jnp.float32)
        return value * value

    for row in range(0, channels, LANES):
        sums = []
        for at in range(row, min(row + LANES, channels), ROWS):
            total = jnp.where(early, square(at, TILES), square(at, 0))
            for m in range(1, TILES):
                total = total + square(at, m)
            sums.append(total)
        across = jnp.concatenate(sums, axis=0)
        power = jnp.sum(jnp.transpose(across), axis=0, keepdims=True) / L
        gain_ref[0, :, row : row + across.shape[0]] = lax.rsqrt(power + EPSILON)


def prepare(x_refs, off, row, w_refs, at):
    lane = lanes(ROWS)
    early = lane < off
    even = lax.rem(lane + off, 2) == 0
    first_ref, second_ref, both_ref = w_refs

    def tile(m):
        return x_refs[m][row : row + ROWS, :]

    for p in range(PAIRS):
        a, b, c = tile(2 * p), tile(2 * p + 1), tile(2 * p + 2)
        low = jnp.where(early, b, a)
        high = jnp.where(early, c, b)
        first = jnp.where(even, low, pltpu.roll(high, 1, 1))
        second = jnp.where(even, pltpu.roll(low, LANES - 1, 1), high)
        first_ref[p, at : at + ROWS, :] = first
        second_ref[p, at : at + ROWS, :] = second
        both_ref[p, at : at + ROWS, :] = first + second


def dot(a_ref, w_ref, width):
    a = jnp.concatenate([a_ref[p] for p in range(PAIRS)], axis=1)
    w = jnp.concatenate([w_ref[p, :width, :] for p in range(PAIRS)], axis=1)
    return lax.dot_general(a, w, (((1,), (1,)), ((), ())), preferred_element_type=jnp.float32)


def stack_kernel(src_count, blocks, scale, offsets_ref, win_ref, gain_ref, quality_ref, u_ref, *refs):
    refs = list(refs)

    def take(number):
        taken = refs[:number]
        del refs[:number]
        return taken

    x_refs = take(TILES + 1)
    outs = take(2)
    a_slots = (take(3), take(3))
    c1, c2, c3 = take(3)
    w_slots = (take(3), take(3))
    n = pl.program_id(0)
    last = pl.num_programs(0) - 1
    off = offsets_ref[n]
    count = u_ref.shape[1]

    @pl.when(n == 0)
    def _():
        for c in (c1, c2, c3):
            c[...] = jnp.zeros_like(c)
        for piece in builders(u_ref, 0, off, a_slots[0], count):
            piece()

    def pieces(k):
        start, width = blocks[k]
        return [
            functools.partial(prepare, x_refs, off, start + at, w_slots[k % 2], at)
            for at in range(0, width, ROWS)
        ]

    def segment(parity):
        for piece in pieces(0):
            piece()
        later = jnp.minimum(n + 1, last)
        built = builders(u_ref, later, offsets_ref[later], a_slots[1 - parity], count)
        for k, (start, width) in enumerate(blocks):
            todo = pieces(k + 1) if k + 1 < len(blocks) else []
            first, second, both = w_slots[k % 2]
            gain = gain_ref[n, :, start : start + width]
            for i, (a, w, c) in enumerate(
                zip(a_slots[parity], (both, second, first), (c1, c2, c3))
            ):
                term = dot(a, w, width) * gain
                for at in range(0, width, LANES):
                    size = min(LANES, width - at)
                    c[(start + at) // LANES, :, :size] += term[:, at : at + size]
                share = pl.cdiv(len(todo), 3 - i)
                built_share = pl.cdiv(len(built), 3 * (len(blocks) - k) - i)
                for piece in todo[:share] + built[:built_share]:
                    piece()
                todo, built = todo[share:], built[built_share:]

    for parity in (0, 1):
        pl.when(n % 2 == parity)(functools.partial(segment, parity))

    @pl.when(n == last)
    def _():
        groups = c1.shape[0]
        for group in range(groups):
            usable = quality_ref[group : group + 1, :] * scale
            c2[group] = (c1[group] + c2[group]) * usable
            c3[group] = (c1[group, : ODD * count, :] + c3[group]) * usable
        for slot in range(4):
            step = win_ref[0] ^ slot
            out = outs[slot % 2]
            base = slot // 2 * src_count * LAGS * groups
            for group in range(groups):
                evens, odds = c2.at[group], c3.at[group]
                for i in range(src_count):
                    row = step * src_count + i
                    here = base + i * LAGS * groups + group
                    out[pl.ds(here, EVEN, stride=2 * groups), :] = evens[
                        pl.ds(row, EVEN, stride=count), :
                    ]
                    out[pl.ds(here + groups, ODD, stride=2 * groups), :] = odds[
                        pl.ds(row, ODD, stride=count), :
                    ]


def exchange(value, axis, size, offsets, works):
    me = lax.axis_index(axis)

    def swap(v, bit):
        return lax.ppermute(v, axis, [(d, d ^ bit) for d in range(size)])

    def scatter(v, bit):
        low = me & bit == 0
        half = v.shape[0] // 2
        one, two = v[:half], v[half:]
        return jnp.where(low, one, two) + swap(jnp.where(low, two, one), bit)

    def whole(v, bit):
        return v + swap(v, bit)

    def gather(v, bit):
        low = me & bit == 0
        other = swap(v, bit)
        return jnp.concatenate([jnp.where(low, v, other), jnp.where(low, other, v)], axis=0)

    bits = [1 << b for b in range(2, size.bit_length() - 1)]
    plans = [
        [(scatter, p), (scatter, q)] + [(whole, b) for b in bits] + [(gather, q), (gather, p)]
        for p, q in ((1, 2), (2, 1))
    ]
    half = value.shape[0] // 2
    values = [value[:half], value[half:]]
    results = []
    works = list(works)
    for index, steps in enumerate(zip(*plans)):
        values = [step(v, bit) for v, (step, bit) in zip(values, steps)]
        left = len(plans[0]) - index
        share = pl.cdiv(len(works), left)
        now = [work(offsets) for work in works[:share]]
        works = works[share:]
        if works:
            values, now, offsets = lax.optimization_barrier((values, now, offsets))
        results += now
    return jnp.concatenate(values, axis=0), results


def solution(mesh):
    chan = mesh.shape["chan"]
    win = mesh.shape["win"]

    def body(records, offsets, src_index, quality):
        channels, samples = records.shape
        seg_count = offsets.shape[0]
        stride = samples // seg_count
        step_count, src_count = src_index.shape
        count = step_count * src_count
        flat = src_index.reshape(-1)
        own = (lax.div(flat, channels) == lax.axis_index("chan")).astype(jnp.int32)[:, None]
        rows = jnp.take(records, lax.rem(flat, channels), axis=0, mode="clip")
        smem = pl.BlockSpec(memory_space=pltpu.SMEM)
        vmem = pl.BlockSpec(memory_space=pltpu.VMEM)
        sources = pl.pallas_call(
            source_kernel,
            out_shape=jax.ShapeDtypeStruct((seg_count, count, L), jnp.bfloat16),
            in_specs=[smem, vmem, vmem],
            out_specs=vmem,
            compiler_params=pltpu.CompilerParams(vmem_limit_bytes=32 * 2**20),
            name="sources",
        )(offsets, rows, own)

        def tiles(begin):
            per = stride // LANES

            def place(m):
                return pl.BlockSpec((channels, LANES), lambda g: (0, (begin + g) * per + m))

            return [place(m) for m in range(TILES + 1)]

        def power(begin, number):
            return lambda starts: pl.pallas_call(
                functools.partial(power_kernel, begin),
                grid=(number,),
                out_shape=jax.ShapeDtypeStruct((number, 1, channels), jnp.float32),
                in_specs=[smem] + tiles(begin),
                out_specs=pl.BlockSpec((1, 1, channels), lambda g: (g, 0, 0)),
                compiler_params=pltpu.CompilerParams(vmem_limit_bytes=32 * 2**20),
                cost_estimate=pl.CostEstimate(
                    flops=2 * number * channels * stride,
                    bytes_accessed=2 * number * channels * stride,
                    transcendentals=0,
                ),
                name="power",
            )(starts, *([records] * (TILES + 1)))

        cuts = [0, 2, 3, 5, 6, seg_count]
        works = [power(a, b - a) for a, b in zip(cuts, cuts[1:])]
        sources, gains = exchange(sources, "chan", chan, offsets, works)
        gain = jnp.concatenate(gains, axis=0)

        w = lax.axis_index("win").astype(jnp.int32).reshape(1)
        bf16 = functools.partial(pltpu.VMEM, dtype=jnp.bfloat16)
        f32 = functools.partial(pltpu.VMEM, dtype=jnp.float32)
        groups = pl.cdiv(channels, LANES)
        row_counts = (EVEN * count, EVEN * count, ODD * count)
        head = channels % COLUMNS or COLUMNS
        blocks = [(0, head)] + [(at, COLUMNS) for at in range(head, channels, COLUMNS)]
        sizes = [max([width for _, width in blocks[parity::2]] + [ROWS]) for parity in (0, 1)]
        usable = jnp.pad(quality.astype(jnp.float32), (0, groups * LANES - channels))
        half = jax.ShapeDtypeStruct((2 * src_count * LAGS * groups, LANES), jnp.float32)
        scale = 1.0 / math.sqrt(seg_count * win * L)
        keep, send = pl.pallas_call(
            functools.partial(stack_kernel, src_count, blocks, scale),
            grid=(seg_count,),
            out_shape=(half, half),
            in_specs=[smem, smem, vmem, vmem, vmem] + tiles(0),
            out_specs=(vmem, vmem),
            scratch_shapes=[bf16((PAIRS, r, LANES)) for r in row_counts] * 2
            + [f32((groups, r, LANES)) for r in row_counts]
            + [bf16((PAIRS, size, LANES)) for size in sizes for _ in range(3)],
            compiler_params=pltpu.CompilerParams(vmem_limit_bytes=58 * 2**20),
            cost_estimate=pl.CostEstimate(
                flops=seg_count * sum(row_counts) * L * channels,
                bytes_accessed=2 * channels * samples,
                transcendentals=0,
            ),
            name="stacks",
        )(offsets, w, gain, usable.reshape(groups, LANES), sources, *([records] * (TILES + 1)))

        def swap(v, bit):
            return lax.ppermute(v, "win", [(d, d ^ bit) for d in range(win)])

        pair = keep + swap(send, 1)
        cut = pair.shape[0] // 2
        total = pair[:cut] + swap(pair[cut:].astype(jnp.bfloat16), 2).astype(jnp.float32)
        return total.reshape(1, src_count * LAGS, groups * LANES)[..., :channels]

    return jax.shard_map(
        body,
        mesh=mesh,
        in_specs=(P("chan", "win"), P("win"), P(), P("chan")),
        out_specs=P("win", None, "chan"),
        check_vma=False,
    )
```

time: 164 us -> 169 us (1.030)
  Pallas kernels: 124 us -> 109 us
  other arithmetic: 3.31 us -> 18.3 us
  waiting for transfers between devices: 11.4 us -> 20.5 us
  starting transfers between devices: 16.5 us -> 13.8 us
    pallas_call x2 -> x1, Pallas kernels: 89.3 us -> 70.6 us  [body(): pl.pallas_call(functools.partial(stack_kernel, src_count, blocks, scale),...]
    ppermute x4 -> x2, waiting for transfers between devices: 11.3 us -> 16.2 us  [swap(): return lax.ppermute(v, 'win', [(d, d ^ bit) for d in range(win)])]
    ppermute x10, waiting for transfers between devices: 0.05 us -> 4.33 us  [swap(): return lax.ppermute(v, axis, [(d, d ^ bit) for d in range(size)])]
    add x3, other arithmetic: 0.09 us -> 4.18 us  [scatter(): return jnp.where(low, one, two) + swap(jnp.where(low, two, one), bit)]
    pallas_call x5, Pallas kernels: 32.9 us -> 36.2 us  [power(): pl.pallas_call(functools.partial(power_kernel, begin), grid=(number,), ou...]
    unnamed x16 -> x24, local copies, waits for them, and re-layouts: 0.05 us -> 3.29 us
    add x2, other arithmetic: 0.05 us -> 3.21 us  [whole(): return v + swap(v, bit)]
    add x2, other arithmetic: 0.35 us -> 3.02 us  [the longest x1 1.93 us: body(): pair = keep + swap(send, 1)]
  transfers between devices with their start and end apart: 14 -> 12, of which waited for: 3 -> 4; matrix products, arithmetic and copies ran while one was open for 1% -> 5% of each run, Pallas kernels for 20% -> 16%
where the time goes in v4:
time: 169 us
  Pallas kernels  109 us (64%)
  waiting for transfers between devices  20.5 us (12%)
  other arithmetic  18.3 us (11%)
  starting transfers between devices  13.8 us (8%)
  local copies, waits for them, and re-layouts  7.33 us (4%)
    pallas_call x1, Pallas kernels, body(): pl.pallas_call(functools.partial(stack_kernel, src_count, blocks, scale),...  70.6 us
    pallas_call x5, Pallas kernels, power(): pl.pallas_call(functools.partial(power_kernel, begin), grid=(number,), ou...  36.2 us
    ppermute x2, waiting for transfers between devices, swap(): return lax.ppermute(v, 'win', [(d, d ^ bit) for d in range(win)])  16.2 us
    ppermute x10, starting transfers between devices, swap(): return lax.ppermute(v, axis, [(d, d ^ bit) for d in range(size)])  12.2 us
    ppermute x10, waiting for transfers between devices, swap(): return lax.ppermute(v, axis, [(d, d ^ bit) for d in range(size)])  4.33 us
    add x3, other arithmetic, scatter(): return jnp.where(low, one, two) + swap(jnp.where(low, two, one), bit)  4.18 us
  transfers between devices with their start and end apart: 12, of which 4 were waited for; matrix products, arithmetic and copies ran while one was open for 5% of the time, Pallas kernels for 16%

profile of v4, /device:TPU:0, one launch (start us, length us, event | category | flops | bytes accessed | tf_op | source)
XLA Modules:
  0.0 168.7 jit_solution(13521754292956076166)
XLA Ops:
  1.6 3.2 %gather_fusion = bf16[16,25600]{1,0:T(8,128)(2,1)S(1)} fusion(bf16[1280,25600]{1,0:T(8,128)(2,1)} %refs_24_.11, s32[1024]{0:T(1024)S(1)} %pad_clamp_fusion), kind=kCustom, calls=%fused_computation | custom fusion | bytes 1638464 | tf_op jit(solution)/shard_map/jit(_take)/gather | solution.py:301
  4.8 1.8 %sources.1 = bf16[8,16,3072]{2,1,0:T(8,128)(2,1)S(1)} custom-call(s32[8]{0:T(128)S(1)} %copy-done.2, bf16[16,25600]{1,0:T(8,128)(2,1)S(1)} %gather_fusion, s32[16,1]{1,0:T(8,128)S(1)} %reshape.57.own_ref), custom_call_target="tpu_custom_call" | custom-call | tf_op jit(solution)/shard_map/sources/pallas_call | solution.py:304
  8.3 3.0 %collective-permute-start.1 = (bf16[2,16,3072]{2,1,0:T(8,128)(2,1)}, bf16[2,16,3072]{2,1,0:T(8,128)(2,1)}, u32[]{:S(2)}, u32[]{:S(2)}) collective-permute-start(bf16[2,16,3072]{2,1,0:T(8,128)(2,1)} %get-tuple-element.43), channel_id=1, source_target_pairs={{0,8},{4,12},{8,0},{12,4},{16,24},{20,28},{24,16},{28,20},{1,9},{5... | collective-permute-start | bytes 589832 | tf_op jit(solution)/shard_map/ppermute | solution.py:252
  11.3 1.5 collective-permute-start
  12.8 8.5 %power.5 = f32[2,1,1280]{2,1,0:T(1,128)S(1)} custom-call(s32[8]{0:T(128)S(1)} %copy-done.2, bf16[1280,25600]{1,0:T(8,128)(2,1)} %refs_24_.11, bf16[1280,25600]{1,0:T(8,128)(2,1)} %refs_24_.11, bf16[1280,25600]{1,0:T(8,128)(2,1)} %refs_24_.11, bf16[1280,25600]{1,0:T(8,128)(2,1)} %refs_24_.11, bf16[1280,25600]{1,0:T(8,128)(2,1)} %refs_24_.11, ...), custom_call_target="tpu_custom_call" | custom-call | flops 16384000 | bytes 16384000 | tf_op jit(solution)/shard_map/power/pallas_call | solution.py:322
  22.0 1.1 select_add_fusion
  25.6 5.3 %power.6 = f32[1,1,1280]{2,1,0:T(1,128)S(1)} custom-call(s32[8]{0:T(128)S(1)} %copy-done.2, bf16[1280,25600]{1,0:T(8,128)(2,1)} %refs_24_.11, bf16[1280,25600]{1,0:T(8,128)(2,1)} %refs_24_.11, bf16[1280,25600]{1,0:T(8,128)(2,1)} %refs_24_.11, bf16[1280,25600]{1,0:T(8,128)(2,1)} %refs_24_.11, bf16[1280,25600]{1,0:T(8,128)(2,1)} %refs_24_.11, ...), custom_call_target="tpu_custom_call" | custom-call | flops 8192000 | bytes 8192000 | tf_op jit(solution)/shard_map/power/pallas_call | solution.py:322
  31.0 1.5 select_add_fusion.2
  32.5 1.6 select_add_fusion.3
  34.1 3.0 %collective-permute-start.4 = (bf16[1,16,3072]{2,1,0:T(8,128)(2,1)}, bf16[1,16,3072]{2,1,0:T(8,128)(2,1)}, u32[]{:S(2)}, u32[]{:S(2)}) collective-permute-start(bf16[1,16,3072]{2,1,0:T(8,128)(2,1)} %select_add_fusion.3), channel_id=1, source_target_pairs={{0,16},{4,20},{8,24},{12,28},{16,0},{20,4},{24,8},{28,12},{1,17},{... | collective-permute-start | bytes 294920 | tf_op jit(solution)/shard_map/ppermute | solution.py:252
  37.7 8.5 %power.7 = f32[2,1,1280]{2,1,0:T(1,128)S(1)} custom-call(s32[8]{0:T(128)S(1)} %copy-done.2, bf16[1280,25600]{1,0:T(8,128)(2,1)} %refs_24_.11, bf16[1280,25600]{1,0:T(8,128)(2,1)} %refs_24_.11, bf16[1280,25600]{1,0:T(8,128)(2,1)} %refs_24_.11, bf16[1280,25600]{1,0:T(8,128)(2,1)} %refs_24_.11, bf16[1280,25600]{1,0:T(8,128)(2,1)} %refs_24_.11, ...), custom_call_target="tpu_custom_call" | custom-call | flops 16384000 | bytes 16384000 | tf_op jit(solution)/shard_map/power/pallas_call | solution.py:322
  46.2 1.6 add.28
  47.8 1.6 add.29
  49.4 1.9 %collective-permute-start.6 = (bf16[1,16,3072]{2,1,0:T(8,128)(2,1)}, bf16[1,16,3072]{2,1,0:T(8,128)(2,1)}, u32[]{:S(2)}, u32[]{:S(2)}) collective-permute-start(bf16[1,16,3072]{2,1,0:T(8,128)(2,1)} %add.28), channel_id=1, source_target_pairs={{0,8},{4,12},{8,0},{12,4},{16,24},{20,28},{24,16},{28,20},{1,9},{5... | collective-permute-start | bytes 294920 | tf_op jit(solution)/shard_map/ppermute | solution.py:252
  51.3 1.5 collective-permute-start.7
  53.4 5.3 %power.8 = f32[1,1,1280]{2,1,0:T(1,128)S(1)} custom-call(s32[8]{0:T(128)S(1)} %copy-done.2, bf16[1280,25600]{1,0:T(8,128)(2,1)} %refs_24_.11, bf16[1280,25600]{1,0:T(8,128)(2,1)} %refs_24_.11, bf16[1280,25600]{1,0:T(8,128)(2,1)} %refs_24_.11, bf16[1280,25600]{1,0:T(8,128)(2,1)} %refs_24_.11, bf16[1280,25600]{1,0:T(8,128)(2,1)} %refs_24_.11, ...), custom_call_target="tpu_custom_call" | custom-call | flops 8192000 | bytes 8192000 | tf_op jit(solution)/shard_map/power/pallas_call | solution.py:322
  61.4 8.5 %power.9 = f32[2,1,1280]{2,1,0:T(1,128)S(1)} custom-call(s32[8]{0:T(128)S(1)} %copy-done.2, bf16[1280,25600]{1,0:T(8,128)(2,1)} %refs_24_.11, bf16[1280,25600]{1,0:T(8,128)(2,1)} %refs_24_.11, bf16[1280,25600]{1,0:T(8,128)(2,1)} %refs_24_.11, bf16[1280,25600]{1,0:T(8,128)(2,1)} %refs_24_.11, bf16[1280,25600]{1,0:T(8,128)(2,1)} %refs_24_.11, ...), custom_call_target="tpu_custom_call" | custom-call | flops 16384000 | bytes 16384000 | tf_op jit(solution)/shard_map/power/pallas_call | solution.py:322
  71.8 3.8 %collective-permute-done.8 = bf16[2,16,3072]{2,1,0:T(8,128)(2,1)S(1)} collective-permute-done((bf16[2,16,3072]{2,1,0:T(8,128)(2,1)S(1)}, bf16[2,16,3072]{2,1,0:T(8,128)(2,1)S(1)}, u32[]{:S(2)}, u32[]{:S(2)}) %collective-permute-start.8) | collective-permute-done | bytes 196640 | tf_op jit(solution)/shard_map/ppermute | solution.py:252
  77.2 70.6 %stacks.1 = (f32[3920,128]{1,0:T(8,128)}, f32[3920,128]{1,0:T(8,128)}) custom-call(s32[8]{0:T(128)} %offsets_ref.9, s32[1]{0:T(128)} %bitcast.win_ref, f32[8,1,1280]{2,1,0:T(1,128)} %constant_dynamic-update-slice_fusion.gain_ref, f32[10,128]{1,0:T(8,128)} %convert_bitcast_fusion.quality_ref, bf16[8,16,3072]{2,1,0:T(8,128)(2,1)} %pad_maximum_fusion.u_ref, ...), custom_call_target="tpu_custom_call" | custom-call | flops 37245419520 | bytes 65536000 | tf_op jit(solution)/shard_map/stacks/pallas_call | solution.py:353
  147.9 4.2 %collective-permute-done.10 = f32[3920,128]{1,0:T(8,128)S(1)} collective-permute-done((f32[3920,128]{1,0:T(8,128)}, f32[3920,128]{1,0:T(8,128)S(1)}, u32[]{:S(2)}, u32[]{:S(2)}) %collective-permute-start.10) | collective-permute-done | bytes 2007072 | tf_op jit(solution)/shard_map/ppermute | solution.py:372
  152.1 1.9 %add.30 = f32[3920,128]{1,0:T(8,128)S(1)} add(f32[3920,128]{1,0:T(8,128)} %get-tuple-element.39, f32[3920,128]{1,0:T(8,128)S(1)} %collective-permute-done.10) | non-fusion elementwise | flops 501760 | bytes 6021120 | tf_op jit(solution)/shard_map/add | solution.py:374
  154.1 1.6 collective-permute-start.11
  155.7 12.0 %collective-permute-done.11 = bf16[1960,128]{1,0:T(8,128)(2,1)S(1)} collective-permute-done((bf16[1960,128]{1,0:T(8,128)(2,1)S(1)}, bf16[1960,128]{1,0:T(8,128)(2,1)S(1)}, u32[]{:S(2)}, u32[]{:S(2)}) %collective-permute-start.11) | collective-permute-done | bytes 501792 | tf_op jit(solution)/shard_map/ppermute | solution.py:372
  167.6 1.1 slice_add_fusion
  (56 shorter events, 13.9 us)
Async XLA Ops:
  1.5 3.2 %copy-start.2 = (s32[8]{0:T(128)S(1)}, s32[8]{0:T(128)}, u32[]{:S(2)}) copy-start(s32[8]{0:T(128)} %offsets_ref.9) | copy-start | bytes 100
  6.6 0.9 copy-start
  8.3 13.7 %collective-permute-start.1 = (bf16[2,16,3072]{2,1,0:T(8,128)(2,1)}, bf16[2,16,3072]{2,1,0:T(8,128)(2,1)}, u32[]{:S(2)}, u32[]{:S(2)}) collective-permute-start(bf16[2,16,3072]{2,1,0:T(8,128)(2,1)} %get-tuple-element.43), channel_id=1, source_target_pairs={{0,8},{4,12},{8,0},{12,4},{16,24},{20,28},{24,16},{28,20},{1,9},{5... | collective-permute-start | bytes 589832 | tf_op jit(solution)/shard_map/ppermute | solution.py:252
  11.3 10.7 %collective-permute-start = (bf16[2,16,3072]{2,1,0:T(8,128)(2,1)}, bf16[2,16,3072]{2,1,0:T(8,128)(2,1)}, u32[]{:S(2)}, u32[]{:S(2)}) collective-permute-start(bf16[2,16,3072]{2,1,0:T(8,128)(2,1)} %get-tuple-element.44), channel_id=1, source_target_pairs={{0,4},{4,0},{8,12},{12,8},{16,20},{20,16},{24,28},{28,24},{1,5},{5... | collective-permute-start | bytes 589832 | tf_op jit(solution)/shard_map/ppermute | solution.py:252
  12.8 8.6 %copy-start.9 = (s32[1280]{0:T(1024)S(1)}, s32[1280]{0:T(1024)}, u32[]{:S(2)}) copy-start(s32[1280]{0:T(1024)} %param.7) | copy-start | bytes 15364
  12.8 9.2 %copy-start.1 = (bf16[8,16,3072]{2,1,0:T(8,128)(2,1)S(1)}, bf16[8,16,3072]{2,1,0:T(8,128)(2,1)}, u32[]{:S(2)}) copy-start(bf16[8,16,3072]{2,1,0:T(8,128)(2,1)} %copy-done) | copy-start | bytes 2359300
  23.0 2.5 %copy-start.3 = (bf16[2,16,3072]{2,1,0:T(8,128)(2,1)}, bf16[2,16,3072]{2,1,0:T(8,128)(2,1)S(1)}, u32[]{:S(2)}) copy-start(bf16[2,16,3072]{2,1,0:T(8,128)(2,1)S(1)} %get-tuple-element.24) | copy-start | bytes 589828
  23.1 2.5 %copy-start.5 = (bf16[2,16,3072]{2,1,0:T(8,128)(2,1)}, bf16[2,16,3072]{2,1,0:T(8,128)(2,1)S(1)}, u32[]{:S(2)}) copy-start(bf16[2,16,3072]{2,1,0:T(8,128)(2,1)S(1)} %get-tuple-element.25) | copy-start | bytes 589828
  24.4 6.5 %collective-permute-start.3 = (bf16[1,16,3072]{2,1,0:T(8,128)(2,1)}, bf16[1,16,3072]{2,1,0:T(8,128)(2,1)}, u32[]{:S(2)}, u32[]{:S(2)}) collective-permute-start(bf16[1,16,3072]{2,1,0:T(8,128)(2,1)} %broadcast_select_fusion.8), channel_id=1, source_target_pairs={{0,4},{4,0},{8,12},{12,8},{16,20},{20,16},{24,28},{28,24},{1,5},{5... | collective-permute-start | bytes 294920 | tf_op jit(solution)/shard_map/ppermute | solution.py:252
  25.6 7.0 %collective-permute-start.2 = (bf16[1,16,3072]{2,1,0:T(8,128)(2,1)}, bf16[1,16,3072]{2,1,0:T(8,128)(2,1)}, u32[]{:S(2)}, u32[]{:S(2)}) collective-permute-start(bf16[1,16,3072]{2,1,0:T(8,128)(2,1)} %broadcast_select_fusion.11), channel_id=1, source_target_pairs={{0,8},{4,12},{8,0},{12,4},{16,24},{20,28},{24,16},{28,20},{1,9},{5... | collective-permute-start | bytes 294920 | tf_op jit(solution)/shard_map/ppermute | solution.py:252
  25.6 5.4 %copy-start.6 = (bf16[2,16,3072]{2,1,0:T(8,128)(2,1)S(1)}, bf16[2,16,3072]{2,1,0:T(8,128)(2,1)}, u32[]{:S(2)}) copy-start(bf16[2,16,3072]{2,1,0:T(8,128)(2,1)} %copy-done.5) | copy-start | bytes 589828
  25.6 6.9 %copy-start.4 = (bf16[2,16,3072]{2,1,0:T(8,128)(2,1)S(1)}, bf16[2,16,3072]{2,1,0:T(8,128)(2,1)}, u32[]{:S(2)}) copy-start(bf16[2,16,3072]{2,1,0:T(8,128)(2,1)} %copy-done.3) | copy-start | bytes 589828
  34.1 12.1 %collective-permute-start.4 = (bf16[1,16,3072]{2,1,0:T(8,128)(2,1)}, bf16[1,16,3072]{2,1,0:T(8,128)(2,1)}, u32[]{:S(2)}, u32[]{:S(2)}) collective-permute-start(bf16[1,16,3072]{2,1,0:T(8,128)(2,1)} %select_add_fusion.3), channel_id=1, source_target_pairs={{0,16},{4,20},{8,24},{12,28},{16,0},{20,4},{24,8},{28,12},{1,17},{... | collective-permute-start | bytes 294920 | tf_op jit(solution)/shard_map/ppermute | solution.py:252
  37.0 10.8 %collective-permute-start.5 = (bf16[1,16,3072]{2,1,0:T(8,128)(2,1)}, bf16[1,16,3072]{2,1,0:T(8,128)(2,1)}, u32[]{:S(2)}, u32[]{:S(2)}) collective-permute-start(bf16[1,16,3072]{2,1,0:T(8,128)(2,1)} %select_add_fusion.2), channel_id=1, source_target_pairs={{0,16},{4,20},{8,24},{12,28},{16,0},{20,4},{24,8},{28,12},{1,17},{... | collective-permute-start | bytes 294920 | tf_op jit(solution)/shard_map/ppermute | solution.py:252
  49.4 9.2 %collective-permute-start.6 = (bf16[1,16,3072]{2,1,0:T(8,128)(2,1)}, bf16[1,16,3072]{2,1,0:T(8,128)(2,1)}, u32[]{:S(2)}, u32[]{:S(2)}) collective-permute-start(bf16[1,16,3072]{2,1,0:T(8,128)(2,1)} %add.28), channel_id=1, source_target_pairs={{0,8},{4,12},{8,0},{12,4},{16,24},{20,28},{24,16},{28,20},{1,9},{5... | collective-permute-start | bytes 294920 | tf_op jit(solution)/shard_map/ppermute | solution.py:252
  51.3 8.3 %collective-permute-start.7 = (bf16[1,16,3072]{2,1,0:T(8,128)(2,1)}, bf16[1,16,3072]{2,1,0:T(8,128)(2,1)}, u32[]{:S(2)}, u32[]{:S(2)}) collective-permute-start(bf16[1,16,3072]{2,1,0:T(8,128)(2,1)} %add.29), channel_id=1, source_target_pairs={{0,4},{4,0},{8,12},{12,8},{16,20},{20,16},{24,28},{28,24},{1,5},{5... | collective-permute-start | bytes 294920 | tf_op jit(solution)/shard_map/ppermute | solution.py:252
  61.4 8.5 %copy-start.8 = (bf16[2,16,3072]{2,1,0:T(8,128)(2,1)S(1)}, bf16[2,16,3072]{2,1,0:T(8,128)(2,1)}, u32[]{:S(2)}) copy-start(bf16[2,16,3072]{2,1,0:T(8,128)(2,1)} %get-tuple-element.37) | copy-start | bytes 589828
  61.4 9.1 %copy-start.7 = (bf16[2,16,3072]{2,1,0:T(8,128)(2,1)S(1)}, bf16[2,16,3072]{2,1,0:T(8,128)(2,1)}, u32[]{:S(2)}) copy-start(bf16[2,16,3072]{2,1,0:T(8,128)(2,1)} %get-tuple-element.38) | copy-start | bytes 589828
  69.9 5.7 %collective-permute-start.8 = (bf16[2,16,3072]{2,1,0:T(8,128)(2,1)S(1)}, bf16[2,16,3072]{2,1,0:T(8,128)(2,1)S(1)}, u32[]{:S(2)}, u32[]{:S(2)}) collective-permute-start(bf16[2,16,3072]{2,1,0:T(8,128)(2,1)S(1)} %copy-done.8), channel_id=1, source_target_pairs={{0,4},{4,0},{8,12},{12,8},{16,20},{20,16},{24,28},{28,24},{1,5},{5... | collective-permute-start | bytes 589832 | tf_op jit(solution)/shard_map/ppermute | solution.py:252
  70.5 5.7 %collective-permute-start.9 = (bf16[2,16,3072]{2,1,0:T(8,128)(2,1)S(1)}, bf16[2,16,3072]{2,1,0:T(8,128)(2,1)S(1)}, u32[]{:S(2)}, u32[]{:S(2)}) collective-permute-start(bf16[2,16,3072]{2,1,0:T(8,128)(2,1)S(1)} %copy-done.7), channel_id=1, source_target_pairs={{0,8},{4,12},{8,0},{12,4},{16,24},{20,28},{24,16},{28,20},{1,9},{5... | collective-permute-start | bytes 589832 | tf_op jit(solution)/shard_map/ppermute | solution.py:252
  147.8 4.3 %collective-permute-start.10 = (f32[3920,128]{1,0:T(8,128)}, f32[3920,128]{1,0:T(8,128)S(1)}, u32[]{:S(2)}, u32[]{:S(2)}) collective-permute-start(f32[3920,128]{1,0:T(8,128)} %get-tuple-element.40), channel_id=1, source_target_pairs={{0,1},{1,0},{2,3},{3,2},{4,5},{5,4},{6,7},{7,6},{8,9},{9,8},{10,11... | collective-permute-start | bytes 6021128 | tf_op jit(solution)/shard_map/ppermute | solution.py:372
  154.1 13.5 %collective-permute-start.11 = (bf16[1960,128]{1,0:T(8,128)(2,1)S(1)}, bf16[1960,128]{1,0:T(8,128)(2,1)S(1)}, u32[]{:S(2)}, u32[]{:S(2)}) collective-permute-start(bf16[1960,128]{1,0:T(8,128)(2,1)S(1)} %slice.73), channel_id=1, source_target_pairs={{0,2},{1,3},{2,0},{3,1},{4,6},{5,7},{6,4},{7,5},{8,10},{9,11},{10,... | collective-permute-start | bytes 1505288 | tf_op jit(solution)/shard_map/ppermute | solution.py:372

commit v5 on v0

v5 whole, which is shorter than its diff:
```python
import functools
import math

import jax
import jax.numpy as jnp
from jax import lax
from jax.experimental import pallas as pl
from jax.experimental.pallas import tpu as pltpu
from jax.sharding import PartitionSpec as P

L = 3072
LAGS = 49
HALF = (LAGS - 1) // 2
EPSILON = 1e-06
LANES = 128
TILES = L // LANES
COLUMNS = 512


def lanes(rows, dtype=jnp.int32):
    return lax.broadcasted_iota(dtype, (rows, LANES), 1)


def source_kernel(offsets_ref, rows_ref, own_ref, out_ref):
    count = rows_ref.shape[0]
    seg_count = out_ref.shape[0]
    stride = rows_ref.shape[1] // seg_count
    lane = lanes(count)
    owned = own_ref[...] > 0

    def one(g, carry):
        off = offsets_ref[g]
        back = lax.rem(LANES - off, LANES)
        base = g * stride
        tiles = []
        for m in range(TILES + 1):
            start = pl.multiple_of(base + m * LANES, LANES)
            tiles.append(rows_ref[:, pl.ds(start, LANES)].astype(jnp.float32))
        cut = [jnp.where(lane < off, tiles[m + 1], tiles[m]) for m in range(TILES)]
        total = cut[0] * cut[0]
        for m in range(1, TILES):
            total = total + cut[m] * cut[m]
        power = jnp.sum(total, axis=1, keepdims=True) / L
        root = jnp.sqrt(power + EPSILON)
        for m in range(TILES):
            white = jnp.where(owned, pltpu.roll(cut[m], back, 1) / root, 0.0)
            out_ref[g, :, m * LANES : (m + 1) * LANES] = white.astype(jnp.bfloat16)
        return carry

    lax.fori_loop(0, seg_count, one, 0)


def builders(u_ref, seg, off, a_ref, count):
    lane = lanes(count)
    wide = lanes(count * (TILES + 1))
    zero = jnp.zeros((count, LANES), jnp.bfloat16)
    held = []

    def start():
        plain = [u_ref[seg, :, m * LANES : (m + 1) * LANES] for m in range(TILES)]
        turned = [pltpu.roll(tile, lax.rem(off, LANES), 1) for tile in plain]
        early = lane < off
        moved = [
            jnp.where(early, before, after)
            for before, after in zip([zero] + turned, turned + [zero])
        ]
        for part in (moved, [zero] + moved[:-1], moved[1:] + [zero]):
            held.append(jnp.concatenate(part, axis=0))

    def one(index):
        now, before, after = held
        s = index - HALF
        if s > 0:
            z = pltpu.roll(jnp.where(wide >= LANES - s, before, now), s, 1)
        elif s < 0:
            z = pltpu.roll(jnp.where(wide < -s, after, now), LANES + s, 1)
        else:
            z = now
        z = z.reshape(TILES + 1, count, LANES)
        rows = slice(index * count, (index + 1) * count)
        a_ref[0, rows, :] = jnp.where(lane < off, z[TILES], z[0])
        a_ref[1:, rows, :] = z[1:TILES]

    return [start] + [functools.partial(one, index) for index in range(LAGS)]


def weigh(x_ref, off, row, size, gain_ref):
    early = lanes(size) < off

    def square(m):
        value = x_ref[row : row + size, m * LANES : (m + 1) * LANES].astype(jnp.float32)
        return value * value

    total = jnp.where(early, square(TILES), square(0))
    for m in range(1, TILES):
        total = total + square(m)
    power = jnp.sum(jnp.transpose(total), axis=0, keepdims=True) / L
    gain_ref[:, row : row + size] = lax.rsqrt(power + EPSILON)


def dot(a_ref, x_ref, off, start, width):
    a = jnp.concatenate([a_ref[m] for m in range(TILES)], axis=1)
    rows = slice(start, start + width)
    first = jnp.where(lanes(width) < off, x_ref[rows, L : L + LANES], x_ref[rows, :LANES])
    x = jnp.concatenate([first, x_ref[rows, LANES:L]], axis=1)
    return lax.dot_general(a, x, (((1,), (1,)), ((), ())), preferred_element_type=jnp.float32)


def stack_kernel(
    src_count, blocks, scale, offsets_ref, win_ref, quality_ref, u_ref, x_ref,
    keep_ref, send_ref, a0, a1, total, gain_ref,
):
    outs = (keep_ref, send_ref)
    slots = (a0, a1)
    n = pl.program_id(0)
    last = pl.num_programs(0) - 1
    off = offsets_ref[n]
    count = u_ref.shape[1]
    groups = total.shape[0]

    @pl.when(n == 0)
    def _():
        total[...] = jnp.zeros_like(total)
        for piece in builders(u_ref, 0, off, a0, count):
            piece()

    def pieces(k):
        start, width = blocks[k]
        return [
            functools.partial(
                weigh, x_ref, off, start + at, min(LANES, width - at), gain_ref
            )
            for at in range(0, width, LANES)
        ]

    def segment(parity):
        later = jnp.minimum(n + 1, last)
        built = builders(u_ref, later, offsets_ref[later], slots[1 - parity], count)
        for piece in pieces(0):
            piece()
        for k, (start, width) in enumerate(blocks):
            term = dot(slots[parity], x_ref, off, start, width)
            share = pl.cdiv(len(built), len(blocks) - k)
            for piece in (pieces(k + 1) if k + 1 < len(blocks) else []) + built[:share]:
                piece()
            built = built[share:]
            term = term * gain_ref[:, start : start + width]
            for at in range(0, width, LANES):
                size = min(LANES, width - at)
                total[(start + at) // LANES, :, :size] += term[:, at : at + size]

    for parity in (0, 1):
        pl.when(n % 2 == parity)(functools.partial(segment, parity))

    @pl.when(n == last)
    def _():
        for group in range(groups):
            total[group] = total[group] * (quality_ref[group : group + 1, :] * scale)
        for slot in range(4):
            step = win_ref[0] ^ slot
            base = slot // 2 * src_count * LAGS * groups
            for group in range(groups):
                for i in range(src_count):
                    here = base + i * LAGS * groups + group
                    outs[slot % 2][pl.ds(here, LAGS, stride=groups), :] = total.at[group][
                        pl.ds(step * src_count + i, LAGS, stride=count), :
                    ]


def exchange(value, axis, size):
    me = lax.axis_index(axis)

    def swap(v, bit):
        return lax.ppermute(v, axis, [(d, d ^ bit) for d in range(size)])

    def scatter(v, bit):
        low = me & bit == 0
        half = v.shape[0] // 2
        one, two = v[:half], v[half:]
        return jnp.where(low, one, two) + swap(jnp.where(low, two, one), bit)

    def whole(v, bit):
        return v + swap(v, bit)

    def gather(v, bit):
        low = me & bit == 0
        other = swap(v, bit)
        return jnp.concatenate([jnp.where(low, v, other), jnp.where(low, other, v)], axis=0)

    bits = [1 << b for b in range(2, size.bit_length() - 1)]
    plans = [
        [(scatter, p), (scatter, q)] + [(whole, b) for b in bits] + [(gather, q), (gather, p)]
        for p, q in ((1, 2), (2, 1))
    ]
    half = value.shape[0] // 2
    values = [value[:half], value[half:]]
    for steps in zip(*plans):
        values = [step(v, bit) for v, (step, bit) in zip(values, steps)]
    return jnp.concatenate(values, axis=0)


def solution(mesh):
    chan = mesh.shape["chan"]
    win = mesh.shape["win"]

    def body(records, offsets, src_index, quality):
        channels, samples = records.shape
        seg_count = offsets.shape[0]
        stride = samples // seg_count
        step_count, src_count = src_index.shape
        count = step_count * src_count
        flat = src_index.reshape(-1)
        own = (lax.div(flat, channels) == lax.axis_index("chan")).astype(jnp.int32)[:, None]
        rows = jnp.take(records, lax.rem(flat, channels), axis=0, mode="clip")
        smem = pl.BlockSpec(memory_space=pltpu.SMEM)
        vmem = pl.BlockSpec(memory_space=pltpu.VMEM)
        sources = pl.pallas_call(
            source_kernel,
            out_shape=jax.ShapeDtypeStruct((seg_count, count, L), jnp.bfloat16),
            in_specs=[smem, vmem, vmem],
            out_specs=vmem,
            compiler_params=pltpu.CompilerParams(vmem_limit_bytes=32 * 2**20),
            name="sources",
        )(offsets, rows, own)

        sources = exchange(sources, "chan", chan)

        w = lax.axis_index("win").astype(jnp.int32).reshape(1)
        groups = pl.cdiv(channels, LANES)
        rows = LAGS * count
        head = channels % COLUMNS or COLUMNS
        blocks = [(0, head)] + [(at, COLUMNS) for at in range(head, channels, COLUMNS)]
        usable = jnp.pad(quality.astype(jnp.float32), (0, groups * LANES - channels))
        half = jax.ShapeDtypeStruct((2 * src_count * LAGS * groups, LANES), jnp.float32)
        scale = 1.0 / math.sqrt(seg_count * win * L)
        keep, send = pl.pallas_call(
            functools.partial(stack_kernel, src_count, blocks, scale),
            grid=(seg_count,),
            out_shape=(half, half),
            in_specs=[
                smem,
                smem,
                vmem,
                vmem,
                pl.BlockSpec((channels, stride), lambda g: (0, g)),
            ],
            out_specs=(vmem, vmem),
            scratch_shapes=[pltpu.VMEM((TILES, rows, LANES), jnp.bfloat16)] * 2
            + [
                pltpu.VMEM((groups, rows, LANES), jnp.float32),
                pltpu.VMEM((1, groups * LANES), jnp.float32),
            ],
            compiler_params=pltpu.CompilerParams(vmem_limit_bytes=52 * 2**20),
            cost_estimate=pl.CostEstimate(
                flops=2 * seg_count * rows * L * channels,
                bytes_accessed=2 * channels * samples,
                transcendentals=0,
            ),
            name="stacks",
        )(offsets, w, usable.reshape(groups, LANES), sources, records)

        def swap(v, bit):
            return lax.ppermute(v, "win", [(d, d ^ bit) for d in range(win)])

        pair = keep + swap(send.astype(jnp.bfloat16), 1).astype(jnp.float32)
        cut = pair.shape[0] // 2
        total = pair[:cut] + swap(pair[cut:].astype(jnp.bfloat16), 2).astype(jnp.float32)
        return total.reshape(1, src_count * LAGS, groups * LANES)[..., :channels]

    return jax.shard_map(
        body,
        mesh=mesh,
        in_specs=(P("chan", "win"), P("win"), P(), P("chan")),
        out_specs=P("win", None, "chan"),
        check_vma=False,
    )
```

time: 768 us -> 131 us (0.17)
  local copies, waits for them, and re-layouts: 320 us -> 3.46 us
  matrix products: 169 us -> 0 us
  other arithmetic: 134 us -> 4.86 us
  waiting for transfers between devices: 121 us -> 33.5 us
  Pallas kernels: 0 us -> 71.3 us
  starting transfers between devices: 0.63 us -> 17.1 us
  between operations: 16.3 us -> 0.14 us
    unnamed x202 -> x6, local copies, waits for them, and re-layouts: 176 us -> 0.01 us
    dot_general x4 -> x0, matrix products: 169 us -> none  [step_term(): lax.dot_general(shifted, white, (((0, 2), (0, 2)), ((), ())), preferred_e...]
    gather x28 -> x1, local copies, waits for them, and re-layouts: 103 us -> 3.23 us  [body(): rows = jnp.take(records, lax.rem(flat, channels), axis=0, mode='clip')]
    psum x1 -> x0, waiting for transfers between devices: 77.4 us -> none  [spread(): return lax.psum(kept, axis)]
    pallas_call x0 -> x2, Pallas kernels: none -> 71.3 us  [the longest x1 69.5 us: body(): pl.pallas_call(functools.partial(stack_kernel, src_count, blocks, scale),...]
    reduce_sum x1 -> x0, other arithmetic: 64.4 us -> none  [whiten(): power = jnp.mean(values * values, axis=-1, keepdims=True)]
    convert_element_type x1 -> x2, other arithmetic: 59.6 us -> 2.49 us  [the longest x1 1.8 us: body(): pair = keep + swap(send.astype(jnp.bfloat16), 1).astype(jnp.float32)]
    reduce_scatter x1 -> x0, waiting for transfers between devices: 43.1 us -> none  [body(): summed = lax.psum_scatter(terms, 'win', scatter_dimension=0, tiled=True)]
  transfers between devices with their start and end apart: 2 -> 12, of which waited for: 2 -> 12; matrix products, arithmetic and copies ran while one was open for 0% -> 0% of each run, Pallas kernels for 0% -> 0%
where the time goes in v5:
time: 131 us; the launch traced here: 130 us
  Pallas kernels  71.3 us (54%)
  waiting for transfers between devices  33.5 us (26%)
  starting transfers between devices  17.1 us (13%)
  other arithmetic  4.86 us (4%)
  local copies, waits for them, and re-layouts  3.46 us (3%)
    pallas_call x1, Pallas kernels, body(): pl.pallas_call(functools.partial(stack_kernel, src_count, blocks, scale),...  69.5 us
    ppermute x10, waiting for transfers between devices, swap(): return lax.ppermute(v, axis, [(d, d ^ bit) for d in range(size)])  19 us
    ppermute x10, starting transfers between devices, swap(): return lax.ppermute(v, axis, [(d, d ^ bit) for d in range(size)])  15.4 us
    ppermute x2, waiting for transfers between devices, swap(): return lax.ppermute(v, 'win', [(d, d ^ bit) for d in range(win)])  14.5 us
    gather x1, local copies, waits for them, and re-layouts, body(): rows = jnp.take(records, lax.rem(flat, channels), axis=0, mode='clip')  3.23 us
  transfers between devices with their start and end apart: 12, of which 12 were waited for; matrix products, arithmetic and copies ran while one was open for 0% of the time, Pallas kernels for 0%

profile of v5, /device:TPU:0, one launch (start us, length us, event | category | flops | bytes accessed | tf_op | source)
XLA Modules:
  0.0 130.4 jit_solution(11654040715719131415)
XLA Ops:
  0.0 0.7 broadcast_remainder_fusion
  1.6 3.2 %gather_fusion = bf16[16,25600]{1,0:T(8,128)(2,1)S(1)} fusion(bf16[1280,25600]{1,0:T(8,128)(2,1)} %x_ref.1, s32[1024]{0:T(1024)S(1)} %pad_clamp_fusion), kind=kCustom, calls=%fused_computation | custom fusion | bytes 1638464 | tf_op jit(solution)/shard_map/jit(_take)/gather | solution.py:214
  4.8 1.8 %sources.1 = bf16[8,16,3072]{2,1,0:T(8,128)(2,1)S(1)} custom-call(s32[8]{0:T(128)S(1)} %copy-done, bf16[16,25600]{1,0:T(8,128)(2,1)S(1)} %gather_fusion, s32[16,1]{1,0:T(8,128)S(1)} %reshape.57.own_ref), custom_call_target="tpu_custom_call" | custom-call | tf_op jit(solution)/shard_map/sources/pallas_call | solution.py:217
  6.7 3.0 %collective-permute-start = (bf16[2,16,3072]{2,1,0:T(8,128)(2,1)S(1)}, bf16[2,16,3072]{2,1,0:T(8,128)(2,1)S(1)}, u32[]{:S(2)}, u32[]{:S(2)}) collective-permute-start(bf16[2,16,3072]{2,1,0:T(8,128)(2,1)S(1)} %get-tuple-element.11), channel_id=1, source_target_pairs={{0,4},{4,0},{8,12},{12,8},{16,20},{20,16},{24,28},{28,24},{1,5},{5... | collective-permute-start | bytes 589832 | tf_op jit(solution)/shard_map/ppermute | solution.py:174
  9.7 1.6 %collective-permute-start.5 = (bf16[2,16,3072]{2,1,0:T(8,128)(2,1)S(1)}, bf16[2,16,3072]{2,1,0:T(8,128)(2,1)S(1)}, u32[]{:S(2)}, u32[]{:S(2)}) collective-permute-start(bf16[2,16,3072]{2,1,0:T(8,128)(2,1)S(1)} %get-tuple-element.12), channel_id=1, source_target_pairs={{0,8},{4,12},{8,0},{12,4},{16,24},{20,28},{24,16},{28,20},{1,9},{5... | collective-permute-start | bytes 589832 | tf_op jit(solution)/shard_map/ppermute | solution.py:174
  11.2 3.3 %collective-permute-done = bf16[2,16,3072]{2,1,0:T(8,128)(2,1)S(1)} collective-permute-done((bf16[2,16,3072]{2,1,0:T(8,128)(2,1)S(1)}, bf16[2,16,3072]{2,1,0:T(8,128)(2,1)S(1)}, u32[]{:S(2)}, u32[]{:S(2)}) %collective-permute-start) | collective-permute-done | bytes 196640 | tf_op jit(solution)/shard_map/ppermute | solution.py:174
  14.6 1.5 %collective-permute-done.5 = bf16[2,16,3072]{2,1,0:T(8,128)(2,1)S(1)} collective-permute-done((bf16[2,16,3072]{2,1,0:T(8,128)(2,1)S(1)}, bf16[2,16,3072]{2,1,0:T(8,128)(2,1)S(1)}, u32[]{:S(2)}, u32[]{:S(2)}) %collective-permute-start.5) | collective-permute-done | bytes 196640 | tf_op jit(solution)/shard_map/ppermute | solution.py:174
  16.6 1.7 %collective-permute-start.1 = (bf16[1,16,3072]{2,1,0:T(8,128)(2,1)S(1)}, bf16[1,16,3072]{2,1,0:T(8,128)(2,1)S(1)}, u32[]{:S(2)}, u32[]{:S(2)}) collective-permute-start(bf16[1,16,3072]{2,1,0:T(8,128)(2,1)S(1)} %broadcast_select_fusion.11), channel_id=1, source_target_pairs={{0,8},{4,12},{8,0},{12,4},{16,24},{20,28},{24,16},{28,20},{1,9},{5... | collective-permute-start | bytes 294920 | tf_op jit(solution)/shard_map/ppermute | solution.py:174
  18.3 2.5 %collective-permute-done.6 = bf16[1,16,3072]{2,1,0:T(8,128)(2,1)S(1)} collective-permute-done((bf16[1,16,3072]{2,1,0:T(8,128)(2,1)S(1)}, bf16[1,16,3072]{2,1,0:T(8,128)(2,1)S(1)}, u32[]{:S(2)}, u32[]{:S(2)}) %collective-permute-start.6) | collective-permute-done | bytes 98336 | tf_op jit(solution)/shard_map/ppermute | solution.py:174
  21.2 2.9 %collective-permute-start.7 = (bf16[1,16,3072]{2,1,0:T(8,128)(2,1)S(1)}, bf16[1,16,3072]{2,1,0:T(8,128)(2,1)S(1)}, u32[]{:S(2)}, u32[]{:S(2)}) collective-permute-start(bf16[1,16,3072]{2,1,0:T(8,128)(2,1)S(1)} %get-tuple-element.21), channel_id=1, source_target_pairs={{0,16},{4,20},{8,24},{12,28},{16,0},{20,4},{24,8},{28,12},{1,17},{... | collective-permute-start | bytes 294920 | tf_op jit(solution)/shard_map/ppermute | solution.py:174
  24.3 4.5 %collective-permute-done.7 = bf16[1,16,3072]{2,1,0:T(8,128)(2,1)S(1)} collective-permute-done((bf16[1,16,3072]{2,1,0:T(8,128)(2,1)S(1)}, bf16[1,16,3072]{2,1,0:T(8,128)(2,1)S(1)}, u32[]{:S(2)}, u32[]{:S(2)}) %collective-permute-start.7) | collective-permute-done | bytes 98336 | tf_op jit(solution)/shard_map/ppermute | solution.py:174
  28.8 1.6 %collective-permute-start.8 = (bf16[1,16,3072]{2,1,0:T(8,128)(2,1)S(1)}, bf16[1,16,3072]{2,1,0:T(8,128)(2,1)S(1)}, u32[]{:S(2)}, u32[]{:S(2)}) collective-permute-start(bf16[1,16,3072]{2,1,0:T(8,128)(2,1)S(1)} %add.29), channel_id=1, source_target_pairs={{0,4},{4,0},{8,12},{12,8},{16,20},{20,16},{24,28},{28,24},{1,5},{5... | collective-permute-start | bytes 294920 | tf_op jit(solution)/shard_map/ppermute | solution.py:174
  31.0 0.9 collective-permute-start.3
  31.9 1.6 %collective-permute-done.8 = bf16[1,16,3072]{2,1,0:T(8,128)(2,1)S(1)} collective-permute-done((bf16[1,16,3072]{2,1,0:T(8,128)(2,1)S(1)}, bf16[1,16,3072]{2,1,0:T(8,128)(2,1)S(1)}, u32[]{:S(2)}, u32[]{:S(2)}) %collective-permute-start.8) | collective-permute-done | bytes 98336 | tf_op jit(solution)/shard_map/ppermute | solution.py:174
  33.5 1.6 %collective-permute-start.9 = (bf16[2,16,3072]{2,1,0:T(8,128)(2,1)S(1)}, bf16[2,16,3072]{2,1,0:T(8,128)(2,1)S(1)}, u32[]{:S(2)}, u32[]{:S(2)}) collective-permute-start(bf16[2,16,3072]{2,1,0:T(8,128)(2,1)S(1)} %pad_maximum_fusion.2), channel_id=1, source_target_pairs={{0,8},{4,12},{8,0},{12,4},{16,24},{20,28},{24,16},{28,20},{1,9},{5... | collective-permute-start | bytes 589832 | tf_op jit(solution)/shard_map/ppermute | solution.py:174
  35.7 1.6 %collective-permute-start.4 = (bf16[2,16,3072]{2,1,0:T(8,128)(2,1)S(1)}, bf16[2,16,3072]{2,1,0:T(8,128)(2,1)S(1)}, u32[]{:S(2)}, u32[]{:S(2)}) collective-permute-start(bf16[2,16,3072]{2,1,0:T(8,128)(2,1)S(1)} %pad_maximum_fusion.1), channel_id=1, source_target_pairs={{0,4},{4,0},{8,12},{12,8},{16,20},{20,16},{24,28},{28,24},{1,5},{5... | collective-permute-start | bytes 589832 | tf_op jit(solution)/shard_map/ppermute | solution.py:174
  37.3 1.9 %collective-permute-done.9 = bf16[2,16,3072]{2,1,0:T(8,128)(2,1)S(1)} collective-permute-done((bf16[2,16,3072]{2,1,0:T(8,128)(2,1)S(1)}, bf16[2,16,3072]{2,1,0:T(8,128)(2,1)S(1)}, u32[]{:S(2)}, u32[]{:S(2)}) %collective-permute-start.9) | collective-permute-done | bytes 196640 | tf_op jit(solution)/shard_map/ppermute | solution.py:174
  39.3 2.2 %collective-permute-done.4 = bf16[2,16,3072]{2,1,0:T(8,128)(2,1)S(1)} collective-permute-done((bf16[2,16,3072]{2,1,0:T(8,128)(2,1)S(1)}, bf16[2,16,3072]{2,1,0:T(8,128)(2,1)S(1)}, u32[]{:S(2)}, u32[]{:S(2)}) %collective-permute-start.4) | collective-permute-done | bytes 196640 | tf_op jit(solution)/shard_map/ppermute | solution.py:174
  41.6 69.5 %stacks.1 = (f32[3920,128]{1,0:T(8,128)}, f32[3920,128]{1,0:T(8,128)}) custom-call(s32[8]{0:T(128)S(1)} %copy-done, s32[1]{0:T(128)} %bitcast.win_ref, f32[10,128]{1,0:T(8,128)S(1)} %convert_bitcast_fusion.quality_ref, bf16[8,16,3072]{2,1,0:T(8,128)(2,1)S(1)} %pad_maximum_fusion.u_ref, bf16[1280,25600]{1,0:T(8,128)(2,1)} %x_ref.1), custom_call_target="tpu_custom_call" | custom-call | flops 49325015040 | bytes 65536000 | tf_op jit(solution)/shard_map/stacks/pallas_call | solution.py:236
  111.1 1.8 %convert_element_type.29 = bf16[3920,128]{1,0:T(8,128)(2,1)S(1)} convert(f32[3920,128]{1,0:T(8,128)} %get-tuple-element.8) | non-fusion elementwise | flops 501760 | bytes 3010560 | tf_op jit(solution)/shard_map/convert_element_type | solution.py:265
  113.0 2.6 %collective-permute-done.10 = bf16[3920,128]{1,0:T(8,128)(2,1)S(1)} collective-permute-done((bf16[3920,128]{1,0:T(8,128)(2,1)S(1)}, bf16[3920,128]{1,0:T(8,128)(2,1)S(1)}, u32[]{:S(2)}, u32[]{:S(2)}) %collective-permute-start.10) | collective-permute-done | bytes 1003552 | tf_op jit(solution)/shard_map/ppermute | solution.py:263
  115.8 1.6 %collective-permute-start.11 = (bf16[1960,128]{1,0:T(8,128)(2,1)S(1)}, bf16[1960,128]{1,0:T(8,128)(2,1)S(1)}, u32[]{:S(2)}, u32[]{:S(2)}) collective-permute-start(bf16[1960,128]{1,0:T(8,128)(2,1)S(1)} %slice.77), channel_id=1, source_target_pairs={{0,2},{1,3},{2,0},{3,1},{4,6},{5,7},{6,4},{7,5},{8,10},{9,11},{10,... | collective-permute-start | bytes 1505288 | tf_op jit(solution)/shard_map/ppermute | solution.py:263
  117.4 12.0 %collective-permute-done.11 = bf16[1960,128]{1,0:T(8,128)(2,1)S(1)} collective-permute-done((bf16[1960,128]{1,0:T(8,128)(2,1)S(1)}, bf16[1960,128]{1,0:T(8,128)(2,1)S(1)}, u32[]{:S(2)}, u32[]{:S(2)}) %collective-permute-start.11) | collective-permute-done | bytes 501792 | tf_op jit(solution)/shard_map/ppermute | solution.py:263
  129.4 1.0 slice_add_fusion
  (33 shorter events, 3.7 us)
Async XLA Ops:
  1.5 3.2 %copy-start = (s32[8]{0:T(128)S(1)}, s32[8]{0:T(128)}, u32[]{:S(2)}) copy-start(s32[8]{0:T(128)} %offsets_ref.3) | copy-start | bytes 100
  6.6 23.8 %copy-start.2 = (s32[1280]{0:T(1024)S(1)}, s32[1280]{0:T(1024)}, u32[]{:S(2)}) copy-start(s32[1280]{0:T(1024)} %param.7) | copy-start | bytes 15364
  6.7 7.9 %collective-permute-start = (bf16[2,16,3072]{2,1,0:T(8,128)(2,1)S(1)}, bf16[2,16,3072]{2,1,0:T(8,128)(2,1)S(1)}, u32[]{:S(2)}, u32[]{:S(2)}) collective-permute-start(bf16[2,16,3072]{2,1,0:T(8,128)(2,1)S(1)} %get-tuple-element.11), channel_id=1, source_target_pairs={{0,4},{4,0},{8,12},{12,8},{16,20},{20,16},{24,28},{28,24},{1,5},{5... | collective-permute-start | bytes 589832 | tf_op jit(solution)/shard_map/ppermute | solution.py:174
  9.7 6.4 %collective-permute-start.5 = (bf16[2,16,3072]{2,1,0:T(8,128)(2,1)S(1)}, bf16[2,16,3072]{2,1,0:T(8,128)(2,1)S(1)}, u32[]{:S(2)}, u32[]{:S(2)}) collective-permute-start(bf16[2,16,3072]{2,1,0:T(8,128)(2,1)S(1)} %get-tuple-element.12), channel_id=1, source_target_pairs={{0,8},{4,12},{8,0},{12,4},{16,24},{20,28},{24,16},{28,20},{1,9},{5... | collective-permute-start | bytes 589832 | tf_op jit(solution)/shard_map/ppermute | solution.py:174
  16.1 4.7 %collective-permute-start.6 = (bf16[1,16,3072]{2,1,0:T(8,128)(2,1)S(1)}, bf16[1,16,3072]{2,1,0:T(8,128)(2,1)S(1)}, u32[]{:S(2)}, u32[]{:S(2)}) collective-permute-start(bf16[1,16,3072]{2,1,0:T(8,128)(2,1)S(1)} %broadcast_select_fusion.8), channel_id=1, source_target_pairs={{0,4},{4,0},{8,12},{12,8},{16,20},{20,16},{24,28},{28,24},{1,5},{5... | collective-permute-start | bytes 294920 | tf_op jit(solution)/shard_map/ppermute | solution.py:174
  16.6 4.6 %collective-permute-start.1 = (bf16[1,16,3072]{2,1,0:T(8,128)(2,1)S(1)}, bf16[1,16,3072]{2,1,0:T(8,128)(2,1)S(1)}, u32[]{:S(2)}, u32[]{:S(2)}) collective-permute-start(bf16[1,16,3072]{2,1,0:T(8,128)(2,1)S(1)} %broadcast_select_fusion.11), channel_id=1, source_target_pairs={{0,8},{4,12},{8,0},{12,4},{16,24},{20,28},{24,16},{28,20},{1,9},{5... | collective-permute-start | bytes 294920 | tf_op jit(solution)/shard_map/ppermute | solution.py:174
  21.2 7.5 %collective-permute-start.7 = (bf16[1,16,3072]{2,1,0:T(8,128)(2,1)S(1)}, bf16[1,16,3072]{2,1,0:T(8,128)(2,1)S(1)}, u32[]{:S(2)}, u32[]{:S(2)}) collective-permute-start(bf16[1,16,3072]{2,1,0:T(8,128)(2,1)S(1)} %get-tuple-element.21), channel_id=1, source_target_pairs={{0,16},{4,20},{8,24},{12,28},{16,0},{20,4},{24,8},{28,12},{1,17},{... | collective-permute-start | bytes 294920 | tf_op jit(solution)/shard_map/ppermute | solution.py:174
  24.2 6.8 %collective-permute-start.2 = (bf16[1,16,3072]{2,1,0:T(8,128)(2,1)S(1)}, bf16[1,16,3072]{2,1,0:T(8,128)(2,1)S(1)}, u32[]{:S(2)}, u32[]{:S(2)}) collective-permute-start(bf16[1,16,3072]{2,1,0:T(8,128)(2,1)S(1)} %get-tuple-element.22), channel_id=1, source_target_pairs={{0,16},{4,20},{8,24},{12,28},{16,0},{20,4},{24,8},{28,12},{1,17},{... | collective-permute-start | bytes 294920 | tf_op jit(solution)/shard_map/ppermute | solution.py:174
  28.8 4.7 %collective-permute-start.8 = (bf16[1,16,3072]{2,1,0:T(8,128)(2,1)S(1)}, bf16[1,16,3072]{2,1,0:T(8,128)(2,1)S(1)}, u32[]{:S(2)}, u32[]{:S(2)}) collective-permute-start(bf16[1,16,3072]{2,1,0:T(8,128)(2,1)S(1)} %add.29), channel_id=1, source_target_pairs={{0,4},{4,0},{8,12},{12,8},{16,20},{20,16},{24,28},{28,24},{1,5},{5... | collective-permute-start | bytes 294920 | tf_op jit(solution)/shard_map/ppermute | solution.py:174
  31.0 4.7 %collective-permute-start.3 = (bf16[1,16,3072]{2,1,0:T(8,128)(2,1)S(1)}, bf16[1,16,3072]{2,1,0:T(8,128)(2,1)S(1)}, u32[]{:S(2)}, u32[]{:S(2)}) collective-permute-start(bf16[1,16,3072]{2,1,0:T(8,128)(2,1)S(1)} %add.26), channel_id=1, source_target_pairs={{0,8},{4,12},{8,0},{12,4},{16,24},{20,28},{24,16},{28,20},{1,9},{5... | collective-permute-start | bytes 294920 | tf_op jit(solution)/shard_map/ppermute | solution.py:174
  33.5 5.7 %collective-permute-start.9 = (bf16[2,16,3072]{2,1,0:T(8,128)(2,1)S(1)}, bf16[2,16,3072]{2,1,0:T(8,128)(2,1)S(1)}, u32[]{:S(2)}, u32[]{:S(2)}) collective-permute-start(bf16[2,16,3072]{2,1,0:T(8,128)(2,1)S(1)} %pad_maximum_fusion.2), channel_id=1, source_target_pairs={{0,8},{4,12},{8,0},{12,4},{16,24},{20,28},{24,16},{28,20},{1,9},{5... | collective-permute-start | bytes 589832 | tf_op jit(solution)/shard_map/ppermute | solution.py:174
  35.7 5.7 %collective-permute-start.4 = (bf16[2,16,3072]{2,1,0:T(8,128)(2,1)S(1)}, bf16[2,16,3072]{2,1,0:T(8,128)(2,1)S(1)}, u32[]{:S(2)}, u32[]{:S(2)}) collective-permute-start(bf16[2,16,3072]{2,1,0:T(8,128)(2,1)S(1)} %pad_maximum_fusion.1), channel_id=1, source_target_pairs={{0,4},{4,0},{8,12},{12,8},{16,20},{20,16},{24,28},{28,24},{1,5},{5... | collective-permute-start | bytes 589832 | tf_op jit(solution)/shard_map/ppermute | solution.py:174
  111.1 4.5 %copy-start.1 = (f32[3920,128]{1,0:T(8,128)S(1)}, f32[3920,128]{1,0:T(8,128)}, u32[]{:S(2)}) copy-start(f32[3920,128]{1,0:T(8,128)} %get-tuple-element.7) | copy-start | bytes 6021124
  112.9 2.7 %collective-permute-start.10 = (bf16[3920,128]{1,0:T(8,128)(2,1)S(1)}, bf16[3920,128]{1,0:T(8,128)(2,1)S(1)}, u32[]{:S(2)}, u32[]{:S(2)}) collective-permute-start(bf16[3920,128]{1,0:T(8,128)(2,1)S(1)} %convert_element_type.29), channel_id=1, source_target_pairs={{0,1},{1,0},{2,3},{3,2},{4,5},{5,4},{6,7},{7,6},{8,9},{9,8},{10,11... | collective-permute-start | bytes 3010568 | tf_op jit(solution)/shard_map/ppermute | solution.py:263
  115.8 13.5 %collective-permute-start.11 = (bf16[1960,128]{1,0:T(8,128)(2,1)S(1)}, bf16[1960,128]{1,0:T(8,128)(2,1)S(1)}, u32[]{:S(2)}, u32[]{:S(2)}) collective-permute-start(bf16[1960,128]{1,0:T(8,128)(2,1)S(1)} %slice.77), channel_id=1, source_target_pairs={{0,2},{1,3},{2,0},{3,1},{4,6},{5,7},{6,4},{7,5},{8,10},{9,11},{10,... | collective-permute-start | bytes 1505288 | tf_op jit(solution)/shard_map/ppermute | solution.py:263

commit v6 on v5

--- a/solution.py
+++ b/solution.py
@@ -21,12 +21,16 @@
     return lax.broadcasted_iota(dtype, (rows, LANES), 1)
 
 
-def source_kernel(offsets_ref, rows_ref, own_ref, out_ref):
+def source_kernel(channels, offsets_ref, flat_ref, me_ref, rows_ref, out_ref):
     count = rows_ref.shape[0]
     seg_count = out_ref.shape[0]
     stride = rows_ref.shape[1] // seg_count
     lane = lanes(count)
-    owned = own_ref[...] > 0
+    row = lax.broadcasted_iota(jnp.int32, (count, LANES), 0)
+    holder = jnp.zeros((count, LANES), jnp.int32)
+    for i in range(count):
+        holder = jnp.where(row == i, lax.div(flat_ref[i], channels), holder)
+    owned = holder == me_ref[0]
 
     def one(g, carry):
         off = offsets_ref[g]
@@ -88,29 +92,34 @@
     early = lanes(size) < off
 
     def square(m):
-        value = x_ref[row : row + size, m * LANES : (m + 1) * LANES].astype(jnp.float32)
+        value = x_ref[row : row + size, m * LANES : (m + 1) * LANES]
         return value * value
 
-    total = jnp.where(early, square(TILES), square(0))
-    for m in range(1, TILES):
-        total = total + square(m)
+    squares = [jnp.where(early, square(TILES), square(0))]
+    squares += [square(m) for m in range(1, TILES)]
+    total = jnp.zeros((size, LANES), jnp.float32)
+    for m in range(0, TILES, 4):
+        four = (squares[m] + squares[m + 1]) + (squares[m + 2] + squares[m + 3])
+        total = total + four.astype(jnp.float32)
     power = jnp.sum(jnp.transpose(total), axis=0, keepdims=True) / L
     gain_ref[:, row : row + size] = lax.rsqrt(power + EPSILON)
 
 
-def dot(a_ref, x_ref, off, start, width):
-    a = jnp.concatenate([a_ref[m] for m in range(TILES)], axis=1)
+def dot(a_ref, x_ref, off, start, width, begin, end):
+    a = jnp.concatenate([a_ref[m] for m in range(begin, end)], axis=1)
     rows = slice(start, start + width)
-    first = jnp.where(lanes(width) < off, x_ref[rows, L : L + LANES], x_ref[rows, :LANES])
-    x = jnp.concatenate([first, x_ref[rows, LANES:L]], axis=1)
+    x = x_ref[rows, max(begin, 1) * LANES : end * LANES]
+    if begin == 0:
+        first = jnp.where(lanes(width) < off, x_ref[rows, L : L + LANES], x_ref[rows, :LANES])
+        x = jnp.concatenate([first, x], axis=1)
     return lax.dot_general(a, x, (((1,), (1,)), ((), ())), preferred_element_type=jnp.float32)
 
 
 def stack_kernel(
     src_count, blocks, scale, offsets_ref, win_ref, quality_ref, u_ref, x_ref,
-    keep_ref, send_ref, a0, a1, total, gain_ref,
+    keep_ref, send_ref, a0, a1, total, gain_ref, away_ref,
 ):
-    outs = (keep_ref, send_ref)
+    outs = (keep_ref, away_ref)
     slots = (a0, a1)
     n = pl.program_id(0)
     last = pl.num_programs(0) - 1
@@ -139,12 +148,16 @@
         for piece in pieces(0):
             piece()
         for k, (start, width) in enumerate(blocks):
-            term = dot(slots[parity], x_ref, off, start, width)
+            cuts = (0, TILES) if width == COLUMNS else (0, TILES // 2, TILES)
+            terms = [
+                dot(slots[parity], x_ref, off, start, width, begin, end)
+                for begin, end in zip(cuts, cuts[1:])
+            ]
             share = pl.cdiv(len(built), len(blocks) - k)
             for piece in (pieces(k + 1) if k + 1 < len(blocks) else []) + built[:share]:
                 piece()
             built = built[share:]
-            term = term * gain_ref[:, start : start + width]
+            term = sum(terms[1:], terms[0]) * gain_ref[:, start : start + width]
             for at in range(0, width, LANES):
                 size = min(LANES, width - at)
                 total[(start + at) // LANES, :, :size] += term[:, at : at + size]
@@ -165,6 +178,7 @@
                     outs[slot % 2][pl.ds(here, LAGS, stride=groups), :] = total.at[group][
                         pl.ds(step * src_count + i, LAGS, stride=count), :
                     ]
+        send_ref[...] = away_ref[...].astype(jnp.bfloat16)
 
 
 def exchange(value, axis, size):
@@ -210,18 +224,18 @@
         step_count, src_count = src_index.shape
         count = step_count * src_count
         flat = src_index.reshape(-1)
-        own = (lax.div(flat, channels) == lax.axis_index("chan")).astype(jnp.int32)[:, None]
-        rows = jnp.take(records, lax.rem(flat, channels), axis=0, mode="clip")
+        me = lax.axis_index("chan").astype(jnp.int32).reshape(1)
+        rows = records.at[lax.rem(flat, channels)].get(mode="promise_in_bounds")
         smem = pl.BlockSpec(memory_space=pltpu.SMEM)
         vmem = pl.BlockSpec(memory_space=pltpu.VMEM)
         sources = pl.pallas_call(
-            source_kernel,
+            functools.partial(source_kernel, channels),
             out_shape=jax.ShapeDtypeStruct((seg_count, count, L), jnp.bfloat16),
-            in_specs=[smem, vmem, vmem],
+            in_specs=[smem, smem, smem, vmem],
             out_specs=vmem,
             compiler_params=pltpu.CompilerParams(vmem_limit_bytes=32 * 2**20),
             name="sources",
-        )(offsets, rows, own)
+        )(offsets, flat, me, rows)
 
         sources = exchange(sources, "chan", chan)
 
@@ -236,7 +250,7 @@
         keep, send = pl.pallas_call(
             functools.partial(stack_kernel, src_count, blocks, scale),
             grid=(seg_count,),
-            out_shape=(half, half),
+            out_shape=(half, jax.ShapeDtypeStruct(half.shape, jnp.bfloat16)),
             in_specs=[
                 smem,
                 smem,
@@ -249,6 +263,7 @@
             + [
                 pltpu.VMEM((groups, rows, LANES), jnp.float32),
                 pltpu.VMEM((1, groups * LANES), jnp.float32),
+                pltpu.VMEM(half.shape, jnp.float32),
             ],
             compiler_params=pltpu.CompilerParams(vmem_limit_bytes=52 * 2**20),
             cost_estimate=pl.CostEstimate(
@@ -262,7 +277,7 @@
         def swap(v, bit):
             return lax.ppermute(v, "win", [(d, d ^ bit) for d in range(win)])
 
-        pair = keep + swap(send.astype(jnp.bfloat16), 1).astype(jnp.float32)
+        pair = keep + swap(send, 1).astype(jnp.float32)
         cut = pair.shape[0] // 2
         total = pair[:cut] + swap(pair[cut:].astype(jnp.bfloat16), 2).astype(jnp.float32)
         return total.reshape(1, src_count * LAGS, groups * LANES)[..., :channels]

time: 131 us -> 127 us (0.969)
  Pallas kernels: 71.3 us -> 68.2 us
    pallas_call x1, Pallas kernels: 69.5 us -> 66.3 us  [body(): pl.pallas_call(functools.partial(stack_kernel, src_count, blocks, scale),...]
    convert_element_type x2 -> x0, other arithmetic: 2.49 us -> none  [the longest x1 1.8 us: body(): pair = keep + swap(send.astype(jnp.bfloat16), 1).astype(jnp.float32)]
    add x1, other arithmetic: 0.16 us -> 1.82 us  [body(): pair = keep + swap(send, 1).astype(jnp.float32)]
where the time goes in v6:
time: 127 us
  Pallas kernels  68.2 us (54%)
  waiting for transfers between devices  33.5 us (26%)
  starting transfers between devices  17 us (13%)
  local copies, waits for them, and re-layouts  4.14 us (3%)
  other arithmetic  4.1 us (3%)
    pallas_call x1, Pallas kernels, body(): pl.pallas_call(functools.partial(stack_kernel, src_count, blocks, scale),...  66.3 us
    ppermute x10, waiting for transfers between devices, swap(): return lax.ppermute(v, axis, [(d, d ^ bit) for d in range(size)])  19 us
    ppermute x10, starting transfers between devices, swap(): return lax.ppermute(v, axis, [(d, d ^ bit) for d in range(size)])  15.4 us
    ppermute x2, waiting for transfers between devices, swap(): return lax.ppermute(v, 'win', [(d, d ^ bit) for d in range(win)])  14.5 us
    gather x1, local copies, waits for them, and re-layouts, body(): rows = records.at[lax.rem(flat, channels)].get(mode='promise_in_bounds')  3.23 us
  transfers between devices with their start and end apart: 12, of which 12 were waited for; matrix products, arithmetic and copies ran while one was open for 0% of the time, Pallas kernels for 0%

profile of v6, /device:TPU:0, one launch (start us, length us, event | category | flops | bytes accessed | tf_op | source)
XLA Modules:
  0.0 127.1 jit_solution(9386449684789435310)
XLA Ops:
  0.0 0.8 reshape.38.flat_ref
  1.6 3.2 %gather_fusion = bf16[16,25600]{1,0:T(8,128)(2,1)S(1)} fusion(bf16[1280,25600]{1,0:T(8,128)(2,1)} %x_ref.1, s32[1024]{0:T(1024)S(1)} %pad_clamp_fusion), kind=kCustom, calls=%fused_computation | custom fusion | bytes 1638464 | tf_op jit(solution)/shard_map/gather | solution.py:228
  4.8 1.9 %sources.1 = bf16[8,16,3072]{2,1,0:T(8,128)(2,1)S(1)} custom-call(s32[8]{0:T(128)S(1)} %copy-done, s32[16]{0:T(128)S(1)} %reshape.38.flat_ref, s32[1]{0:T(128)} %bitcast.2.me_ref, bf16[16,25600]{1,0:T(8,128)(2,1)S(1)} %gather_fusion), custom_call_target="tpu_custom_call" | custom-call | tf_op jit(solution)/shard_map/sources/pallas_call | solution.py:231
  6.8 3.0 %collective-permute-start = (bf16[2,16,3072]{2,1,0:T(8,128)(2,1)S(1)}, bf16[2,16,3072]{2,1,0:T(8,128)(2,1)S(1)}, u32[]{:S(2)}, u32[]{:S(2)}) collective-permute-start(bf16[2,16,3072]{2,1,0:T(8,128)(2,1)S(1)} %get-tuple-element.11), channel_id=1, source_target_pairs={{0,4},{4,0},{8,12},{12,8},{16,20},{20,16},{24,28},{28,24},{1,5},{5... | collective-permute-start | bytes 589832 | tf_op jit(solution)/shard_map/ppermute | solution.py:188
  9.8 1.6 %collective-permute-start.5 = (bf16[2,16,3072]{2,1,0:T(8,128)(2,1)S(1)}, bf16[2,16,3072]{2,1,0:T(8,128)(2,1)S(1)}, u32[]{:S(2)}, u32[]{:S(2)}) collective-permute-start(bf16[2,16,3072]{2,1,0:T(8,128)(2,1)S(1)} %get-tuple-element.12), channel_id=1, source_target_pairs={{0,8},{4,12},{8,0},{12,4},{16,24},{20,28},{24,16},{28,20},{1,9},{5... | collective-permute-start | bytes 589832 | tf_op jit(solution)/shard_map/ppermute | solution.py:188
  11.3 3.3 %collective-permute-done = bf16[2,16,3072]{2,1,0:T(8,128)(2,1)S(1)} collective-permute-done((bf16[2,16,3072]{2,1,0:T(8,128)(2,1)S(1)}, bf16[2,16,3072]{2,1,0:T(8,128)(2,1)S(1)}, u32[]{:S(2)}, u32[]{:S(2)}) %collective-permute-start) | collective-permute-done | bytes 196640 | tf_op jit(solution)/shard_map/ppermute | solution.py:188
  14.7 1.5 %collective-permute-done.5 = bf16[2,16,3072]{2,1,0:T(8,128)(2,1)S(1)} collective-permute-done((bf16[2,16,3072]{2,1,0:T(8,128)(2,1)S(1)}, bf16[2,16,3072]{2,1,0:T(8,128)(2,1)S(1)}, u32[]{:S(2)}, u32[]{:S(2)}) %collective-permute-start.5) | collective-permute-done | bytes 196640 | tf_op jit(solution)/shard_map/ppermute | solution.py:188
  16.7 1.7 %collective-permute-start.1 = (bf16[1,16,3072]{2,1,0:T(8,128)(2,1)S(1)}, bf16[1,16,3072]{2,1,0:T(8,128)(2,1)S(1)}, u32[]{:S(2)}, u32[]{:S(2)}) collective-permute-start(bf16[1,16,3072]{2,1,0:T(8,128)(2,1)S(1)} %broadcast_select_fusion.11), channel_id=1, source_target_pairs={{0,8},{4,12},{8,0},{12,4},{16,24},{20,28},{24,16},{28,20},{1,9},{5... | collective-permute-start | bytes 294920 | tf_op jit(solution)/shard_map/ppermute | solution.py:188
  18.4 2.5 %collective-permute-done.6 = bf16[1,16,3072]{2,1,0:T(8,128)(2,1)S(1)} collective-permute-done((bf16[1,16,3072]{2,1,0:T(8,128)(2,1)S(1)}, bf16[1,16,3072]{2,1,0:T(8,128)(2,1)S(1)}, u32[]{:S(2)}, u32[]{:S(2)}) %collective-permute-start.6) | collective-permute-done | bytes 98336 | tf_op jit(solution)/shard_map/ppermute | solution.py:188
  21.3 2.9 %collective-permute-start.7 = (bf16[1,16,3072]{2,1,0:T(8,128)(2,1)S(1)}, bf16[1,16,3072]{2,1,0:T(8,128)(2,1)S(1)}, u32[]{:S(2)}, u32[]{:S(2)}) collective-permute-start(bf16[1,16,3072]{2,1,0:T(8,128)(2,1)S(1)} %get-tuple-element.21), channel_id=1, source_target_pairs={{0,16},{4,20},{8,24},{12,28},{16,0},{20,4},{24,8},{28,12},{1,17},{... | collective-permute-start | bytes 294920 | tf_op jit(solution)/shard_map/ppermute | solution.py:188
  24.4 4.5 %collective-permute-done.7 = bf16[1,16,3072]{2,1,0:T(8,128)(2,1)S(1)} collective-permute-done((bf16[1,16,3072]{2,1,0:T(8,128)(2,1)S(1)}, bf16[1,16,3072]{2,1,0:T(8,128)(2,1)S(1)}, u32[]{:S(2)}, u32[]{:S(2)}) %collective-permute-start.7) | collective-permute-done | bytes 98336 | tf_op jit(solution)/shard_map/ppermute | solution.py:188
  28.9 1.6 %collective-permute-start.8 = (bf16[1,16,3072]{2,1,0:T(8,128)(2,1)S(1)}, bf16[1,16,3072]{2,1,0:T(8,128)(2,1)S(1)}, u32[]{:S(2)}, u32[]{:S(2)}) collective-permute-start(bf16[1,16,3072]{2,1,0:T(8,128)(2,1)S(1)} %add.40), channel_id=1, source_target_pairs={{0,4},{4,0},{8,12},{12,8},{16,20},{20,16},{24,28},{28,24},{1,5},{5... | collective-permute-start | bytes 294920 | tf_op jit(solution)/shard_map/ppermute | solution.py:188
  31.1 0.9 collective-permute-start.3
  32.0 1.6 %collective-permute-done.8 = bf16[1,16,3072]{2,1,0:T(8,128)(2,1)S(1)} collective-permute-done((bf16[1,16,3072]{2,1,0:T(8,128)(2,1)S(1)}, bf16[1,16,3072]{2,1,0:T(8,128)(2,1)S(1)}, u32[]{:S(2)}, u32[]{:S(2)}) %collective-permute-start.8) | collective-permute-done | bytes 98336 | tf_op jit(solution)/shard_map/ppermute | solution.py:188
  33.6 1.6 %collective-permute-start.9 = (bf16[2,16,3072]{2,1,0:T(8,128)(2,1)S(1)}, bf16[2,16,3072]{2,1,0:T(8,128)(2,1)S(1)}, u32[]{:S(2)}, u32[]{:S(2)}) collective-permute-start(bf16[2,16,3072]{2,1,0:T(8,128)(2,1)S(1)} %pad_maximum_fusion.2), channel_id=1, source_target_pairs={{0,8},{4,12},{8,0},{12,4},{16,24},{20,28},{24,16},{28,20},{1,9},{5... | collective-permute-start | bytes 589832 | tf_op jit(solution)/shard_map/ppermute | solution.py:188
  35.8 1.6 %collective-permute-start.4 = (bf16[2,16,3072]{2,1,0:T(8,128)(2,1)S(1)}, bf16[2,16,3072]{2,1,0:T(8,128)(2,1)S(1)}, u32[]{:S(2)}, u32[]{:S(2)}) collective-permute-start(bf16[2,16,3072]{2,1,0:T(8,128)(2,1)S(1)} %pad_maximum_fusion.1), channel_id=1, source_target_pairs={{0,4},{4,0},{8,12},{12,8},{16,20},{20,16},{24,28},{28,24},{1,5},{5... | collective-permute-start | bytes 589832 | tf_op jit(solution)/shard_map/ppermute | solution.py:188
  37.4 1.9 %collective-permute-done.9 = bf16[2,16,3072]{2,1,0:T(8,128)(2,1)S(1)} collective-permute-done((bf16[2,16,3072]{2,1,0:T(8,128)(2,1)S(1)}, bf16[2,16,3072]{2,1,0:T(8,128)(2,1)S(1)}, u32[]{:S(2)}, u32[]{:S(2)}) %collective-permute-start.9) | collective-permute-done | bytes 196640 | tf_op jit(solution)/shard_map/ppermute | solution.py:188
  39.4 2.2 %collective-permute-done.4 = bf16[2,16,3072]{2,1,0:T(8,128)(2,1)S(1)} collective-permute-done((bf16[2,16,3072]{2,1,0:T(8,128)(2,1)S(1)}, bf16[2,16,3072]{2,1,0:T(8,128)(2,1)S(1)}, u32[]{:S(2)}, u32[]{:S(2)}) %collective-permute-start.4) | collective-permute-done | bytes 196640 | tf_op jit(solution)/shard_map/ppermute | solution.py:188
  41.7 66.3 %stacks.1 = (f32[3920,128]{1,0:T(8,128)}, bf16[3920,128]{1,0:T(8,128)(2,1)S(1)}) custom-call(s32[8]{0:T(128)S(1)} %copy-done, s32[1]{0:T(128)} %bitcast.win_ref, f32[10,128]{1,0:T(8,128)S(1)} %convert_bitcast_fusion.quality_ref, bf16[8,16,3072]{2,1,0:T(8,128)(2,1)S(1)} %pad_maximum_fusion.u_ref, bf16[1280,25600]{1,0:T(8,128)(2,1)} %x_ref.1), custom_call_target="tpu_custom_call" | custom-call | flops 49325015040 | bytes 65536000 | tf_op jit(solution)/shard_map/stacks/pallas_call | solution.py:250
  108.0 2.6 %collective-permute-done.10 = bf16[3920,128]{1,0:T(8,128)(2,1)S(1)} collective-permute-done((bf16[3920,128]{1,0:T(8,128)(2,1)S(1)}, bf16[3920,128]{1,0:T(8,128)(2,1)S(1)}, u32[]{:S(2)}, u32[]{:S(2)}) %collective-permute-start.10) | collective-permute-done | bytes 1003552 | tf_op jit(solution)/shard_map/ppermute | solution.py:278
  110.6 1.8 %convert_add_fusion = f32[3920,128]{1,0:T(8,128)S(1)} fusion(f32[3920,128]{1,0:T(8,128)} %get-tuple-element.7, bf16[3920,128]{1,0:T(8,128)(2,1)S(1)} %collective-permute-done.10), kind=kLoop, calls=%fused_computation.1 | loop fusion | flops 1003520 | bytes 5017600 | tf_op jit(solution)/shard_map/add | solution.py:280
  112.5 1.6 %collective-permute-start.11 = (bf16[1960,128]{1,0:T(8,128)(2,1)S(1)}, bf16[1960,128]{1,0:T(8,128)(2,1)S(1)}, u32[]{:S(2)}, u32[]{:S(2)}) collective-permute-start(bf16[1960,128]{1,0:T(8,128)(2,1)S(1)} %slice.77), channel_id=1, source_target_pairs={{0,2},{1,3},{2,0},{3,1},{4,6},{5,7},{6,4},{7,5},{8,10},{9,11},{10,... | collective-permute-start | bytes 1505288 | tf_op jit(solution)/shard_map/ppermute | solution.py:278
  114.1 12.0 %collective-permute-done.11 = bf16[1960,128]{1,0:T(8,128)(2,1)S(1)} collective-permute-done((bf16[1960,128]{1,0:T(8,128)(2,1)S(1)}, bf16[1960,128]{1,0:T(8,128)(2,1)S(1)}, u32[]{:S(2)}, u32[]{:S(2)}) %collective-permute-start.11) | collective-permute-done | bytes 501792 | tf_op jit(solution)/shard_map/ppermute | solution.py:278
  126.0 1.1 slice_add_fusion
  (30 shorter events, 3.4 us)
Async XLA Ops:
  1.6 3.2 %copy-start = (s32[8]{0:T(128)S(1)}, s32[8]{0:T(128)}, u32[]{:S(2)}) copy-start(s32[8]{0:T(128)} %offsets_ref.3) | copy-start | bytes 100
  6.7 23.8 %copy-start.1 = (s32[1280]{0:T(1024)S(1)}, s32[1280]{0:T(1024)}, u32[]{:S(2)}) copy-start(s32[1280]{0:T(1024)} %param.7) | copy-start | bytes 15364
  6.8 7.9 %collective-permute-start = (bf16[2,16,3072]{2,1,0:T(8,128)(2,1)S(1)}, bf16[2,16,3072]{2,1,0:T(8,128)(2,1)S(1)}, u32[]{:S(2)}, u32[]{:S(2)}) collective-permute-start(bf16[2,16,3072]{2,1,0:T(8,128)(2,1)S(1)} %get-tuple-element.11), channel_id=1, source_target_pairs={{0,4},{4,0},{8,12},{12,8},{16,20},{20,16},{24,28},{28,24},{1,5},{5... | collective-permute-start | bytes 589832 | tf_op jit(solution)/shard_map/ppermute | solution.py:188
  9.8 6.4 %collective-permute-start.5 = (bf16[2,16,3072]{2,1,0:T(8,128)(2,1)S(1)}, bf16[2,16,3072]{2,1,0:T(8,128)(2,1)S(1)}, u32[]{:S(2)}, u32[]{:S(2)}) collective-permute-start(bf16[2,16,3072]{2,1,0:T(8,128)(2,1)S(1)} %get-tuple-element.12), channel_id=1, source_target_pairs={{0,8},{4,12},{8,0},{12,4},{16,24},{20,28},{24,16},{28,20},{1,9},{5... | collective-permute-start | bytes 589832 | tf_op jit(solution)/shard_map/ppermute | solution.py:188
  16.2 4.7 %collective-permute-start.6 = (bf16[1,16,3072]{2,1,0:T(8,128)(2,1)S(1)}, bf16[1,16,3072]{2,1,0:T(8,128)(2,1)S(1)}, u32[]{:S(2)}, u32[]{:S(2)}) collective-permute-start(bf16[1,16,3072]{2,1,0:T(8,128)(2,1)S(1)} %broadcast_select_fusion.8), channel_id=1, source_target_pairs={{0,4},{4,0},{8,12},{12,8},{16,20},{20,16},{24,28},{28,24},{1,5},{5... | collective-permute-start | bytes 294920 | tf_op jit(solution)/shard_map/ppermute | solution.py:188
  16.7 4.6 %collective-permute-start.1 = (bf16[1,16,3072]{2,1,0:T(8,128)(2,1)S(1)}, bf16[1,16,3072]{2,1,0:T(8,128)(2,1)S(1)}, u32[]{:S(2)}, u32[]{:S(2)}) collective-permute-start(bf16[1,16,3072]{2,1,0:T(8,128)(2,1)S(1)} %broadcast_select_fusion.11), channel_id=1, source_target_pairs={{0,8},{4,12},{8,0},{12,4},{16,24},{20,28},{24,16},{28,20},{1,9},{5... | collective-permute-start | bytes 294920 | tf_op jit(solution)/shard_map/ppermute | solution.py:188
  21.3 7.5 %collective-permute-start.7 = (bf16[1,16,3072]{2,1,0:T(8,128)(2,1)S(1)}, bf16[1,16,3072]{2,1,0:T(8,128)(2,1)S(1)}, u32[]{:S(2)}, u32[]{:S(2)}) collective-permute-start(bf16[1,16,3072]{2,1,0:T(8,128)(2,1)S(1)} %get-tuple-element.21), channel_id=1, source_target_pairs={{0,16},{4,20},{8,24},{12,28},{16,0},{20,4},{24,8},{28,12},{1,17},{... | collective-permute-start | bytes 294920 | tf_op jit(solution)/shard_map/ppermute | solution.py:188
  24.3 6.8 %collective-permute-start.2 = (bf16[1,16,3072]{2,1,0:T(8,128)(2,1)S(1)}, bf16[1,16,3072]{2,1,0:T(8,128)(2,1)S(1)}, u32[]{:S(2)}, u32[]{:S(2)}) collective-permute-start(bf16[1,16,3072]{2,1,0:T(8,128)(2,1)S(1)} %get-tuple-element.22), channel_id=1, source_target_pairs={{0,16},{4,20},{8,24},{12,28},{16,0},{20,4},{24,8},{28,12},{1,17},{... | collective-permute-start | bytes 294920 | tf_op jit(solution)/shard_map/ppermute | solution.py:188
  28.9 4.7 %collective-permute-start.8 = (bf16[1,16,3072]{2,1,0:T(8,128)(2,1)S(1)}, bf16[1,16,3072]{2,1,0:T(8,128)(2,1)S(1)}, u32[]{:S(2)}, u32[]{:S(2)}) collective-permute-start(bf16[1,16,3072]{2,1,0:T(8,128)(2,1)S(1)} %add.40), channel_id=1, source_target_pairs={{0,4},{4,0},{8,12},{12,8},{16,20},{20,16},{24,28},{28,24},{1,5},{5... | collective-permute-start | bytes 294920 | tf_op jit(solution)/shard_map/ppermute | solution.py:188
  31.1 4.7 %collective-permute-start.3 = (bf16[1,16,3072]{2,1,0:T(8,128)(2,1)S(1)}, bf16[1,16,3072]{2,1,0:T(8,128)(2,1)S(1)}, u32[]{:S(2)}, u32[]{:S(2)}) collective-permute-start(bf16[1,16,3072]{2,1,0:T(8,128)(2,1)S(1)} %add.37), channel_id=1, source_target_pairs={{0,8},{4,12},{8,0},{12,4},{16,24},{20,28},{24,16},{28,20},{1,9},{5... | collective-permute-start | bytes 294920 | tf_op jit(solution)/shard_map/ppermute | solution.py:188
  33.6 5.7 %collective-permute-start.9 = (bf16[2,16,3072]{2,1,0:T(8,128)(2,1)S(1)}, bf16[2,16,3072]{2,1,0:T(8,128)(2,1)S(1)}, u32[]{:S(2)}, u32[]{:S(2)}) collective-permute-start(bf16[2,16,3072]{2,1,0:T(8,128)(2,1)S(1)} %pad_maximum_fusion.2), channel_id=1, source_target_pairs={{0,8},{4,12},{8,0},{12,4},{16,24},{20,28},{24,16},{28,20},{1,9},{5... | collective-permute-start | bytes 589832 | tf_op jit(solution)/shard_map/ppermute | solution.py:188
  35.8 5.7 %collective-permute-start.4 = (bf16[2,16,3072]{2,1,0:T(8,128)(2,1)S(1)}, bf16[2,16,3072]{2,1,0:T(8,128)(2,1)S(1)}, u32[]{:S(2)}, u32[]{:S(2)}) collective-permute-start(bf16[2,16,3072]{2,1,0:T(8,128)(2,1)S(1)} %pad_maximum_fusion.1), channel_id=1, source_target_pairs={{0,4},{4,0},{8,12},{12,8},{16,20},{20,16},{24,28},{28,24},{1,5},{5... | collective-permute-start | bytes 589832 | tf_op jit(solution)/shard_map/ppermute | solution.py:188
  108.0 2.6 %collective-permute-start.10 = (bf16[3920,128]{1,0:T(8,128)(2,1)S(1)}, bf16[3920,128]{1,0:T(8,128)(2,1)S(1)}, u32[]{:S(2)}, u32[]{:S(2)}) collective-permute-start(bf16[3920,128]{1,0:T(8,128)(2,1)S(1)} %get-tuple-element.8), channel_id=1, source_target_pairs={{0,1},{1,0},{2,3},{3,2},{4,5},{5,4},{6,7},{7,6},{8,9},{9,8},{10,11... | collective-permute-start | bytes 3010568 | tf_op jit(solution)/shard_map/ppermute | solution.py:278
  112.5 13.5 %collective-permute-start.11 = (bf16[1960,128]{1,0:T(8,128)(2,1)S(1)}, bf16[1960,128]{1,0:T(8,128)(2,1)S(1)}, u32[]{:S(2)}, u32[]{:S(2)}) collective-permute-start(bf16[1960,128]{1,0:T(8,128)(2,1)S(1)} %slice.77), channel_id=1, source_target_pairs={{0,2},{1,3},{2,0},{3,1},{4,6},{5,7},{6,4},{7,5},{8,10},{9,11},{10,... | collective-permute-start | bytes 1505288 | tf_op jit(solution)/shard_map/ppermute | solution.py:278

commit v7 on v6

--- a/solution.py
+++ b/solution.py
@@ -116,24 +116,32 @@
 
 
 def stack_kernel(
-    src_count, blocks, scale, offsets_ref, win_ref, quality_ref, u_ref, x_ref,
-    keep_ref, send_ref, a0, a1, total, gain_ref, away_ref,
+    blocks, scale, offsets_ref, quality_ref, u_ref, records_ref,
+    keep0, keep1, send0, send1, a0, a1, x0, x1, total, gain_ref, sems,
 ):
-    outs = (keep_ref, away_ref)
     slots = (a0, a1)
+    x_slots = (x0, x1)
+    stride = x0.shape[1]
     n = pl.program_id(0)
     last = pl.num_programs(0) - 1
     off = offsets_ref[n]
     count = u_ref.shape[1]
     groups = total.shape[0]
 
+    def fetch(seg, slot):
+        start = pl.multiple_of(seg * stride, LANES)
+        return pltpu.make_async_copy(
+            records_ref.at[:, pl.ds(start, stride)], x_slots[slot], sems.at[slot]
+        )
+
     @pl.when(n == 0)
     def _():
+        fetch(0, 0).start()
         total[...] = jnp.zeros_like(total)
         for piece in builders(u_ref, 0, off, a0, count):
             piece()
 
-    def pieces(k):
+    def pieces(k, x_ref):
         start, width = blocks[k]
         return [
             functools.partial(
@@ -143,9 +151,16 @@
         ]
 
     def segment(parity):
+        x_ref = x_slots[parity]
+        fetch(n, parity).wait()
+
+        @pl.when(n < last)
+        def _():
+            fetch(n + 1, 1 - parity).start()
+
         later = jnp.minimum(n + 1, last)
         built = builders(u_ref, later, offsets_ref[later], slots[1 - parity], count)
-        for piece in pieces(0):
+        for piece in pieces(0, x_ref):
             piece()
         for k, (start, width) in enumerate(blocks):
             cuts = (0, TILES) if width == COLUMNS else (0, TILES // 2, TILES)
@@ -154,7 +169,7 @@
                 for begin, end in zip(cuts, cuts[1:])
             ]
             share = pl.cdiv(len(built), len(blocks) - k)
-            for piece in (pieces(k + 1) if k + 1 < len(blocks) else []) + built[:share]:
+            for piece in (pieces(k + 1, x_ref) if k + 1 < len(blocks) else []) + built[:share]:
                 piece()
             built = built[share:]
             term = sum(terms[1:], terms[0]) * gain_ref[:, start : start + width]
@@ -167,18 +182,32 @@
 
     @pl.when(n == last)
     def _():
-        for group in range(groups):
-            total[group] = total[group] * (quality_ref[group : group + 1, :] * scale)
-        for slot in range(4):
-            step = win_ref[0] ^ slot
-            base = slot // 2 * src_count * LAGS * groups
-            for group in range(groups):
-                for i in range(src_count):
-                    here = base + i * LAGS * groups + group
-                    outs[slot % 2][pl.ds(here, LAGS, stride=groups), :] = total.at[group][
-                        pl.ds(step * src_count + i, LAGS, stride=count), :
-                    ]
-        send_ref[...] = away_ref[...].astype(jnp.bfloat16)
+        low = lax.broadcasted_iota(jnp.int32, (LAGS, 8, LANES), 1) < 4
+        for pair in range(groups // 2):
+            parts = []
+            for group in (2 * pair, 2 * pair + 1):
+                sums = total[group] * (quality_ref[group : group + 1, :] * scale)
+                parts.append(sums.reshape(LAGS, count, LANES))
+            rows = slice(pair * LAGS * 8, (pair + 1) * LAGS * 8)
+            for begin, outs in ((0, (keep0, keep1)), (8, (send0, send1))):
+                a, b = (part[:, begin : begin + 8] for part in parts)
+                near = jnp.where(low, a, pltpu.roll(b, 4, 1))
+                far = jnp.where(low, pltpu.roll(a, 4, 1), b)
+                for out, value in zip(outs, (near, far)):
+                    out[rows, :] = value.reshape(LAGS * 8, LANES).astype(out.dtype)
+
+
+def finish_kernel(src_count, keep_ref, core_ref, chip_ref, out_ref, total):
+    total[...] = (
+        keep_ref[...] + core_ref[...].astype(jnp.float32) + chip_ref[...].astype(jnp.float32)
+    )
+    groups = out_ref.shape[0] // (src_count * LAGS)
+    for group in range(groups):
+        for i in range(src_count):
+            row = group // 2 * LAGS * 8 + group % 2 * 4 + i
+            out_ref[pl.ds(i * LAGS * groups + group, LAGS, stride=groups), :] = total[
+                pl.ds(row, LAGS, stride=8), :
+            ]
 
 
 def exchange(value, axis, size):
@@ -223,7 +252,11 @@
         stride = samples // seg_count
         step_count, src_count = src_index.shape
         count = step_count * src_count
-        flat = src_index.reshape(-1)
+        w = lax.axis_index("win")
+        steps = [src_index[k : k + 1] for k in range(step_count)]
+        steps = [jnp.where(w & 1 == 0, steps[k], steps[k ^ 1]) for k in range(step_count)]
+        steps = [jnp.where(w & 2 == 0, steps[k], steps[k ^ 2]) for k in range(step_count)]
+        flat = jnp.concatenate([steps[k] for k in (0, 2, 1, 3)], axis=0).reshape(-1)
         me = lax.axis_index("chan").astype(jnp.int32).reshape(1)
         rows = records.at[lax.rem(flat, channels)].get(mode="promise_in_bounds")
         smem = pl.BlockSpec(memory_space=pltpu.SMEM)
@@ -239,31 +272,28 @@
 
         sources = exchange(sources, "chan", chan)
 
-        w = lax.axis_index("win").astype(jnp.int32).reshape(1)
         groups = pl.cdiv(channels, LANES)
+        even = groups + groups % 2
         rows = LAGS * count
         head = channels % COLUMNS or COLUMNS
         blocks = [(0, head)] + [(at, COLUMNS) for at in range(head, channels, COLUMNS)]
-        usable = jnp.pad(quality.astype(jnp.float32), (0, groups * LANES - channels))
-        half = jax.ShapeDtypeStruct((2 * src_count * LAGS * groups, LANES), jnp.float32)
+        usable = jnp.pad(quality.astype(jnp.float32), (0, even * LANES - channels))
+        shape = (even // 2 * LAGS * 8, LANES)
+        kept = jax.ShapeDtypeStruct(shape, jnp.float32)
+        sent = jax.ShapeDtypeStruct(shape, jnp.bfloat16)
         scale = 1.0 / math.sqrt(seg_count * win * L)
-        keep, send = pl.pallas_call(
-            functools.partial(stack_kernel, src_count, blocks, scale),
+        keep0, keep1, send0, send1 = pl.pallas_call(
+            functools.partial(stack_kernel, blocks, scale),
             grid=(seg_count,),
-            out_shape=(half, jax.ShapeDtypeStruct(half.shape, jnp.bfloat16)),
-            in_specs=[
-                smem,
-                smem,
-                vmem,
-                vmem,
-                pl.BlockSpec((channels, stride), lambda g: (0, g)),
-            ],
-            out_specs=(vmem, vmem),
+            out_shape=(kept, kept, sent, sent),
+            in_specs=[smem, vmem, vmem, pl.BlockSpec(memory_space=pl.ANY)],
+            out_specs=(vmem,) * 4,
             scratch_shapes=[pltpu.VMEM((TILES, rows, LANES), jnp.bfloat16)] * 2
+            + [pltpu.VMEM((channels, stride), jnp.bfloat16)] * 2
             + [
-                pltpu.VMEM((groups, rows, LANES), jnp.float32),
-                pltpu.VMEM((1, groups * LANES), jnp.float32),
-                pltpu.VMEM(half.shape, jnp.float32),
+                pltpu.VMEM((even, rows, LANES), jnp.float32),
+                pltpu.VMEM((1, even * LANES), jnp.float32),
+                pltpu.SemaphoreType.DMA((2,)),
             ],
             compiler_params=pltpu.CompilerParams(vmem_limit_bytes=52 * 2**20),
             cost_estimate=pl.CostEstimate(
@@ -272,14 +302,23 @@
                 transcendentals=0,
             ),
             name="stacks",
-        )(offsets, w, usable.reshape(groups, LANES), sources, records)
+        )(offsets, usable.reshape(even, LANES), sources, records)
 
         def swap(v, bit):
             return lax.ppermute(v, "win", [(d, d ^ bit) for d in range(win)])
 
-        pair = keep + swap(send, 1).astype(jnp.float32)
-        cut = pair.shape[0] // 2
-        total = pair[:cut] + swap(pair[cut:].astype(jnp.bfloat16), 2).astype(jnp.float32)
+        far = keep1 + swap(send1, 1).astype(jnp.float32)
+        chip = swap(far.astype(jnp.bfloat16), 2)
+        core = swap(send0, 1)
+        total = pl.pallas_call(
+            functools.partial(finish_kernel, src_count),
+            out_shape=jax.ShapeDtypeStruct((src_count * LAGS * groups, LANES), jnp.float32),
+            in_specs=[vmem] * 3,
+            out_specs=vmem,
+            scratch_shapes=[pltpu.VMEM(shape, jnp.float32)],
+            compiler_params=pltpu.CompilerParams(vmem_limit_bytes=16 * 2**20),
+            name="finish",
+        )(keep0, core, chip)
         return total.reshape(1, src_count * LAGS, groups * LANES)[..., :channels]
 
     return jax.shard_map(

time: 127 us -> 139 us (1.094)
  Pallas kernels: 68.2 us -> 79.8 us
  waiting for transfers between devices: 33.5 us -> 31.3 us
  local copies, waits for them, and re-layouts: 4.14 us -> 5.91 us
    pallas_call x1 -> x2, Pallas kernels: 66.3 us -> 77.9 us  [the longest x1 76.4 us: body(): pl.pallas_call(functools.partial(stack_kernel, blocks, scale), grid=(seg_...]
    add x2 -> x0, other arithmetic: 2.92 us -> none  [the longest x1 1.82 us: body(): pair = keep + swap(send, 1).astype(jnp.float32)]
    unnamed x4 -> x6, local copies, waits for them, and re-layouts: 0.01 us -> 2.51 us
    ppermute x2 -> x3, waiting for transfers between devices: 14.5 us -> 13.4 us  [swap(): return lax.ppermute(v, 'win', [(d, d ^ bit) for d in range(win)])]
  transfers between devices with their start and end apart: 12 -> 13, of which waited for: 12 -> 11; matrix products, arithmetic and copies ran while one was open for 0% -> 2% of each run, Pallas kernels for 0% -> 0%
where the time goes in v7:
time: 139 us; the launch traced here: 138 us
  Pallas kernels  79.8 us (57%)
  waiting for transfers between devices  31.3 us (23%)
  starting transfers between devices  18 us (13%)
  local copies, waits for them, and re-layouts  5.91 us (4%)
  other arithmetic  3.34 us (2%)
    pallas_call x1, Pallas kernels, body(): pl.pallas_call(functools.partial(stack_kernel, blocks, scale), grid=(seg_...  76.4 us
    ppermute x10, waiting for transfers between devices, swap(): return lax.ppermute(v, axis, [(d, d ^ bit) for d in range(size)])  17.9 us
    ppermute x10, starting transfers between devices, swap(): return lax.ppermute(v, axis, [(d, d ^ bit) for d in range(size)])  15.9 us
    ppermute x3, waiting for transfers between devices, swap(): return lax.ppermute(v, 'win', [(d, d ^ bit) for d in range(win)])  13.4 us
    gather x1, local copies, waits for them, and re-layouts, body(): rows = records.at[lax.rem(flat, channels)].get(mode='promise_in_bounds')  3.23 us
  transfers between devices with their start and end apart: 13, of which 11 were waited for; matrix products, arithmetic and copies ran while one was open for 2% of the time, Pallas kernels for 0%

profile of v7, /device:TPU:0, one launch (start us, length us, event | category | flops | bytes accessed | tf_op | source)
XLA Modules:
  0.0 138.5 jit_solution(5553088533760471739)
XLA Ops:
  1.0 3.2 %gather_fusion = bf16[16,25600]{1,0:T(8,128)(2,1)S(1)} fusion(bf16[1280,25600]{1,0:T(8,128)(2,1)} %records_ref.1, s32[1024]{0:T(1024)S(1)} %pad_clamp_fusion), kind=kCustom, calls=%fused_computation | custom fusion | bytes 1638464 | tf_op jit(solution)/shard_map/gather | solution.py:261
  4.9 1.9 %sources.1 = bf16[8,16,3072]{2,1,0:T(8,128)(2,1)S(1)} custom-call(s32[8]{0:T(128)S(1)} %copy-done.1, s32[16]{0:T(128)S(1)} %reshape.34.flat_ref, s32[1]{0:T(128)} %bitcast.1.me_ref, bf16[16,25600]{1,0:T(8,128)(2,1)S(1)} %gather_fusion), custom_call_target="tpu_custom_call" | custom-call | tf_op jit(solution)/shard_map/sources/pallas_call | solution.py:264
  6.9 3.0 %collective-permute-start = (bf16[2,16,3072]{2,1,0:T(8,128)(2,1)S(1)}, bf16[2,16,3072]{2,1,0:T(8,128)(2,1)S(1)}, u32[]{:S(2)}, u32[]{:S(2)}) collective-permute-start(bf16[2,16,3072]{2,1,0:T(8,128)(2,1)S(1)} %get-tuple-element.15), channel_id=1, source_target_pairs={{0,4},{4,0},{8,12},{12,8},{16,20},{20,16},{24,28},{28,24},{1,5},{5... | collective-permute-start | bytes 589832 | tf_op jit(solution)/shard_map/ppermute | solution.py:217
  9.9 1.6 %collective-permute-start.5 = (bf16[2,16,3072]{2,1,0:T(8,128)(2,1)S(1)}, bf16[2,16,3072]{2,1,0:T(8,128)(2,1)S(1)}, u32[]{:S(2)}, u32[]{:S(2)}) collective-permute-start(bf16[2,16,3072]{2,1,0:T(8,128)(2,1)S(1)} %get-tuple-element.16), channel_id=1, source_target_pairs={{0,8},{4,12},{8,0},{12,4},{16,24},{20,28},{24,16},{28,20},{1,9},{5... | collective-permute-start | bytes 589832 | tf_op jit(solution)/shard_map/ppermute | solution.py:217
  11.5 3.3 %collective-permute-done = bf16[2,16,3072]{2,1,0:T(8,128)(2,1)S(1)} collective-permute-done((bf16[2,16,3072]{2,1,0:T(8,128)(2,1)S(1)}, bf16[2,16,3072]{2,1,0:T(8,128)(2,1)S(1)}, u32[]{:S(2)}, u32[]{:S(2)}) %collective-permute-start) | collective-permute-done | bytes 196640 | tf_op jit(solution)/shard_map/ppermute | solution.py:217
  14.8 1.5 %collective-permute-done.5 = bf16[2,16,3072]{2,1,0:T(8,128)(2,1)S(1)} collective-permute-done((bf16[2,16,3072]{2,1,0:T(8,128)(2,1)S(1)}, bf16[2,16,3072]{2,1,0:T(8,128)(2,1)S(1)}, u32[]{:S(2)}, u32[]{:S(2)}) %collective-permute-start.5) | collective-permute-done | bytes 196640 | tf_op jit(solution)/shard_map/ppermute | solution.py:217
  16.8 1.7 %collective-permute-start.1 = (bf16[1,16,3072]{2,1,0:T(8,128)(2,1)S(1)}, bf16[1,16,3072]{2,1,0:T(8,128)(2,1)S(1)}, u32[]{:S(2)}, u32[]{:S(2)}) collective-permute-start(bf16[1,16,3072]{2,1,0:T(8,128)(2,1)S(1)} %broadcast_select_fusion.11), channel_id=1, source_target_pairs={{0,8},{4,12},{8,0},{12,4},{16,24},{20,28},{24,16},{28,20},{1,9},{5... | collective-permute-start | bytes 294920 | tf_op jit(solution)/shard_map/ppermute | solution.py:217
  18.5 2.5 %collective-permute-done.6 = bf16[1,16,3072]{2,1,0:T(8,128)(2,1)S(1)} collective-permute-done((bf16[1,16,3072]{2,1,0:T(8,128)(2,1)S(1)}, bf16[1,16,3072]{2,1,0:T(8,128)(2,1)S(1)}, u32[]{:S(2)}, u32[]{:S(2)}) %collective-permute-start.6) | collective-permute-done | bytes 98336 | tf_op jit(solution)/shard_map/ppermute | solution.py:217
  21.4 2.9 %collective-permute-start.7 = (bf16[1,16,3072]{2,1,0:T(8,128)(2,1)S(1)}, bf16[1,16,3072]{2,1,0:T(8,128)(2,1)S(1)}, u32[]{:S(2)}, u32[]{:S(2)}) collective-permute-start(bf16[1,16,3072]{2,1,0:T(8,128)(2,1)S(1)} %get-tuple-element.31), channel_id=1, source_target_pairs={{0,16},{4,20},{8,24},{12,28},{16,0},{20,4},{24,8},{28,12},{1,17},{... | collective-permute-start | bytes 294920 | tf_op jit(solution)/shard_map/ppermute | solution.py:217
  24.5 4.5 %collective-permute-done.7 = bf16[1,16,3072]{2,1,0:T(8,128)(2,1)S(1)} collective-permute-done((bf16[1,16,3072]{2,1,0:T(8,128)(2,1)S(1)}, bf16[1,16,3072]{2,1,0:T(8,128)(2,1)S(1)}, u32[]{:S(2)}, u32[]{:S(2)}) %collective-permute-start.7) | collective-permute-done | bytes 98336 | tf_op jit(solution)/shard_map/ppermute | solution.py:217
  29.0 1.6 %collective-permute-start.8 = (bf16[1,16,3072]{2,1,0:T(8,128)(2,1)S(1)}, bf16[1,16,3072]{2,1,0:T(8,128)(2,1)S(1)}, u32[]{:S(2)}, u32[]{:S(2)}) collective-permute-start(bf16[1,16,3072]{2,1,0:T(8,128)(2,1)S(1)} %add.37), channel_id=1, source_target_pairs={{0,4},{4,0},{8,12},{12,8},{16,20},{20,16},{24,28},{28,24},{1,5},{5... | collective-permute-start | bytes 294920 | tf_op jit(solution)/shard_map/ppermute | solution.py:217
  31.3 1.5 %collective-permute-start.3 = (bf16[1,16,3072]{2,1,0:T(8,128)(2,1)S(1)}, bf16[1,16,3072]{2,1,0:T(8,128)(2,1)S(1)}, u32[]{:S(2)}, u32[]{:S(2)}) collective-permute-start(bf16[1,16,3072]{2,1,0:T(8,128)(2,1)S(1)} %add.34), channel_id=1, source_target_pairs={{0,8},{4,12},{8,0},{12,4},{16,24},{20,28},{24,16},{28,20},{1,9},{5... | collective-permute-start | bytes 294920 | tf_op jit(solution)/shard_map/ppermute | solution.py:217
  32.8 0.9 collective-permute-done.8
  33.7 1.6 %collective-permute-start.9 = (bf16[2,16,3072]{2,1,0:T(8,128)(2,1)S(1)}, bf16[2,16,3072]{2,1,0:T(8,128)(2,1)S(1)}, u32[]{:S(2)}, u32[]{:S(2)}) collective-permute-start(bf16[2,16,3072]{2,1,0:T(8,128)(2,1)S(1)} %pad_maximum_fusion.2), channel_id=1, source_target_pairs={{0,8},{4,12},{8,0},{12,4},{16,24},{20,28},{24,16},{28,20},{1,9},{5... | collective-permute-start | bytes 589832 | tf_op jit(solution)/shard_map/ppermute | solution.py:217
  36.0 1.5 %collective-permute-start.4 = (bf16[2,16,3072]{2,1,0:T(8,128)(2,1)S(1)}, bf16[2,16,3072]{2,1,0:T(8,128)(2,1)S(1)}, u32[]{:S(2)}, u32[]{:S(2)}) collective-permute-start(bf16[2,16,3072]{2,1,0:T(8,128)(2,1)S(1)} %pad_maximum_fusion.1), channel_id=1, source_target_pairs={{0,4},{4,0},{8,12},{12,8},{16,20},{20,16},{24,28},{28,24},{1,5},{5... | collective-permute-start | bytes 589832 | tf_op jit(solution)/shard_map/ppermute | solution.py:217
  37.5 1.9 %collective-permute-done.9 = bf16[2,16,3072]{2,1,0:T(8,128)(2,1)S(1)} collective-permute-done((bf16[2,16,3072]{2,1,0:T(8,128)(2,1)S(1)}, bf16[2,16,3072]{2,1,0:T(8,128)(2,1)S(1)}, u32[]{:S(2)}, u32[]{:S(2)}) %collective-permute-start.9) | collective-permute-done | bytes 196640 | tf_op jit(solution)/shard_map/ppermute | solution.py:217
  39.5 2.3 %collective-permute-done.4 = bf16[2,16,3072]{2,1,0:T(8,128)(2,1)S(1)} collective-permute-done((bf16[2,16,3072]{2,1,0:T(8,128)(2,1)S(1)}, bf16[2,16,3072]{2,1,0:T(8,128)(2,1)S(1)}, u32[]{:S(2)}, u32[]{:S(2)}) %collective-permute-start.4) | collective-permute-done | bytes 196640 | tf_op jit(solution)/shard_map/ppermute | solution.py:217
  42.6 76.4 %stacks.1 = (f32[1960,128]{1,0:T(8,128)}, f32[1960,128]{1,0:T(8,128)}, bf16[1960,128]{1,0:T(8,128)(2,1)S(1)}, bf16[1960,128]{1,0:T(8,128)(2,1)S(1)}) custom-call(s32[8]{0:T(128)S(1)} %copy-done.2, f32[10,128]{1,0:T(8,128)S(1)} %convert_bitcast_fusion.quality_ref, bf16[8,16,3072]{2,1,0:T(8,128)(2,1)S(1)} %pad_maximum_fusion.u_ref, bf16[1280,25600]{1,0:T(8,128)(2,1)} %records_ref.1), custom_call_target="tpu_custom_call" | custom-call | flops 49325015040 | bytes 65536000 | tf_op jit(solution)/shard_map/stacks/pallas_call | solution.py:285
  119.6 1.4 collective-permute-done.11
  121.0 1.3 add_convert_fusion
  122.3 1.5 %collective-permute-start.12 = (bf16[1960,128]{1,0:T(8,128)(2,1)S(1)}, bf16[1960,128]{1,0:T(8,128)(2,1)S(1)}, u32[]{:S(2)}, u32[]{:S(2)}) collective-permute-start(bf16[1960,128]{1,0:T(8,128)(2,1)S(1)} %add_convert_fusion), channel_id=1, source_target_pairs={{0,2},{1,3},{2,0},{3,1},{4,6},{5,7},{6,4},{7,5},{8,10},{9,11},{10,... | collective-permute-start | bytes 1505288 | tf_op jit(solution)/shard_map/ppermute | solution.py:308
  123.8 12.1 %collective-permute-done.12.chip_ref = bf16[1960,128]{1,0:T(8,128)(2,1)S(1)} collective-permute-done((bf16[1960,128]{1,0:T(8,128)(2,1)S(1)}, bf16[1960,128]{1,0:T(8,128)(2,1)S(1)}, u32[]{:S(2)}, u32[]{:S(2)}) %collective-permute-start.12) | collective-permute-done | bytes 501792 | tf_op jit(solution)/shard_map/ppermute | solution.py:308
  135.8 1.2 copy-done
  137.0 1.4 %finish.1 = f32[1960,128]{1,0:T(8,128)} custom-call(f32[1960,128]{1,0:T(8,128)S(1)} %copy-done, bf16[1960,128]{1,0:T(8,128)(2,1)S(1)} %collective-permute-done.10.core_ref, bf16[1960,128]{1,0:T(8,128)(2,1)S(1)} %collective-permute-done.12.chip_ref), custom_call_target="tpu_custom_call" | custom-call | tf_op jit(solution)/shard_map/finish/pallas_call | solution.py:313
  (34 shorter events, 5.6 us)
Async XLA Ops:
  4.3 0.7 copy-start.1
  6.9 7.9 %collective-permute-start = (bf16[2,16,3072]{2,1,0:T(8,128)(2,1)S(1)}, bf16[2,16,3072]{2,1,0:T(8,128)(2,1)S(1)}, u32[]{:S(2)}, u32[]{:S(2)}) collective-permute-start(bf16[2,16,3072]{2,1,0:T(8,128)(2,1)S(1)} %get-tuple-element.15), channel_id=1, source_target_pairs={{0,4},{4,0},{8,12},{12,8},{16,20},{20,16},{24,28},{28,24},{1,5},{5... | collective-permute-start | bytes 589832 | tf_op jit(solution)/shard_map/ppermute | solution.py:217
  9.9 6.4 %collective-permute-start.5 = (bf16[2,16,3072]{2,1,0:T(8,128)(2,1)S(1)}, bf16[2,16,3072]{2,1,0:T(8,128)(2,1)S(1)}, u32[]{:S(2)}, u32[]{:S(2)}) collective-permute-start(bf16[2,16,3072]{2,1,0:T(8,128)(2,1)S(1)} %get-tuple-element.16), channel_id=1, source_target_pairs={{0,8},{4,12},{8,0},{12,4},{16,24},{20,28},{24,16},{28,20},{1,9},{5... | collective-permute-start | bytes 589832 | tf_op jit(solution)/shard_map/ppermute | solution.py:217
  16.3 4.7 %collective-permute-start.6 = (bf16[1,16,3072]{2,1,0:T(8,128)(2,1)S(1)}, bf16[1,16,3072]{2,1,0:T(8,128)(2,1)S(1)}, u32[]{:S(2)}, u32[]{:S(2)}) collective-permute-start(bf16[1,16,3072]{2,1,0:T(8,128)(2,1)S(1)} %broadcast_select_fusion.8), channel_id=1, source_target_pairs={{0,4},{4,0},{8,12},{12,8},{16,20},{20,16},{24,28},{28,24},{1,5},{5... | collective-permute-start | bytes 294920 | tf_op jit(solution)/shard_map/ppermute | solution.py:217
  16.8 4.6 %collective-permute-start.1 = (bf16[1,16,3072]{2,1,0:T(8,128)(2,1)S(1)}, bf16[1,16,3072]{2,1,0:T(8,128)(2,1)S(1)}, u32[]{:S(2)}, u32[]{:S(2)}) collective-permute-start(bf16[1,16,3072]{2,1,0:T(8,128)(2,1)S(1)} %broadcast_select_fusion.11), channel_id=1, source_target_pairs={{0,8},{4,12},{8,0},{12,4},{16,24},{20,28},{24,16},{28,20},{1,9},{5... | collective-permute-start | bytes 294920 | tf_op jit(solution)/shard_map/ppermute | solution.py:217
  21.4 7.5 %collective-permute-start.7 = (bf16[1,16,3072]{2,1,0:T(8,128)(2,1)S(1)}, bf16[1,16,3072]{2,1,0:T(8,128)(2,1)S(1)}, u32[]{:S(2)}, u32[]{:S(2)}) collective-permute-start(bf16[1,16,3072]{2,1,0:T(8,128)(2,1)S(1)} %get-tuple-element.31), channel_id=1, source_target_pairs={{0,16},{4,20},{8,24},{12,28},{16,0},{20,4},{24,8},{28,12},{1,17},{... | collective-permute-start | bytes 294920 | tf_op jit(solution)/shard_map/ppermute | solution.py:217
  24.4 6.9 %collective-permute-start.2 = (bf16[1,16,3072]{2,1,0:T(8,128)(2,1)S(1)}, bf16[1,16,3072]{2,1,0:T(8,128)(2,1)S(1)}, u32[]{:S(2)}, u32[]{:S(2)}) collective-permute-start(bf16[1,16,3072]{2,1,0:T(8,128)(2,1)S(1)} %get-tuple-element.32), channel_id=1, source_target_pairs={{0,16},{4,20},{8,24},{12,28},{16,0},{20,4},{24,8},{28,12},{1,17},{... | collective-permute-start | bytes 294920 | tf_op jit(solution)/shard_map/ppermute | solution.py:217
  29.0 4.7 %collective-permute-start.8 = (bf16[1,16,3072]{2,1,0:T(8,128)(2,1)S(1)}, bf16[1,16,3072]{2,1,0:T(8,128)(2,1)S(1)}, u32[]{:S(2)}, u32[]{:S(2)}) collective-permute-start(bf16[1,16,3072]{2,1,0:T(8,128)(2,1)S(1)} %add.37), channel_id=1, source_target_pairs={{0,4},{4,0},{8,12},{12,8},{16,20},{20,16},{24,28},{28,24},{1,5},{5... | collective-permute-start | bytes 294920 | tf_op jit(solution)/shard_map/ppermute | solution.py:217
  31.3 4.7 %collective-permute-start.3 = (bf16[1,16,3072]{2,1,0:T(8,128)(2,1)S(1)}, bf16[1,16,3072]{2,1,0:T(8,128)(2,1)S(1)}, u32[]{:S(2)}, u32[]{:S(2)}) collective-permute-start(bf16[1,16,3072]{2,1,0:T(8,128)(2,1)S(1)} %add.34), channel_id=1, source_target_pairs={{0,8},{4,12},{8,0},{12,4},{16,24},{20,28},{24,16},{28,20},{1,9},{5... | collective-permute-start | bytes 294920 | tf_op jit(solution)/shard_map/ppermute | solution.py:217
  33.7 5.7 %collective-permute-start.9 = (bf16[2,16,3072]{2,1,0:T(8,128)(2,1)S(1)}, bf16[2,16,3072]{2,1,0:T(8,128)(2,1)S(1)}, u32[]{:S(2)}, u32[]{:S(2)}) collective-permute-start(bf16[2,16,3072]{2,1,0:T(8,128)(2,1)S(1)} %pad_maximum_fusion.2), channel_id=1, source_target_pairs={{0,8},{4,12},{8,0},{12,4},{16,24},{20,28},{24,16},{28,20},{1,9},{5... | collective-permute-start | bytes 589832 | tf_op jit(solution)/shard_map/ppermute | solution.py:217
  36.0 5.7 %collective-permute-start.4 = (bf16[2,16,3072]{2,1,0:T(8,128)(2,1)S(1)}, bf16[2,16,3072]{2,1,0:T(8,128)(2,1)S(1)}, u32[]{:S(2)}, u32[]{:S(2)}) collective-permute-start(bf16[2,16,3072]{2,1,0:T(8,128)(2,1)S(1)} %pad_maximum_fusion.1), channel_id=1, source_target_pairs={{0,4},{4,0},{8,12},{12,8},{16,20},{20,16},{24,28},{28,24},{1,5},{5... | collective-permute-start | bytes 589832 | tf_op jit(solution)/shard_map/ppermute | solution.py:217
  41.9 0.7 copy-start.2
  119.0 1.9 %collective-permute-start.11 = (bf16[1960,128]{1,0:T(8,128)(2,1)S(1)}, bf16[1960,128]{1,0:T(8,128)(2,1)S(1)}, u32[]{:S(2)}, u32[]{:S(2)}) collective-permute-start(bf16[1960,128]{1,0:T(8,128)(2,1)S(1)} %get-tuple-element.12), channel_id=1, source_target_pairs={{0,1},{1,0},{2,3},{3,2},{4,5},{5,4},{6,7},{7,6},{8,9},{9,8},{10,11... | collective-permute-start | bytes 1505288 | tf_op jit(solution)/shard_map/ppermute | solution.py:308
  119.1 4.7 %collective-permute-start.10 = (bf16[1960,128]{1,0:T(8,128)(2,1)S(1)}, bf16[1960,128]{1,0:T(8,128)(2,1)S(1)}, u32[]{:S(2)}, u32[]{:S(2)}) collective-permute-start(bf16[1960,128]{1,0:T(8,128)(2,1)S(1)} %get-tuple-element.10), channel_id=1, source_target_pairs={{0,1},{1,0},{2,3},{3,2},{4,5},{5,4},{6,7},{7,6},{8,9},{9,8},{10,11... | collective-permute-start | bytes 1505288 | tf_op jit(solution)/shard_map/ppermute | solution.py:308
  122.3 13.5 %collective-permute-start.12 = (bf16[1960,128]{1,0:T(8,128)(2,1)S(1)}, bf16[1960,128]{1,0:T(8,128)(2,1)S(1)}, u32[]{:S(2)}, u32[]{:S(2)}) collective-permute-start(bf16[1960,128]{1,0:T(8,128)(2,1)S(1)} %add_convert_fusion), channel_id=1, source_target_pairs={{0,2},{1,3},{2,0},{3,1},{4,6},{5,7},{6,4},{7,5},{8,10},{9,11},{10,... | collective-permute-start | bytes 1505288 | tf_op jit(solution)/shard_map/ppermute | solution.py:308
  135.8 1.2 copy-start

commit v8 on v7

--- a/solution.py
+++ b/solution.py
@@ -14,7 +14,7 @@
 EPSILON = 1e-06
 LANES = 128
 TILES = L // LANES
-COLUMNS = 512
+COLUMNS = 256
 
 
 def lanes(rows, dtype=jnp.int32):
@@ -54,45 +54,37 @@
     lax.fori_loop(0, seg_count, one, 0)
 
 
-def builders(u_ref, seg, off, a_ref, count):
-    lane = lanes(count)
-    wide = lanes(count * (TILES + 1))
+def hold(u_ref, seg, off, held_ref):
+    count = u_ref.shape[1]
+    early = lanes(count) < off
     zero = jnp.zeros((count, LANES), jnp.bfloat16)
-    held = []
-
-    def start():
-        plain = [u_ref[seg, :, m * LANES : (m + 1) * LANES] for m in range(TILES)]
-        turned = [pltpu.roll(tile, lax.rem(off, LANES), 1) for tile in plain]
-        early = lane < off
-        moved = [
-            jnp.where(early, before, after)
-            for before, after in zip([zero] + turned, turned + [zero])
-        ]
-        for part in (moved, [zero] + moved[:-1], moved[1:] + [zero]):
-            held.append(jnp.concatenate(part, axis=0))
-
-    def one(index):
-        now, before, after = held
-        s = index - HALF
-        if s > 0:
-            z = pltpu.roll(jnp.where(wide >= LANES - s, before, now), s, 1)
-        elif s < 0:
-            z = pltpu.roll(jnp.where(wide < -s, after, now), LANES + s, 1)
-        else:
-            z = now
-        z = z.reshape(TILES + 1, count, LANES)
-        rows = slice(index * count, (index + 1) * count)
-        a_ref[0, rows, :] = jnp.where(lane < off, z[TILES], z[0])
-        a_ref[1:, rows, :] = z[1:TILES]
-
-    return [start] + [functools.partial(one, index) for index in range(LAGS)]
-
-
-def weigh(x_ref, off, row, size, gain_ref):
+    turned = [
+        pltpu.roll(u_ref[seg, :, m * LANES : (m + 1) * LANES], lax.rem(off, LANES), 1)
+        for m in range(TILES)
+    ]
+    moved = [
+        jnp.where(early, before, after)
+        for before, after in zip([zero] + turned, turned + [zero])
+    ]
+    for which, part in enumerate((moved, [zero] + moved[:-1], moved[1:] + [zero])):
+        held_ref[which] = jnp.concatenate(part, axis=0)
+
+
+def build(held_ref, index, off, a_ref, count):
+    wide = lanes(held_ref.shape[1])
+    s = index - HALF
+    z = jnp.where(wide >= LANES - s, held_ref[1], jnp.where(wide < -s, held_ref[2], held_ref[0]))
+    z = pltpu.roll(z, lax.rem(s + LANES, LANES), 1).reshape(TILES + 1, count, LANES)
+    rows = pl.ds(pl.multiple_of(index * count, count), count)
+    a_ref[0, rows, :] = jnp.where(lanes(count) < off, z[TILES], z[0])
+    a_ref[1:, rows, :] = z[1:TILES]
+
+
+def weigh(x_ref, off, start, group, size, gain_ref):
     early = lanes(size) < off
 
     def square(m):
-        value = x_ref[row : row + size, m * LANES : (m + 1) * LANES]
+        value = x_ref[pl.ds(start, size), m * LANES : (m + 1) * LANES]
         return value * value
 
     squares = [jnp.where(early, square(TILES), square(0))]
@@ -102,80 +94,68 @@
         four = (squares[m] + squares[m + 1]) + (squares[m + 2] + squares[m + 3])
         total = total + four.astype(jnp.float32)
     power = jnp.sum(jnp.transpose(total), axis=0, keepdims=True) / L
-    gain_ref[:, row : row + size] = lax.rsqrt(power + EPSILON)
-
-
-def dot(a_ref, x_ref, off, start, width, begin, end):
-    a = jnp.concatenate([a_ref[m] for m in range(begin, end)], axis=1)
-    rows = slice(start, start + width)
-    x = x_ref[rows, max(begin, 1) * LANES : end * LANES]
-    if begin == 0:
-        first = jnp.where(lanes(width) < off, x_ref[rows, L : L + LANES], x_ref[rows, :LANES])
-        x = jnp.concatenate([first, x], axis=1)
+    gain_ref[group, :, :size] = lax.rsqrt(power + EPSILON)
+
+
+def dot(a_ref, x_ref, off, start, width):
+    a = jnp.concatenate([a_ref[m] for m in range(TILES)], axis=1)
+    rows = pl.ds(start, width)
+    first = jnp.where(lanes(width) < off, x_ref[rows, L : L + LANES], x_ref[rows, :LANES])
+    x = jnp.concatenate([first, x_ref[rows, LANES:L]], axis=1)
     return lax.dot_general(a, x, (((1,), (1,)), ((), ())), preferred_element_type=jnp.float32)
 
 
 def stack_kernel(
-    blocks, scale, offsets_ref, quality_ref, u_ref, records_ref,
-    keep0, keep1, send0, send1, a0, a1, x0, x1, total, gain_ref, sems,
+    width, scale, offsets_ref, quality_ref, u_ref, x_ref,
+    keep0, keep1, send0, send1, a0, a1, held_ref, total, gain_ref,
 ):
     slots = (a0, a1)
-    x_slots = (x0, x1)
-    stride = x0.shape[1]
     n = pl.program_id(0)
     last = pl.num_programs(0) - 1
     off = offsets_ref[n]
     count = u_ref.shape[1]
     groups = total.shape[0]
-
-    def fetch(seg, slot):
-        start = pl.multiple_of(seg * stride, LANES)
-        return pltpu.make_async_copy(
-            records_ref.at[:, pl.ds(start, stride)], x_slots[slot], sems.at[slot]
-        )
+    blocks = x_ref.shape[0] // width
+    per_block = pl.cdiv(width, LANES)
+    share = pl.cdiv(LAGS, blocks)
+
+    def weigh_block(k):
+        for q in range(per_block):
+            at = q * LANES
+            start = pl.multiple_of(k * width + at, 16)
+            weigh(x_ref, off, start, k * per_block + q, min(LANES, width - at), gain_ref)
 
     @pl.when(n == 0)
     def _():
-        fetch(0, 0).start()
         total[...] = jnp.zeros_like(total)
-        for piece in builders(u_ref, 0, off, a0, count):
-            piece()
-
-    def pieces(k, x_ref):
-        start, width = blocks[k]
-        return [
-            functools.partial(
-                weigh, x_ref, off, start + at, min(LANES, width - at), gain_ref
-            )
-            for at in range(0, width, LANES)
-        ]
+        hold(u_ref, 0, off, held_ref)
+
+        def first(index, carry):
+            build(held_ref, index, off, a0, count)
+            return carry
+
+        lax.fori_loop(0, LAGS, first, 0)
+
+    later = jnp.minimum(n + 1, last)
+    later_off = offsets_ref[later]
+    hold(u_ref, later, later_off, held_ref)
+    weigh_block(0)
 
     def segment(parity):
-        x_ref = x_slots[parity]
-        fetch(n, parity).wait()
-
-        @pl.when(n < last)
-        def _():
-            fetch(n + 1, 1 - parity).start()
-
-        later = jnp.minimum(n + 1, last)
-        built = builders(u_ref, later, offsets_ref[later], slots[1 - parity], count)
-        for piece in pieces(0, x_ref):
-            piece()
-        for k, (start, width) in enumerate(blocks):
-            cuts = (0, TILES) if width == COLUMNS else (0, TILES // 2, TILES)
-            terms = [
-                dot(slots[parity], x_ref, off, start, width, begin, end)
-                for begin, end in zip(cuts, cuts[1:])
-            ]
-            share = pl.cdiv(len(built), len(blocks) - k)
-            for piece in (pieces(k + 1, x_ref) if k + 1 < len(blocks) else []) + built[:share]:
-                piece()
-            built = built[share:]
-            term = sum(terms[1:], terms[0]) * gain_ref[:, start : start + width]
-            for at in range(0, width, LANES):
-                size = min(LANES, width - at)
-                total[(start + at) // LANES, :, :size] += term[:, at : at + size]
+        def block(k, carry):
+            term = dot(slots[parity], x_ref, off, pl.multiple_of(k * width, 16), width)
+            if blocks > 1:
+                weigh_block(jnp.minimum(k + 1, blocks - 1))
+            for i in range(share):
+                index = jnp.minimum(k * share + i, LAGS - 1)
+                build(held_ref, index, later_off, slots[1 - parity], count)
+            for q in range(per_block):
+                at, size = q * LANES, min(LANES, width - q * LANES)
+                group = k * per_block + q
+                total[group, :, :size] += term[:, at : at + size] * gain_ref[group, :, :size]
+            return carry
+
+        lax.fori_loop(0, blocks, block, 0)
 
     for parity in (0, 1):
         pl.when(n % 2 == parity)(functools.partial(segment, parity))
@@ -275,25 +255,23 @@
         groups = pl.cdiv(channels, LANES)
         even = groups + groups % 2
         rows = LAGS * count
-        head = channels % COLUMNS or COLUMNS
-        blocks = [(0, head)] + [(at, COLUMNS) for at in range(head, channels, COLUMNS)]
+        width = COLUMNS if channels % COLUMNS == 0 else channels
         usable = jnp.pad(quality.astype(jnp.float32), (0, even * LANES - channels))
         shape = (even // 2 * LAGS * 8, LANES)
         kept = jax.ShapeDtypeStruct(shape, jnp.float32)
         sent = jax.ShapeDtypeStruct(shape, jnp.bfloat16)
         scale = 1.0 / math.sqrt(seg_count * win * L)
         keep0, keep1, send0, send1 = pl.pallas_call(
-            functools.partial(stack_kernel, blocks, scale),
+            functools.partial(stack_kernel, width, scale),
             grid=(seg_count,),
             out_shape=(kept, kept, sent, sent),
-            in_specs=[smem, vmem, vmem, pl.BlockSpec(memory_space=pl.ANY)],
+            in_specs=[smem, vmem, vmem, pl.BlockSpec((channels, stride), lambda g: (0, g))],
             out_specs=(vmem,) * 4,
             scratch_shapes=[pltpu.VMEM((TILES, rows, LANES), jnp.bfloat16)] * 2
-            + [pltpu.VMEM((channels, stride), jnp.bfloat16)] * 2
             + [
+                pltpu.VMEM((3, (TILES + 1) * count, LANES), jnp.bfloat16),
                 pltpu.VMEM((even, rows, LANES), jnp.float32),
-                pltpu.VMEM((1, even * LANES), jnp.float32),
-                pltpu.SemaphoreType.DMA((2,)),
+                pltpu.VMEM((even, 1, LANES), jnp.float32),
             ],
             compiler_params=pltpu.CompilerParams(vmem_limit_bytes=52 * 2**20),
             cost_estimate=pl.CostEstimate(

time: 139 us -> 146 us (1.050)
  Pallas kernels: 79.8 us -> 87.2 us
    pallas_call x1, Pallas kernels: 76.4 us -> 83.8 us  [body(): pl.pallas_call(functools.partial(stack_kernel, width, scale), grid=(seg_c...]
  transfers between devices with their start and end apart: 13 -> 13, of which waited for: 11 -> 11; matrix products, arithmetic and copies ran while one was open for 2% -> 1% of each run, Pallas kernels for 0% -> 0%
where the time goes in v8:
time: 146 us
  Pallas kernels  87.2 us (60%)
  waiting for transfers between devices  31.3 us (21%)
  starting transfers between devices  17.9 us (12%)
  local copies, waits for them, and re-layouts  5.91 us (4%)
  other arithmetic  3.34 us (2%)
    pallas_call x1, Pallas kernels, body(): pl.pallas_call(functools.partial(stack_kernel, width, scale), grid=(seg_c...  83.8 us
    ppermute x10, waiting for transfers between devices, swap(): return lax.ppermute(v, axis, [(d, d ^ bit) for d in range(size)])  17.9 us
    ppermute x10, starting transfers between devices, swap(): return lax.ppermute(v, axis, [(d, d ^ bit) for d in range(size)])  15.9 us
    ppermute x3, waiting for transfers between devices, swap(): return lax.ppermute(v, 'win', [(d, d ^ bit) for d in range(win)])  13.4 us
    gather x1, local copies, waits for them, and re-layouts, body(): rows = records.at[lax.rem(flat, channels)].get(mode='promise_in_bounds')  3.23 us
  transfers between devices with their start and end apart: 13, of which 11 were waited for; matrix products, arithmetic and copies ran while one was open for 1% of the time, Pallas kernels for 0%

profile of v8, /device:TPU:0, one launch (start us, length us, event | category | flops | bytes accessed | tf_op | source)
XLA Modules:
  0.0 145.8 jit_solution(7243867920338024231)
XLA Ops:
  1.0 3.2 %gather_fusion = bf16[16,25600]{1,0:T(8,128)(2,1)S(1)} fusion(bf16[1280,25600]{1,0:T(8,128)(2,1)} %x_ref.1, s32[1024]{0:T(1024)S(1)} %pad_clamp_fusion), kind=kCustom, calls=%fused_computation | custom fusion | bytes 1638464 | tf_op jit(solution)/shard_map/gather | solution.py:241
  4.9 1.9 %sources.1 = bf16[8,16,3072]{2,1,0:T(8,128)(2,1)S(1)} custom-call(s32[8]{0:T(128)S(1)} %copy-done.1, s32[16]{0:T(128)S(1)} %reshape.34.flat_ref, s32[1]{0:T(128)} %bitcast.1.me_ref, bf16[16,25600]{1,0:T(8,128)(2,1)S(1)} %gather_fusion), custom_call_target="tpu_custom_call" | custom-call | tf_op jit(solution)/shard_map/sources/pallas_call | solution.py:244
  6.9 3.0 %collective-permute-start = (bf16[2,16,3072]{2,1,0:T(8,128)(2,1)S(1)}, bf16[2,16,3072]{2,1,0:T(8,128)(2,1)S(1)}, u32[]{:S(2)}, u32[]{:S(2)}) collective-permute-start(bf16[2,16,3072]{2,1,0:T(8,128)(2,1)S(1)} %get-tuple-element.15), channel_id=1, source_target_pairs={{0,4},{4,0},{8,12},{12,8},{16,20},{20,16},{24,28},{28,24},{1,5},{5... | collective-permute-start | bytes 589832 | tf_op jit(solution)/shard_map/ppermute | solution.py:197
  9.9 1.6 %collective-permute-start.5 = (bf16[2,16,3072]{2,1,0:T(8,128)(2,1)S(1)}, bf16[2,16,3072]{2,1,0:T(8,128)(2,1)S(1)}, u32[]{:S(2)}, u32[]{:S(2)}) collective-permute-start(bf16[2,16,3072]{2,1,0:T(8,128)(2,1)S(1)} %get-tuple-element.16), channel_id=1, source_target_pairs={{0,8},{4,12},{8,0},{12,4},{16,24},{20,28},{24,16},{28,20},{1,9},{5... | collective-permute-start | bytes 589832 | tf_op jit(solution)/shard_map/ppermute | solution.py:197
  11.5 3.3 %collective-permute-done = bf16[2,16,3072]{2,1,0:T(8,128)(2,1)S(1)} collective-permute-done((bf16[2,16,3072]{2,1,0:T(8,128)(2,1)S(1)}, bf16[2,16,3072]{2,1,0:T(8,128)(2,1)S(1)}, u32[]{:S(2)}, u32[]{:S(2)}) %collective-permute-start) | collective-permute-done | bytes 196640 | tf_op jit(solution)/shard_map/ppermute | solution.py:197
  14.8 1.5 %collective-permute-done.5 = bf16[2,16,3072]{2,1,0:T(8,128)(2,1)S(1)} collective-permute-done((bf16[2,16,3072]{2,1,0:T(8,128)(2,1)S(1)}, bf16[2,16,3072]{2,1,0:T(8,128)(2,1)S(1)}, u32[]{:S(2)}, u32[]{:S(2)}) %collective-permute-start.5) | collective-permute-done | bytes 196640 | tf_op jit(solution)/shard_map/ppermute | solution.py:197
  16.8 1.7 %collective-permute-start.1 = (bf16[1,16,3072]{2,1,0:T(8,128)(2,1)S(1)}, bf16[1,16,3072]{2,1,0:T(8,128)(2,1)S(1)}, u32[]{:S(2)}, u32[]{:S(2)}) collective-permute-start(bf16[1,16,3072]{2,1,0:T(8,128)(2,1)S(1)} %broadcast_select_fusion.11), channel_id=1, source_target_pairs={{0,8},{4,12},{8,0},{12,4},{16,24},{20,28},{24,16},{28,20},{1,9},{5... | collective-permute-start | bytes 294920 | tf_op jit(solution)/shard_map/ppermute | solution.py:197
  18.5 2.5 %collective-permute-done.6 = bf16[1,16,3072]{2,1,0:T(8,128)(2,1)S(1)} collective-permute-done((bf16[1,16,3072]{2,1,0:T(8,128)(2,1)S(1)}, bf16[1,16,3072]{2,1,0:T(8,128)(2,1)S(1)}, u32[]{:S(2)}, u32[]{:S(2)}) %collective-permute-start.6) | collective-permute-done | bytes 98336 | tf_op jit(solution)/shard_map/ppermute | solution.py:197
  21.4 2.9 %collective-permute-start.7 = (bf16[1,16,3072]{2,1,0:T(8,128)(2,1)S(1)}, bf16[1,16,3072]{2,1,0:T(8,128)(2,1)S(1)}, u32[]{:S(2)}, u32[]{:S(2)}) collective-permute-start(bf16[1,16,3072]{2,1,0:T(8,128)(2,1)S(1)} %get-tuple-element.31), channel_id=1, source_target_pairs={{0,16},{4,20},{8,24},{12,28},{16,0},{20,4},{24,8},{28,12},{1,17},{... | collective-permute-start | bytes 294920 | tf_op jit(solution)/shard_map/ppermute | solution.py:197
  24.5 4.5 %collective-permute-done.7 = bf16[1,16,3072]{2,1,0:T(8,128)(2,1)S(1)} collective-permute-done((bf16[1,16,3072]{2,1,0:T(8,128)(2,1)S(1)}, bf16[1,16,3072]{2,1,0:T(8,128)(2,1)S(1)}, u32[]{:S(2)}, u32[]{:S(2)}) %collective-permute-start.7) | collective-permute-done | bytes 98336 | tf_op jit(solution)/shard_map/ppermute | solution.py:197
  29.0 1.6 %collective-permute-start.8 = (bf16[1,16,3072]{2,1,0:T(8,128)(2,1)S(1)}, bf16[1,16,3072]{2,1,0:T(8,128)(2,1)S(1)}, u32[]{:S(2)}, u32[]{:S(2)}) collective-permute-start(bf16[1,16,3072]{2,1,0:T(8,128)(2,1)S(1)} %add.37), channel_id=1, source_target_pairs={{0,4},{4,0},{8,12},{12,8},{16,20},{20,16},{24,28},{28,24},{1,5},{5... | collective-permute-start | bytes 294920 | tf_op jit(solution)/shard_map/ppermute | solution.py:197
  31.3 1.5 %collective-permute-start.3 = (bf16[1,16,3072]{2,1,0:T(8,128)(2,1)S(1)}, bf16[1,16,3072]{2,1,0:T(8,128)(2,1)S(1)}, u32[]{:S(2)}, u32[]{:S(2)}) collective-permute-start(bf16[1,16,3072]{2,1,0:T(8,128)(2,1)S(1)} %add.34), channel_id=1, source_target_pairs={{0,8},{4,12},{8,0},{12,4},{16,24},{20,28},{24,16},{28,20},{1,9},{5... | collective-permute-start | bytes 294920 | tf_op jit(solution)/shard_map/ppermute | solution.py:197
  32.8 0.9 collective-permute-done.8
  33.7 1.6 %collective-permute-start.9 = (bf16[2,16,3072]{2,1,0:T(8,128)(2,1)S(1)}, bf16[2,16,3072]{2,1,0:T(8,128)(2,1)S(1)}, u32[]{:S(2)}, u32[]{:S(2)}) collective-permute-start(bf16[2,16,3072]{2,1,0:T(8,128)(2,1)S(1)} %pad_maximum_fusion.2), channel_id=1, source_target_pairs={{0,8},{4,12},{8,0},{12,4},{16,24},{20,28},{24,16},{28,20},{1,9},{5... | collective-permute-start | bytes 589832 | tf_op jit(solution)/shard_map/ppermute | solution.py:197
  36.0 1.5 %collective-permute-start.4 = (bf16[2,16,3072]{2,1,0:T(8,128)(2,1)S(1)}, bf16[2,16,3072]{2,1,0:T(8,128)(2,1)S(1)}, u32[]{:S(2)}, u32[]{:S(2)}) collective-permute-start(bf16[2,16,3072]{2,1,0:T(8,128)(2,1)S(1)} %pad_maximum_fusion.1), channel_id=1, source_target_pairs={{0,4},{4,0},{8,12},{12,8},{16,20},{20,16},{24,28},{28,24},{1,5},{5... | collective-permute-start | bytes 589832 | tf_op jit(solution)/shard_map/ppermute | solution.py:197
  37.5 1.9 %collective-permute-done.9 = bf16[2,16,3072]{2,1,0:T(8,128)(2,1)S(1)} collective-permute-done((bf16[2,16,3072]{2,1,0:T(8,128)(2,1)S(1)}, bf16[2,16,3072]{2,1,0:T(8,128)(2,1)S(1)}, u32[]{:S(2)}, u32[]{:S(2)}) %collective-permute-start.9) | collective-permute-done | bytes 196640 | tf_op jit(solution)/shard_map/ppermute | solution.py:197
  39.5 2.3 %collective-permute-done.4 = bf16[2,16,3072]{2,1,0:T(8,128)(2,1)S(1)} collective-permute-done((bf16[2,16,3072]{2,1,0:T(8,128)(2,1)S(1)}, bf16[2,16,3072]{2,1,0:T(8,128)(2,1)S(1)}, u32[]{:S(2)}, u32[]{:S(2)}) %collective-permute-start.4) | collective-permute-done | bytes 196640 | tf_op jit(solution)/shard_map/ppermute | solution.py:197
  42.6 83.8 %stacks.1 = (f32[1960,128]{1,0:T(8,128)}, f32[1960,128]{1,0:T(8,128)}, bf16[1960,128]{1,0:T(8,128)(2,1)S(1)}, bf16[1960,128]{1,0:T(8,128)(2,1)S(1)}) custom-call(s32[8]{0:T(128)S(1)} %copy-done.2, f32[10,128]{1,0:T(8,128)S(1)} %convert_bitcast_fusion.quality_ref, bf16[8,16,3072]{2,1,0:T(8,128)(2,1)S(1)} %pad_maximum_fusion.u_ref, bf16[1280,25600]{1,0:T(8,128)(2,1)} %x_ref.1), custom_call_target="tpu_custom_call" | custom-call | flops 49325015040 | bytes 65536000 | tf_op jit(solution)/shard_map/stacks/pallas_call | solution.py:264
  126.9 1.4 collective-permute-done.11
  128.3 1.3 add_convert_fusion
  129.6 1.5 %collective-permute-start.12 = (bf16[1960,128]{1,0:T(8,128)(2,1)S(1)}, bf16[1960,128]{1,0:T(8,128)(2,1)S(1)}, u32[]{:S(2)}, u32[]{:S(2)}) collective-permute-start(bf16[1960,128]{1,0:T(8,128)(2,1)S(1)} %add_convert_fusion), channel_id=1, source_target_pairs={{0,2},{1,3},{2,0},{3,1},{4,6},{5,7},{6,4},{7,5},{8,10},{9,11},{10,... | collective-permute-start | bytes 1505288 | tf_op jit(solution)/shard_map/ppermute | solution.py:286
  131.1 12.1 %collective-permute-done.12.chip_ref = bf16[1960,128]{1,0:T(8,128)(2,1)S(1)} collective-permute-done((bf16[1960,128]{1,0:T(8,128)(2,1)S(1)}, bf16[1960,128]{1,0:T(8,128)(2,1)S(1)}, u32[]{:S(2)}, u32[]{:S(2)}) %collective-permute-start.12) | collective-permute-done | bytes 501792 | tf_op jit(solution)/shard_map/ppermute | solution.py:286
  143.2 1.2 copy-done
  144.4 1.4 finish.1
  (34 shorter events, 5.6 us)
Async XLA Ops:
  4.3 0.7 copy-start.1
  6.9 7.9 %collective-permute-start = (bf16[2,16,3072]{2,1,0:T(8,128)(2,1)S(1)}, bf16[2,16,3072]{2,1,0:T(8,128)(2,1)S(1)}, u32[]{:S(2)}, u32[]{:S(2)}) collective-permute-start(bf16[2,16,3072]{2,1,0:T(8,128)(2,1)S(1)} %get-tuple-element.15), channel_id=1, source_target_pairs={{0,4},{4,0},{8,12},{12,8},{16,20},{20,16},{24,28},{28,24},{1,5},{5... | collective-permute-start | bytes 589832 | tf_op jit(solution)/shard_map/ppermute | solution.py:197
  9.9 6.4 %collective-permute-start.5 = (bf16[2,16,3072]{2,1,0:T(8,128)(2,1)S(1)}, bf16[2,16,3072]{2,1,0:T(8,128)(2,1)S(1)}, u32[]{:S(2)}, u32[]{:S(2)}) collective-permute-start(bf16[2,16,3072]{2,1,0:T(8,128)(2,1)S(1)} %get-tuple-element.16), channel_id=1, source_target_pairs={{0,8},{4,12},{8,0},{12,4},{16,24},{20,28},{24,16},{28,20},{1,9},{5... | collective-permute-start | bytes 589832 | tf_op jit(solution)/shard_map/ppermute | solution.py:197
  16.3 4.7 %collective-permute-start.6 = (bf16[1,16,3072]{2,1,0:T(8,128)(2,1)S(1)}, bf16[1,16,3072]{2,1,0:T(8,128)(2,1)S(1)}, u32[]{:S(2)}, u32[]{:S(2)}) collective-permute-start(bf16[1,16,3072]{2,1,0:T(8,128)(2,1)S(1)} %broadcast_select_fusion.8), channel_id=1, source_target_pairs={{0,4},{4,0},{8,12},{12,8},{16,20},{20,16},{24,28},{28,24},{1,5},{5... | collective-permute-start | bytes 294920 | tf_op jit(solution)/shard_map/ppermute | solution.py:197
  16.8 4.6 %collective-permute-start.1 = (bf16[1,16,3072]{2,1,0:T(8,128)(2,1)S(1)}, bf16[1,16,3072]{2,1,0:T(8,128)(2,1)S(1)}, u32[]{:S(2)}, u32[]{:S(2)}) collective-permute-start(bf16[1,16,3072]{2,1,0:T(8,128)(2,1)S(1)} %broadcast_select_fusion.11), channel_id=1, source_target_pairs={{0,8},{4,12},{8,0},{12,4},{16,24},{20,28},{24,16},{28,20},{1,9},{5... | collective-permute-start | bytes 294920 | tf_op jit(solution)/shard_map/ppermute | solution.py:197
  21.4 7.5 %collective-permute-start.7 = (bf16[1,16,3072]{2,1,0:T(8,128)(2,1)S(1)}, bf16[1,16,3072]{2,1,0:T(8,128)(2,1)S(1)}, u32[]{:S(2)}, u32[]{:S(2)}) collective-permute-start(bf16[1,16,3072]{2,1,0:T(8,128)(2,1)S(1)} %get-tuple-element.31), channel_id=1, source_target_pairs={{0,16},{4,20},{8,24},{12,28},{16,0},{20,4},{24,8},{28,12},{1,17},{... | collective-permute-start | bytes 294920 | tf_op jit(solution)/shard_map/ppermute | solution.py:197
  24.4 6.9 %collective-permute-start.2 = (bf16[1,16,3072]{2,1,0:T(8,128)(2,1)S(1)}, bf16[1,16,3072]{2,1,0:T(8,128)(2,1)S(1)}, u32[]{:S(2)}, u32[]{:S(2)}) collective-permute-start(bf16[1,16,3072]{2,1,0:T(8,128)(2,1)S(1)} %get-tuple-element.32), channel_id=1, source_target_pairs={{0,16},{4,20},{8,24},{12,28},{16,0},{20,4},{24,8},{28,12},{1,17},{... | collective-permute-start | bytes 294920 | tf_op jit(solution)/shard_map/ppermute | solution.py:197
  29.0 4.7 %collective-permute-start.8 = (bf16[1,16,3072]{2,1,0:T(8,128)(2,1)S(1)}, bf16[1,16,3072]{2,1,0:T(8,128)(2,1)S(1)}, u32[]{:S(2)}, u32[]{:S(2)}) collective-permute-start(bf16[1,16,3072]{2,1,0:T(8,128)(2,1)S(1)} %add.37), channel_id=1, source_target_pairs={{0,4},{4,0},{8,12},{12,8},{16,20},{20,16},{24,28},{28,24},{1,5},{5... | collective-permute-start | bytes 294920 | tf_op jit(solution)/shard_map/ppermute | solution.py:197
  31.3 4.7 %collective-permute-start.3 = (bf16[1,16,3072]{2,1,0:T(8,128)(2,1)S(1)}, bf16[1,16,3072]{2,1,0:T(8,128)(2,1)S(1)}, u32[]{:S(2)}, u32[]{:S(2)}) collective-permute-start(bf16[1,16,3072]{2,1,0:T(8,128)(2,1)S(1)} %add.34), channel_id=1, source_target_pairs={{0,8},{4,12},{8,0},{12,4},{16,24},{20,28},{24,16},{28,20},{1,9},{5... | collective-permute-start | bytes 294920 | tf_op jit(solution)/shard_map/ppermute | solution.py:197
  33.7 5.7 %collective-permute-start.9 = (bf16[2,16,3072]{2,1,0:T(8,128)(2,1)S(1)}, bf16[2,16,3072]{2,1,0:T(8,128)(2,1)S(1)}, u32[]{:S(2)}, u32[]{:S(2)}) collective-permute-start(bf16[2,16,3072]{2,1,0:T(8,128)(2,1)S(1)} %pad_maximum_fusion.2), channel_id=1, source_target_pairs={{0,8},{4,12},{8,0},{12,4},{16,24},{20,28},{24,16},{28,20},{1,9},{5... | collective-permute-start | bytes 589832 | tf_op jit(solution)/shard_map/ppermute | solution.py:197
  36.0 5.7 %collective-permute-start.4 = (bf16[2,16,3072]{2,1,0:T(8,128)(2,1)S(1)}, bf16[2,16,3072]{2,1,0:T(8,128)(2,1)S(1)}, u32[]{:S(2)}, u32[]{:S(2)}) collective-permute-start(bf16[2,16,3072]{2,1,0:T(8,128)(2,1)S(1)} %pad_maximum_fusion.1), channel_id=1, source_target_pairs={{0,4},{4,0},{8,12},{12,8},{16,20},{20,16},{24,28},{28,24},{1,5},{5... | collective-permute-start | bytes 589832 | tf_op jit(solution)/shard_map/ppermute | solution.py:197
  41.9 0.7 copy-start.2
  126.4 1.9 %collective-permute-start.11 = (bf16[1960,128]{1,0:T(8,128)(2,1)S(1)}, bf16[1960,128]{1,0:T(8,128)(2,1)S(1)}, u32[]{:S(2)}, u32[]{:S(2)}) collective-permute-start(bf16[1960,128]{1,0:T(8,128)(2,1)S(1)} %get-tuple-element.12), channel_id=1, source_target_pairs={{0,1},{1,0},{2,3},{3,2},{4,5},{5,4},{6,7},{7,6},{8,9},{9,8},{10,11... | collective-permute-start | bytes 1505288 | tf_op jit(solution)/shard_map/ppermute | solution.py:286
  126.4 4.7 %collective-permute-start.10 = (bf16[1960,128]{1,0:T(8,128)(2,1)S(1)}, bf16[1960,128]{1,0:T(8,128)(2,1)S(1)}, u32[]{:S(2)}, u32[]{:S(2)}) collective-permute-start(bf16[1960,128]{1,0:T(8,128)(2,1)S(1)} %get-tuple-element.10), channel_id=1, source_target_pairs={{0,1},{1,0},{2,3},{3,2},{4,5},{5,4},{6,7},{7,6},{8,9},{9,8},{10,11... | collective-permute-start | bytes 1505288 | tf_op jit(solution)/shard_map/ppermute | solution.py:286
  129.6 13.5 %collective-permute-start.12 = (bf16[1960,128]{1,0:T(8,128)(2,1)S(1)}, bf16[1960,128]{1,0:T(8,128)(2,1)S(1)}, u32[]{:S(2)}, u32[]{:S(2)}) collective-permute-start(bf16[1960,128]{1,0:T(8,128)(2,1)S(1)} %add_convert_fusion), channel_id=1, source_target_pairs={{0,2},{1,3},{2,0},{3,1},{4,6},{5,7},{6,4},{7,5},{8,10},{9,11},{10,... | collective-permute-start | bytes 1505288 | tf_op jit(solution)/shard_map/ppermute | solution.py:286
  143.2 1.2 copy-start

commit v9 on v7

--- a/solution.py
+++ b/solution.py
@@ -116,27 +116,18 @@
 
 
 def stack_kernel(
-    blocks, scale, offsets_ref, quality_ref, u_ref, records_ref,
-    keep0, keep1, send0, send1, a0, a1, x0, x1, total, gain_ref, sems,
+    blocks, scale, offsets_ref, quality_ref, u_ref, x_ref,
+    keep0, keep1, send0, send1, a0, a1, total, gain_ref,
 ):
     slots = (a0, a1)
-    x_slots = (x0, x1)
-    stride = x0.shape[1]
     n = pl.program_id(0)
     last = pl.num_programs(0) - 1
     off = offsets_ref[n]
     count = u_ref.shape[1]
     groups = total.shape[0]
 
-    def fetch(seg, slot):
-        start = pl.multiple_of(seg * stride, LANES)
-        return pltpu.make_async_copy(
-            records_ref.at[:, pl.ds(start, stride)], x_slots[slot], sems.at[slot]
-        )
-
     @pl.when(n == 0)
     def _():
-        fetch(0, 0).start()
         total[...] = jnp.zeros_like(total)
         for piece in builders(u_ref, 0, off, a0, count):
             piece()
@@ -151,13 +142,6 @@
         ]
 
     def segment(parity):
-        x_ref = x_slots[parity]
-        fetch(n, parity).wait()
-
-        @pl.when(n < last)
-        def _():
-            fetch(n + 1, 1 - parity).start()
-
         later = jnp.minimum(n + 1, last)
         built = builders(u_ref, later, offsets_ref[later], slots[1 - parity], count)
         for piece in pieces(0, x_ref):
@@ -197,10 +181,8 @@
                     out[rows, :] = value.reshape(LAGS * 8, LANES).astype(out.dtype)
 
 
-def finish_kernel(src_count, keep_ref, core_ref, chip_ref, out_ref, total):
-    total[...] = (
-        keep_ref[...] + core_ref[...].astype(jnp.float32) + chip_ref[...].astype(jnp.float32)
-    )
+def finish_kernel(src_count, near_ref, chip_ref, out_ref, total):
+    total[...] = near_ref[...] + chip_ref[...].astype(jnp.float32)
     groups = out_ref.shape[0] // (src_count * LAGS)
     for group in range(groups):
         for i in range(src_count):
@@ -275,8 +257,7 @@
         groups = pl.cdiv(channels, LANES)
         even = groups + groups % 2
         rows = LAGS * count
-        head = channels % COLUMNS or COLUMNS
-        blocks = [(0, head)] + [(at, COLUMNS) for at in range(head, channels, COLUMNS)]
+        blocks = [(at, min(COLUMNS, channels - at)) for at in range(0, channels, COLUMNS)]
         usable = jnp.pad(quality.astype(jnp.float32), (0, even * LANES - channels))
         shape = (even // 2 * LAGS * 8, LANES)
         kept = jax.ShapeDtypeStruct(shape, jnp.float32)
@@ -286,14 +267,12 @@
             functools.partial(stack_kernel, blocks, scale),
             grid=(seg_count,),
             out_shape=(kept, kept, sent, sent),
-            in_specs=[smem, vmem, vmem, pl.BlockSpec(memory_space=pl.ANY)],
+            in_specs=[smem, vmem, vmem, pl.BlockSpec((channels, stride), lambda g: (0, g))],
             out_specs=(vmem,) * 4,
             scratch_shapes=[pltpu.VMEM((TILES, rows, LANES), jnp.bfloat16)] * 2
-            + [pltpu.VMEM((channels, stride), jnp.bfloat16)] * 2
             + [
                 pltpu.VMEM((even, rows, LANES), jnp.float32),
                 pltpu.VMEM((1, even * LANES), jnp.float32),
-                pltpu.SemaphoreType.DMA((2,)),
             ],
             compiler_params=pltpu.CompilerParams(vmem_limit_bytes=52 * 2**20),
             cost_estimate=pl.CostEstimate(
@@ -309,16 +288,16 @@
 
         far = keep1 + swap(send1, 1).astype(jnp.float32)
         chip = swap(far.astype(jnp.bfloat16), 2)
-        core = swap(send0, 1)
+        near = keep0 + swap(send0, 1).astype(jnp.float32)
         total = pl.pallas_call(
             functools.partial(finish_kernel, src_count),
             out_shape=jax.ShapeDtypeStruct((src_count * LAGS * groups, LANES), jnp.float32),
-            in_specs=[vmem] * 3,
+            in_specs=[vmem] * 2,
             out_specs=vmem,
             scratch_shapes=[pltpu.VMEM(shape, jnp.float32)],
             compiler_params=pltpu.CompilerParams(vmem_limit_bytes=16 * 2**20),
             name="finish",
-        )(keep0, core, chip)
+        )(near, chip)
         return total.reshape(1, src_count * LAGS, groups * LANES)[..., :channels]
 
     return jax.shard_map(

time: 139 us -> 127 us (0.914)
  Pallas kernels: 79.8 us -> 67.4 us
  starting transfers between devices: 18 us -> 13.7 us
  waiting for transfers between devices: 31.3 us -> 35.6 us
    pallas_call x1, Pallas kernels: 76.4 us -> 64.3 us  [body(): pl.pallas_call(functools.partial(stack_kernel, blocks, scale), grid=(seg_...]
    ppermute x10, waiting for transfers between devices: 17.9 us -> 23.6 us  [swap(): return lax.ppermute(v, axis, [(d, d ^ bit) for d in range(size)])]
    ppermute x10, starting transfers between devices: 15.9 us -> 11.6 us  [swap(): return lax.ppermute(v, axis, [(d, d ^ bit) for d in range(size)])]
  transfers between devices with their start and end apart: 13 -> 13, of which waited for: 11 -> 12; matrix products, arithmetic and copies ran while one was open for 2% -> 3% of each run, Pallas kernels for 0% -> 0%
where the time goes in v9:
time: 127 us; the launch traced here: 126 us
  Pallas kernels  67.4 us (53%)
  waiting for transfers between devices  35.6 us (28%)
  starting transfers between devices  13.7 us (11%)
  local copies, waits for them, and re-layouts  4.7 us (4%)
  other arithmetic  4.67 us (4%)
    pallas_call x1, Pallas kernels, body(): pl.pallas_call(functools.partial(stack_kernel, blocks, scale), grid=(seg_...  64.3 us
    ppermute x10, waiting for transfers between devices, swap(): return lax.ppermute(v, axis, [(d, d ^ bit) for d in range(size)])  23.6 us
    ppermute x3, waiting for transfers between devices, swap(): return lax.ppermute(v, 'win', [(d, d ^ bit) for d in range(win)])  12 us
    ppermute x10, starting transfers between devices, swap(): return lax.ppermute(v, axis, [(d, d ^ bit) for d in range(size)])  11.6 us
    gather x1, local copies, waits for them, and re-layouts, body(): rows = records.at[lax.rem(flat, channels)].get(mode='promise_in_bounds')  3.23 us
  transfers between devices with their start and end apart: 13, of which 12 were waited for; matrix products, arithmetic and copies ran while one was open for 3% of the time, Pallas kernels for 0%

profile of v9, /device:TPU:0, one launch (start us, length us, event | category | flops | bytes accessed | tf_op | source)
XLA Modules:
  0.0 126.2 jit_solution(4266789880196430715)
XLA Ops:
  0.0 0.8 broadcast_select_fusion.19
  1.0 3.2 %gather_fusion = bf16[16,25600]{1,0:T(8,128)(2,1)S(1)} fusion(bf16[1280,25600]{1,0:T(8,128)(2,1)} %x_ref.1, s32[1024]{0:T(1024)S(1)} %pad_clamp_fusion), kind=kCustom, calls=%fused_computation | custom fusion | bytes 1638464 | tf_op jit(solution)/shard_map/gather | solution.py:243
  4.9 1.9 %sources.1 = bf16[8,16,3072]{2,1,0:T(8,128)(2,1)S(1)} custom-call(s32[8]{0:T(128)S(1)} %copy-done, s32[16]{0:T(128)S(1)} %reshape.34.flat_ref, s32[1]{0:T(128)} %bitcast.1.me_ref, bf16[16,25600]{1,0:T(8,128)(2,1)S(1)} %gather_fusion), custom_call_target="tpu_custom_call" | custom-call | tf_op jit(solution)/shard_map/sources/pallas_call | solution.py:246
  6.9 3.0 %collective-permute-start = (bf16[2,16,3072]{2,1,0:T(8,128)(2,1)S(1)}, bf16[2,16,3072]{2,1,0:T(8,128)(2,1)S(1)}, u32[]{:S(2)}, u32[]{:S(2)}) collective-permute-start(bf16[2,16,3072]{2,1,0:T(8,128)(2,1)S(1)} %get-tuple-element.15), channel_id=1, source_target_pairs={{0,4},{4,0},{8,12},{12,8},{16,20},{20,16},{24,28},{28,24},{1,5},{5... | collective-permute-start | bytes 589832 | tf_op jit(solution)/shard_map/ppermute | solution.py:199
  9.9 1.6 %collective-permute-start.5 = (bf16[2,16,3072]{2,1,0:T(8,128)(2,1)S(1)}, bf16[2,16,3072]{2,1,0:T(8,128)(2,1)S(1)}, u32[]{:S(2)}, u32[]{:S(2)}) collective-permute-start(bf16[2,16,3072]{2,1,0:T(8,128)(2,1)S(1)} %get-tuple-element.16), channel_id=1, source_target_pairs={{0,8},{4,12},{8,0},{12,4},{16,24},{20,28},{24,16},{28,20},{1,9},{5... | collective-permute-start | bytes 589832 | tf_op jit(solution)/shard_map/ppermute | solution.py:199
  11.5 3.3 %collective-permute-done = bf16[2,16,3072]{2,1,0:T(8,128)(2,1)S(1)} collective-permute-done((bf16[2,16,3072]{2,1,0:T(8,128)(2,1)S(1)}, bf16[2,16,3072]{2,1,0:T(8,128)(2,1)S(1)}, u32[]{:S(2)}, u32[]{:S(2)}) %collective-permute-start) | collective-permute-done | bytes 196640 | tf_op jit(solution)/shard_map/ppermute | solution.py:199
  14.8 1.5 %collective-permute-done.5 = bf16[2,16,3072]{2,1,0:T(8,128)(2,1)S(1)} collective-permute-done((bf16[2,16,3072]{2,1,0:T(8,128)(2,1)S(1)}, bf16[2,16,3072]{2,1,0:T(8,128)(2,1)S(1)}, u32[]{:S(2)}, u32[]{:S(2)}) %collective-permute-start.5) | collective-permute-done | bytes 196640 | tf_op jit(solution)/shard_map/ppermute | solution.py:199
  16.3 1.6 %collective-permute-start.1 = (bf16[1,16,3072]{2,1,0:T(8,128)(2,1)S(1)}, bf16[1,16,3072]{2,1,0:T(8,128)(2,1)S(1)}, u32[]{:S(2)}, u32[]{:S(2)}) collective-permute-start(bf16[1,16,3072]{2,1,0:T(8,128)(2,1)S(1)} %broadcast_select_fusion.11), channel_id=1, source_target_pairs={{0,8},{4,12},{8,0},{12,4},{16,24},{20,28},{24,16},{28,20},{1,9},{5... | collective-permute-start | bytes 294920 | tf_op jit(solution)/shard_map/ppermute | solution.py:199
  18.6 2.4 %collective-permute-done.1 = bf16[1,16,3072]{2,1,0:T(8,128)(2,1)S(1)} collective-permute-done((bf16[1,16,3072]{2,1,0:T(8,128)(2,1)S(1)}, bf16[1,16,3072]{2,1,0:T(8,128)(2,1)S(1)}, u32[]{:S(2)}, u32[]{:S(2)}) %collective-permute-start.1) | collective-permute-done | bytes 98336 | tf_op jit(solution)/shard_map/ppermute | solution.py:199
  21.0 1.7 %collective-permute-done.6 = bf16[1,16,3072]{2,1,0:T(8,128)(2,1)S(1)} collective-permute-done((bf16[1,16,3072]{2,1,0:T(8,128)(2,1)S(1)}, bf16[1,16,3072]{2,1,0:T(8,128)(2,1)S(1)}, u32[]{:S(2)}, u32[]{:S(2)}) %collective-permute-start.6) | collective-permute-done | bytes 98336 | tf_op jit(solution)/shard_map/ppermute | solution.py:199
  22.7 2.6 %collective-permute-start.2 = (bf16[1,16,3072]{2,1,0:T(8,128)(2,1)S(1)}, bf16[1,16,3072]{2,1,0:T(8,128)(2,1)S(1)}, u32[]{:S(2)}, u32[]{:S(2)}) collective-permute-start(bf16[1,16,3072]{2,1,0:T(8,128)(2,1)S(1)} %get-tuple-element.32), channel_id=1, source_target_pairs={{0,16},{4,20},{8,24},{12,28},{16,0},{20,4},{24,8},{28,12},{1,17},{... | collective-permute-start | bytes 294920 | tf_op jit(solution)/shard_map/ppermute | solution.py:199
  25.7 4.5 %collective-permute-done.2 = bf16[1,16,3072]{2,1,0:T(8,128)(2,1)S(1)} collective-permute-done((bf16[1,16,3072]{2,1,0:T(8,128)(2,1)S(1)}, bf16[1,16,3072]{2,1,0:T(8,128)(2,1)S(1)}, u32[]{:S(2)}, u32[]{:S(2)}) %collective-permute-start.2) | collective-permute-done | bytes 98336 | tf_op jit(solution)/shard_map/ppermute | solution.py:199
  31.0 1.1 collective-permute-done.7
  32.7 2.2 %collective-permute-done.3 = bf16[1,16,3072]{2,1,0:T(8,128)(2,1)S(1)} collective-permute-done((bf16[1,16,3072]{2,1,0:T(8,128)(2,1)S(1)}, bf16[1,16,3072]{2,1,0:T(8,128)(2,1)S(1)}, u32[]{:S(2)}, u32[]{:S(2)}) %collective-permute-start.3) | collective-permute-done | bytes 98336 | tf_op jit(solution)/shard_map/ppermute | solution.py:199
  35.6 1.7 %collective-permute-done.8 = bf16[1,16,3072]{2,1,0:T(8,128)(2,1)S(1)} collective-permute-done((bf16[1,16,3072]{2,1,0:T(8,128)(2,1)S(1)}, bf16[1,16,3072]{2,1,0:T(8,128)(2,1)S(1)}, u32[]{:S(2)}, u32[]{:S(2)}) %collective-permute-start.8) | collective-permute-done | bytes 98336 | tf_op jit(solution)/shard_map/ppermute | solution.py:199
  37.8 2.8 %collective-permute-done.4 = bf16[2,16,3072]{2,1,0:T(8,128)(2,1)S(1)} collective-permute-done((bf16[2,16,3072]{2,1,0:T(8,128)(2,1)S(1)}, bf16[2,16,3072]{2,1,0:T(8,128)(2,1)S(1)}, u32[]{:S(2)}, u32[]{:S(2)}) %collective-permute-start.4) | collective-permute-done | bytes 196640 | tf_op jit(solution)/shard_map/ppermute | solution.py:199
  40.7 2.4 %collective-permute-done.9 = bf16[2,16,3072]{2,1,0:T(8,128)(2,1)S(1)} collective-permute-done((bf16[2,16,3072]{2,1,0:T(8,128)(2,1)S(1)}, bf16[2,16,3072]{2,1,0:T(8,128)(2,1)S(1)}, u32[]{:S(2)}, u32[]{:S(2)}) %collective-permute-start.9) | collective-permute-done | bytes 196640 | tf_op jit(solution)/shard_map/ppermute | solution.py:199
  43.9 64.3 %stacks.1 = (f32[1960,128]{1,0:T(8,128)}, f32[1960,128]{1,0:T(8,128)}, bf16[1960,128]{1,0:T(8,128)(2,1)S(1)}, bf16[1960,128]{1,0:T(8,128)(2,1)S(1)}) custom-call(s32[8]{0:T(128)S(1)} %copy-done.1, f32[10,128]{1,0:T(8,128)S(1)} %convert_bitcast_fusion.quality_ref, bf16[8,16,3072]{2,1,0:T(8,128)(2,1)S(1)} %pad_maximum_fusion.u_ref, bf16[1280,25600]{1,0:T(8,128)(2,1)} %x_ref.1), custom_call_target="tpu_custom_call" | custom-call | flops 49325015040 | bytes 65536000 | tf_op jit(solution)/shard_map/stacks/pallas_call | solution.py:266
  108.7 1.4 %collective-permute-done.11 = bf16[1960,128]{1,0:T(8,128)(2,1)S(1)} collective-permute-done((bf16[1960,128]{1,0:T(8,128)(2,1)S(1)}, bf16[1960,128]{1,0:T(8,128)(2,1)S(1)}, u32[]{:S(2)}, u32[]{:S(2)}) %collective-permute-start.11) | collective-permute-done | bytes 501792 | tf_op jit(solution)/shard_map/ppermute | solution.py:287
  110.0 1.3 %add_convert_fusion = bf16[1960,128]{1,0:T(8,128)(2,1)S(1)} fusion(f32[1960,128]{1,0:T(8,128)} %get-tuple-element.11, bf16[1960,128]{1,0:T(8,128)(2,1)S(1)} %collective-permute-done.11), kind=kLoop, calls=%fused_computation.1 | loop fusion | flops 752640 | bytes 2007040 | tf_op jit(solution)/shard_map/convert_element_type | solution.py:290
  111.4 1.6 %collective-permute-start.12 = (bf16[1960,128]{1,0:T(8,128)(2,1)S(1)}, bf16[1960,128]{1,0:T(8,128)(2,1)S(1)}, u32[]{:S(2)}, u32[]{:S(2)}) collective-permute-start(bf16[1960,128]{1,0:T(8,128)(2,1)S(1)} %add_convert_fusion), channel_id=1, source_target_pairs={{0,2},{1,3},{2,0},{3,1},{4,6},{5,7},{6,4},{7,5},{8,10},{9,11},{10,... | collective-permute-start | bytes 1505288 | tf_op jit(solution)/shard_map/ppermute | solution.py:287
  113.0 1.3 %convert_add_fusion.near_ref = f32[1960,128]{1,0:T(8,128)S(1)} fusion(f32[1960,128]{1,0:T(8,128)} %get-tuple-element.9, bf16[1960,128]{1,0:T(8,128)(2,1)S(1)} %collective-permute-done.10), kind=kLoop, calls=%fused_computation.2 | loop fusion | flops 501760 | bytes 2508800 | tf_op jit(solution)/shard_map/add | solution.py:291
  114.3 10.7 %collective-permute-done.12.chip_ref = bf16[1960,128]{1,0:T(8,128)(2,1)S(1)} collective-permute-done((bf16[1960,128]{1,0:T(8,128)(2,1)S(1)}, bf16[1960,128]{1,0:T(8,128)(2,1)S(1)}, u32[]{:S(2)}, u32[]{:S(2)}) %collective-permute-start.12) | collective-permute-done | bytes 501792 | tf_op jit(solution)/shard_map/ppermute | solution.py:287
  124.9 1.3 %finish.1 = f32[1960,128]{1,0:T(8,128)} custom-call(f32[1960,128]{1,0:T(8,128)S(1)} %convert_add_fusion.near_ref, bf16[1960,128]{1,0:T(8,128)(2,1)S(1)} %collective-permute-done.12.chip_ref), custom_call_target="tpu_custom_call" | custom-call | tf_op jit(solution)/shard_map/finish/pallas_call | solution.py:292
  (33 shorter events, 5.9 us)
Async XLA Ops:
  4.3 0.7 copy-start
  6.9 7.9 %collective-permute-start = (bf16[2,16,3072]{2,1,0:T(8,128)(2,1)S(1)}, bf16[2,16,3072]{2,1,0:T(8,128)(2,1)S(1)}, u32[]{:S(2)}, u32[]{:S(2)}) collective-permute-start(bf16[2,16,3072]{2,1,0:T(8,128)(2,1)S(1)} %get-tuple-element.15), channel_id=1, source_target_pairs={{0,4},{4,0},{8,12},{12,8},{16,20},{20,16},{24,28},{28,24},{1,5},{5... | collective-permute-start | bytes 589832 | tf_op jit(solution)/shard_map/ppermute | solution.py:199
  9.9 6.4 %collective-permute-start.5 = (bf16[2,16,3072]{2,1,0:T(8,128)(2,1)S(1)}, bf16[2,16,3072]{2,1,0:T(8,128)(2,1)S(1)}, u32[]{:S(2)}, u32[]{:S(2)}) collective-permute-start(bf16[2,16,3072]{2,1,0:T(8,128)(2,1)S(1)} %get-tuple-element.16), channel_id=1, source_target_pairs={{0,8},{4,12},{8,0},{12,4},{16,24},{20,28},{24,16},{28,20},{1,9},{5... | collective-permute-start | bytes 589832 | tf_op jit(solution)/shard_map/ppermute | solution.py:199
  16.3 4.7 %collective-permute-start.1 = (bf16[1,16,3072]{2,1,0:T(8,128)(2,1)S(1)}, bf16[1,16,3072]{2,1,0:T(8,128)(2,1)S(1)}, u32[]{:S(2)}, u32[]{:S(2)}) collective-permute-start(bf16[1,16,3072]{2,1,0:T(8,128)(2,1)S(1)} %broadcast_select_fusion.11), channel_id=1, source_target_pairs={{0,8},{4,12},{8,0},{12,4},{16,24},{20,28},{24,16},{28,20},{1,9},{5... | collective-permute-start | bytes 294920 | tf_op jit(solution)/shard_map/ppermute | solution.py:199
  18.0 4.7 %collective-permute-start.6 = (bf16[1,16,3072]{2,1,0:T(8,128)(2,1)S(1)}, bf16[1,16,3072]{2,1,0:T(8,128)(2,1)S(1)}, u32[]{:S(2)}, u32[]{:S(2)}) collective-permute-start(bf16[1,16,3072]{2,1,0:T(8,128)(2,1)S(1)} %broadcast_select_fusion.8), channel_id=1, source_target_pairs={{0,4},{4,0},{8,12},{12,8},{16,20},{20,16},{24,28},{28,24},{1,5},{5... | collective-permute-start | bytes 294920 | tf_op jit(solution)/shard_map/ppermute | solution.py:199
  22.7 7.4 %collective-permute-start.2 = (bf16[1,16,3072]{2,1,0:T(8,128)(2,1)S(1)}, bf16[1,16,3072]{2,1,0:T(8,128)(2,1)S(1)}, u32[]{:S(2)}, u32[]{:S(2)}) collective-permute-start(bf16[1,16,3072]{2,1,0:T(8,128)(2,1)S(1)} %get-tuple-element.32), channel_id=1, source_target_pairs={{0,16},{4,20},{8,24},{12,28},{16,0},{20,4},{24,8},{28,12},{1,17},{... | collective-permute-start | bytes 294920 | tf_op jit(solution)/shard_map/ppermute | solution.py:199
  25.4 6.7 %collective-permute-start.7 = (bf16[1,16,3072]{2,1,0:T(8,128)(2,1)S(1)}, bf16[1,16,3072]{2,1,0:T(8,128)(2,1)S(1)}, u32[]{:S(2)}, u32[]{:S(2)}) collective-permute-start(bf16[1,16,3072]{2,1,0:T(8,128)(2,1)S(1)} %get-tuple-element.31), channel_id=1, source_target_pairs={{0,16},{4,20},{8,24},{12,28},{16,0},{20,4},{24,8},{28,12},{1,17},{... | collective-permute-start | bytes 294920 | tf_op jit(solution)/shard_map/ppermute | solution.py:199
  30.2 4.7 %collective-permute-start.3 = (bf16[1,16,3072]{2,1,0:T(8,128)(2,1)S(1)}, bf16[1,16,3072]{2,1,0:T(8,128)(2,1)S(1)}, u32[]{:S(2)}, u32[]{:S(2)}) collective-permute-start(bf16[1,16,3072]{2,1,0:T(8,128)(2,1)S(1)} %add.37), channel_id=1, source_target_pairs={{0,8},{4,12},{8,0},{12,4},{16,24},{20,28},{24,16},{28,20},{1,9},{5... | collective-permute-start | bytes 294920 | tf_op jit(solution)/shard_map/ppermute | solution.py:199
  32.1 5.2 %collective-permute-start.8 = (bf16[1,16,3072]{2,1,0:T(8,128)(2,1)S(1)}, bf16[1,16,3072]{2,1,0:T(8,128)(2,1)S(1)}, u32[]{:S(2)}, u32[]{:S(2)}) collective-permute-start(bf16[1,16,3072]{2,1,0:T(8,128)(2,1)S(1)} %add.40), channel_id=1, source_target_pairs={{0,4},{4,0},{8,12},{12,8},{16,20},{20,16},{24,28},{28,24},{1,5},{5... | collective-permute-start | bytes 294920 | tf_op jit(solution)/shard_map/ppermute | solution.py:199
  34.9 5.7 %collective-permute-start.4 = (bf16[2,16,3072]{2,1,0:T(8,128)(2,1)S(1)}, bf16[2,16,3072]{2,1,0:T(8,128)(2,1)S(1)}, u32[]{:S(2)}, u32[]{:S(2)}) collective-permute-start(bf16[2,16,3072]{2,1,0:T(8,128)(2,1)S(1)} %pad_maximum_fusion.1), channel_id=1, source_target_pairs={{0,4},{4,0},{8,12},{12,8},{16,20},{20,16},{24,28},{28,24},{1,5},{5... | collective-permute-start | bytes 589832 | tf_op jit(solution)/shard_map/ppermute | solution.py:199
  37.4 5.7 %collective-permute-start.9 = (bf16[2,16,3072]{2,1,0:T(8,128)(2,1)S(1)}, bf16[2,16,3072]{2,1,0:T(8,128)(2,1)S(1)}, u32[]{:S(2)}, u32[]{:S(2)}) collective-permute-start(bf16[2,16,3072]{2,1,0:T(8,128)(2,1)S(1)} %pad_maximum_fusion.2), channel_id=1, source_target_pairs={{0,8},{4,12},{8,0},{12,4},{16,24},{20,28},{24,16},{28,20},{1,9},{5... | collective-permute-start | bytes 589832 | tf_op jit(solution)/shard_map/ppermute | solution.py:199
  43.2 0.7 copy-start.1
  108.2 1.9 %collective-permute-start.11 = (bf16[1960,128]{1,0:T(8,128)(2,1)S(1)}, bf16[1960,128]{1,0:T(8,128)(2,1)S(1)}, u32[]{:S(2)}, u32[]{:S(2)}) collective-permute-start(bf16[1960,128]{1,0:T(8,128)(2,1)S(1)} %get-tuple-element.12), channel_id=1, source_target_pairs={{0,1},{1,0},{2,3},{3,2},{4,5},{5,4},{6,7},{7,6},{8,9},{9,8},{10,11... | collective-permute-start | bytes 1505288 | tf_op jit(solution)/shard_map/ppermute | solution.py:287
  108.2 4.8 %collective-permute-start.10 = (bf16[1960,128]{1,0:T(8,128)(2,1)S(1)}, bf16[1960,128]{1,0:T(8,128)(2,1)S(1)}, u32[]{:S(2)}, u32[]{:S(2)}) collective-permute-start(bf16[1960,128]{1,0:T(8,128)(2,1)S(1)} %get-tuple-element.10), channel_id=1, source_target_pairs={{0,1},{1,0},{2,3},{3,2},{4,5},{5,4},{6,7},{7,6},{8,9},{9,8},{10,11... | collective-permute-start | bytes 1505288 | tf_op jit(solution)/shard_map/ppermute | solution.py:287
  111.4 13.5 %collective-permute-start.12 = (bf16[1960,128]{1,0:T(8,128)(2,1)S(1)}, bf16[1960,128]{1,0:T(8,128)(2,1)S(1)}, u32[]{:S(2)}, u32[]{:S(2)}) collective-permute-start(bf16[1960,128]{1,0:T(8,128)(2,1)S(1)} %add_convert_fusion), channel_id=1, source_target_pairs={{0,2},{1,3},{2,0},{3,1},{4,6},{5,7},{6,4},{7,5},{8,10},{9,11},{10,... | collective-permute-start | bytes 1505288 | tf_op jit(solution)/shard_map/ppermute | solution.py:287

commit v10 on v9

--- a/solution.py
+++ b/solution.py
@@ -14,7 +14,7 @@
 EPSILON = 1e-06
 LANES = 128
 TILES = L // LANES
-COLUMNS = 512
+COLUMNS = 1280
 
 
 def lanes(rows, dtype=jnp.int32):

time: 127 us -> 128 us (level)
  Pallas kernels: 67.4 us -> 68.8 us
    pallas_call x1, Pallas kernels: 64.3 us -> 65.6 us  [body(): pl.pallas_call(functools.partial(stack_kernel, blocks, scale), grid=(seg_...]
where the time goes in v10:
time: 128 us
  Pallas kernels  68.8 us (54%)
  waiting for transfers between devices  35.6 us (28%)
  starting transfers between devices  13.7 us (11%)
  local copies, waits for them, and re-layouts  4.7 us (4%)
  other arithmetic  4.67 us (4%)
    pallas_call x1, Pallas kernels, body(): pl.pallas_call(functools.partial(stack_kernel, blocks, scale), grid=(seg_...  65.6 us
    ppermute x10, waiting for transfers between devices, swap(): return lax.ppermute(v, axis, [(d, d ^ bit) for d in range(size)])  23.6 us
    ppermute x3, waiting for transfers between devices, swap(): return lax.ppermute(v, 'win', [(d, d ^ bit) for d in range(win)])  12 us
    ppermute x10, starting transfers between devices, swap(): return lax.ppermute(v, axis, [(d, d ^ bit) for d in range(size)])  11.6 us
    gather x1, local copies, waits for them, and re-layouts, body(): rows = records.at[lax.rem(flat, channels)].get(mode='promise_in_bounds')  3.23 us
  transfers between devices with their start and end apart: 13, of which 12 were waited for; matrix products, arithmetic and copies ran while one was open for 3% of the time, Pallas kernels for 0%

profile of v10, /device:TPU:0, one launch (start us, length us, event | category | flops | bytes accessed | tf_op | source)
XLA Modules:
  0.0 127.6 jit_solution(7380441335261999580)
XLA Ops:
  0.0 0.8 broadcast_select_fusion.19
  1.0 3.2 %gather_fusion = bf16[16,25600]{1,0:T(8,128)(2,1)S(1)} fusion(bf16[1280,25600]{1,0:T(8,128)(2,1)} %x_ref.1, s32[1024]{0:T(1024)S(1)} %pad_clamp_fusion), kind=kCustom, calls=%fused_computation | custom fusion | bytes 1638464 | tf_op jit(solution)/shard_map/gather | solution.py:243
  4.9 1.9 %sources.1 = bf16[8,16,3072]{2,1,0:T(8,128)(2,1)S(1)} custom-call(s32[8]{0:T(128)S(1)} %copy-done, s32[16]{0:T(128)S(1)} %reshape.34.flat_ref, s32[1]{0:T(128)} %bitcast.1.me_ref, bf16[16,25600]{1,0:T(8,128)(2,1)S(1)} %gather_fusion), custom_call_target="tpu_custom_call" | custom-call | tf_op jit(solution)/shard_map/sources/pallas_call | solution.py:246
  6.9 3.0 %collective-permute-start = (bf16[2,16,3072]{2,1,0:T(8,128)(2,1)S(1)}, bf16[2,16,3072]{2,1,0:T(8,128)(2,1)S(1)}, u32[]{:S(2)}, u32[]{:S(2)}) collective-permute-start(bf16[2,16,3072]{2,1,0:T(8,128)(2,1)S(1)} %get-tuple-element.15), channel_id=1, source_target_pairs={{0,4},{4,0},{8,12},{12,8},{16,20},{20,16},{24,28},{28,24},{1,5},{5... | collective-permute-start | bytes 589832 | tf_op jit(solution)/shard_map/ppermute | solution.py:199
  9.9 1.6 %collective-permute-start.5 = (bf16[2,16,3072]{2,1,0:T(8,128)(2,1)S(1)}, bf16[2,16,3072]{2,1,0:T(8,128)(2,1)S(1)}, u32[]{:S(2)}, u32[]{:S(2)}) collective-permute-start(bf16[2,16,3072]{2,1,0:T(8,128)(2,1)S(1)} %get-tuple-element.16), channel_id=1, source_target_pairs={{0,8},{4,12},{8,0},{12,4},{16,24},{20,28},{24,16},{28,20},{1,9},{5... | collective-permute-start | bytes 589832 | tf_op jit(solution)/shard_map/ppermute | solution.py:199
  11.5 3.3 %collective-permute-done = bf16[2,16,3072]{2,1,0:T(8,128)(2,1)S(1)} collective-permute-done((bf16[2,16,3072]{2,1,0:T(8,128)(2,1)S(1)}, bf16[2,16,3072]{2,1,0:T(8,128)(2,1)S(1)}, u32[]{:S(2)}, u32[]{:S(2)}) %collective-permute-start) | collective-permute-done | bytes 196640 | tf_op jit(solution)/shard_map/ppermute | solution.py:199
  14.8 1.5 %collective-permute-done.5 = bf16[2,16,3072]{2,1,0:T(8,128)(2,1)S(1)} collective-permute-done((bf16[2,16,3072]{2,1,0:T(8,128)(2,1)S(1)}, bf16[2,16,3072]{2,1,0:T(8,128)(2,1)S(1)}, u32[]{:S(2)}, u32[]{:S(2)}) %collective-permute-start.5) | collective-permute-done | bytes 196640 | tf_op jit(solution)/shard_map/ppermute | solution.py:199
  16.3 1.6 %collective-permute-start.1 = (bf16[1,16,3072]{2,1,0:T(8,128)(2,1)S(1)}, bf16[1,16,3072]{2,1,0:T(8,128)(2,1)S(1)}, u32[]{:S(2)}, u32[]{:S(2)}) collective-permute-start(bf16[1,16,3072]{2,1,0:T(8,128)(2,1)S(1)} %broadcast_select_fusion.11), channel_id=1, source_target_pairs={{0,8},{4,12},{8,0},{12,4},{16,24},{20,28},{24,16},{28,20},{1,9},{5... | collective-permute-start | bytes 294920 | tf_op jit(solution)/shard_map/ppermute | solution.py:199
  18.6 2.4 %collective-permute-done.1 = bf16[1,16,3072]{2,1,0:T(8,128)(2,1)S(1)} collective-permute-done((bf16[1,16,3072]{2,1,0:T(8,128)(2,1)S(1)}, bf16[1,16,3072]{2,1,0:T(8,128)(2,1)S(1)}, u32[]{:S(2)}, u32[]{:S(2)}) %collective-permute-start.1) | collective-permute-done | bytes 98336 | tf_op jit(solution)/shard_map/ppermute | solution.py:199
  21.0 1.7 %collective-permute-done.6 = bf16[1,16,3072]{2,1,0:T(8,128)(2,1)S(1)} collective-permute-done((bf16[1,16,3072]{2,1,0:T(8,128)(2,1)S(1)}, bf16[1,16,3072]{2,1,0:T(8,128)(2,1)S(1)}, u32[]{:S(2)}, u32[]{:S(2)}) %collective-permute-start.6) | collective-permute-done | bytes 98336 | tf_op jit(solution)/shard_map/ppermute | solution.py:199
  22.7 2.6 %collective-permute-start.2 = (bf16[1,16,3072]{2,1,0:T(8,128)(2,1)S(1)}, bf16[1,16,3072]{2,1,0:T(8,128)(2,1)S(1)}, u32[]{:S(2)}, u32[]{:S(2)}) collective-permute-start(bf16[1,16,3072]{2,1,0:T(8,128)(2,1)S(1)} %get-tuple-element.32), channel_id=1, source_target_pairs={{0,16},{4,20},{8,24},{12,28},{16,0},{20,4},{24,8},{28,12},{1,17},{... | collective-permute-start | bytes 294920 | tf_op jit(solution)/shard_map/ppermute | solution.py:199
  25.7 4.5 %collective-permute-done.2 = bf16[1,16,3072]{2,1,0:T(8,128)(2,1)S(1)} collective-permute-done((bf16[1,16,3072]{2,1,0:T(8,128)(2,1)S(1)}, bf16[1,16,3072]{2,1,0:T(8,128)(2,1)S(1)}, u32[]{:S(2)}, u32[]{:S(2)}) %collective-permute-start.2) | collective-permute-done | bytes 98336 | tf_op jit(solution)/shard_map/ppermute | solution.py:199
  31.0 1.1 collective-permute-done.7
  32.7 2.2 %collective-permute-done.3 = bf16[1,16,3072]{2,1,0:T(8,128)(2,1)S(1)} collective-permute-done((bf16[1,16,3072]{2,1,0:T(8,128)(2,1)S(1)}, bf16[1,16,3072]{2,1,0:T(8,128)(2,1)S(1)}, u32[]{:S(2)}, u32[]{:S(2)}) %collective-permute-start.3) | collective-permute-done | bytes 98336 | tf_op jit(solution)/shard_map/ppermute | solution.py:199
  35.6 1.7 %collective-permute-done.8 = bf16[1,16,3072]{2,1,0:T(8,128)(2,1)S(1)} collective-permute-done((bf16[1,16,3072]{2,1,0:T(8,128)(2,1)S(1)}, bf16[1,16,3072]{2,1,0:T(8,128)(2,1)S(1)}, u32[]{:S(2)}, u32[]{:S(2)}) %collective-permute-start.8) | collective-permute-done | bytes 98336 | tf_op jit(solution)/shard_map/ppermute | solution.py:199
  37.8 2.8 %collective-permute-done.4 = bf16[2,16,3072]{2,1,0:T(8,128)(2,1)S(1)} collective-permute-done((bf16[2,16,3072]{2,1,0:T(8,128)(2,1)S(1)}, bf16[2,16,3072]{2,1,0:T(8,128)(2,1)S(1)}, u32[]{:S(2)}, u32[]{:S(2)}) %collective-permute-start.4) | collective-permute-done | bytes 196640 | tf_op jit(solution)/shard_map/ppermute | solution.py:199
  40.7 2.4 %collective-permute-done.9 = bf16[2,16,3072]{2,1,0:T(8,128)(2,1)S(1)} collective-permute-done((bf16[2,16,3072]{2,1,0:T(8,128)(2,1)S(1)}, bf16[2,16,3072]{2,1,0:T(8,128)(2,1)S(1)}, u32[]{:S(2)}, u32[]{:S(2)}) %collective-permute-start.9) | collective-permute-done | bytes 196640 | tf_op jit(solution)/shard_map/ppermute | solution.py:199
  43.9 65.6 %stacks.1 = (f32[1960,128]{1,0:T(8,128)}, f32[1960,128]{1,0:T(8,128)}, bf16[1960,128]{1,0:T(8,128)(2,1)S(1)}, bf16[1960,128]{1,0:T(8,128)(2,1)S(1)}) custom-call(s32[8]{0:T(128)S(1)} %copy-done.1, f32[10,128]{1,0:T(8,128)S(1)} %convert_bitcast_fusion.quality_ref, bf16[8,16,3072]{2,1,0:T(8,128)(2,1)S(1)} %pad_maximum_fusion.u_ref, bf16[1280,25600]{1,0:T(8,128)(2,1)} %x_ref.1), custom_call_target="tpu_custom_call" | custom-call | flops 49325015040 | bytes 65536000 | tf_op jit(solution)/shard_map/stacks/pallas_call | solution.py:266
  110.0 1.4 %collective-permute-done.11 = bf16[1960,128]{1,0:T(8,128)(2,1)S(1)} collective-permute-done((bf16[1960,128]{1,0:T(8,128)(2,1)S(1)}, bf16[1960,128]{1,0:T(8,128)(2,1)S(1)}, u32[]{:S(2)}, u32[]{:S(2)}) %collective-permute-start.11) | collective-permute-done | bytes 501792 | tf_op jit(solution)/shard_map/ppermute | solution.py:287
  111.4 1.3 %add_convert_fusion = bf16[1960,128]{1,0:T(8,128)(2,1)S(1)} fusion(f32[1960,128]{1,0:T(8,128)} %get-tuple-element.11, bf16[1960,128]{1,0:T(8,128)(2,1)S(1)} %collective-permute-done.11), kind=kLoop, calls=%fused_computation.1 | loop fusion | flops 752640 | bytes 2007040 | tf_op jit(solution)/shard_map/convert_element_type | solution.py:290
  112.7 1.6 %collective-permute-start.12 = (bf16[1960,128]{1,0:T(8,128)(2,1)S(1)}, bf16[1960,128]{1,0:T(8,128)(2,1)S(1)}, u32[]{:S(2)}, u32[]{:S(2)}) collective-permute-start(bf16[1960,128]{1,0:T(8,128)(2,1)S(1)} %add_convert_fusion), channel_id=1, source_target_pairs={{0,2},{1,3},{2,0},{3,1},{4,6},{5,7},{6,4},{7,5},{8,10},{9,11},{10,... | collective-permute-start | bytes 1505288 | tf_op jit(solution)/shard_map/ppermute | solution.py:287
  114.3 1.3 %convert_add_fusion.near_ref = f32[1960,128]{1,0:T(8,128)S(1)} fusion(f32[1960,128]{1,0:T(8,128)} %get-tuple-element.9, bf16[1960,128]{1,0:T(8,128)(2,1)S(1)} %collective-permute-done.10), kind=kLoop, calls=%fused_computation.2 | loop fusion | flops 501760 | bytes 2508800 | tf_op jit(solution)/shard_map/add | solution.py:291
  115.6 10.7 %collective-permute-done.12.chip_ref = bf16[1960,128]{1,0:T(8,128)(2,1)S(1)} collective-permute-done((bf16[1960,128]{1,0:T(8,128)(2,1)S(1)}, bf16[1960,128]{1,0:T(8,128)(2,1)S(1)}, u32[]{:S(2)}, u32[]{:S(2)}) %collective-permute-start.12) | collective-permute-done | bytes 501792 | tf_op jit(solution)/shard_map/ppermute | solution.py:287
  126.3 1.3 %finish.1 = f32[1960,128]{1,0:T(8,128)} custom-call(f32[1960,128]{1,0:T(8,128)S(1)} %convert_add_fusion.near_ref, bf16[1960,128]{1,0:T(8,128)(2,1)S(1)} %collective-permute-done.12.chip_ref), custom_call_target="tpu_custom_call" | custom-call | tf_op jit(solution)/shard_map/finish/pallas_call | solution.py:292
  (33 shorter events, 5.9 us)
Async XLA Ops:
  4.3 0.7 copy-start
  6.9 7.9 %collective-permute-start = (bf16[2,16,3072]{2,1,0:T(8,128)(2,1)S(1)}, bf16[2,16,3072]{2,1,0:T(8,128)(2,1)S(1)}, u32[]{:S(2)}, u32[]{:S(2)}) collective-permute-start(bf16[2,16,3072]{2,1,0:T(8,128)(2,1)S(1)} %get-tuple-element.15), channel_id=1, source_target_pairs={{0,4},{4,0},{8,12},{12,8},{16,20},{20,16},{24,28},{28,24},{1,5},{5... | collective-permute-start | bytes 589832 | tf_op jit(solution)/shard_map/ppermute | solution.py:199
  9.9 6.4 %collective-permute-start.5 = (bf16[2,16,3072]{2,1,0:T(8,128)(2,1)S(1)}, bf16[2,16,3072]{2,1,0:T(8,128)(2,1)S(1)}, u32[]{:S(2)}, u32[]{:S(2)}) collective-permute-start(bf16[2,16,3072]{2,1,0:T(8,128)(2,1)S(1)} %get-tuple-element.16), channel_id=1, source_target_pairs={{0,8},{4,12},{8,0},{12,4},{16,24},{20,28},{24,16},{28,20},{1,9},{5... | collective-permute-start | bytes 589832 | tf_op jit(solution)/shard_map/ppermute | solution.py:199
  16.3 4.7 %collective-permute-start.1 = (bf16[1,16,3072]{2,1,0:T(8,128)(2,1)S(1)}, bf16[1,16,3072]{2,1,0:T(8,128)(2,1)S(1)}, u32[]{:S(2)}, u32[]{:S(2)}) collective-permute-start(bf16[1,16,3072]{2,1,0:T(8,128)(2,1)S(1)} %broadcast_select_fusion.11), channel_id=1, source_target_pairs={{0,8},{4,12},{8,0},{12,4},{16,24},{20,28},{24,16},{28,20},{1,9},{5... | collective-permute-start | bytes 294920 | tf_op jit(solution)/shard_map/ppermute | solution.py:199
  18.0 4.7 %collective-permute-start.6 = (bf16[1,16,3072]{2,1,0:T(8,128)(2,1)S(1)}, bf16[1,16,3072]{2,1,0:T(8,128)(2,1)S(1)}, u32[]{:S(2)}, u32[]{:S(2)}) collective-permute-start(bf16[1,16,3072]{2,1,0:T(8,128)(2,1)S(1)} %broadcast_select_fusion.8), channel_id=1, source_target_pairs={{0,4},{4,0},{8,12},{12,8},{16,20},{20,16},{24,28},{28,24},{1,5},{5... | collective-permute-start | bytes 294920 | tf_op jit(solution)/shard_map/ppermute | solution.py:199
  22.7 7.4 %collective-permute-start.2 = (bf16[1,16,3072]{2,1,0:T(8,128)(2,1)S(1)}, bf16[1,16,3072]{2,1,0:T(8,128)(2,1)S(1)}, u32[]{:S(2)}, u32[]{:S(2)}) collective-permute-start(bf16[1,16,3072]{2,1,0:T(8,128)(2,1)S(1)} %get-tuple-element.32), channel_id=1, source_target_pairs={{0,16},{4,20},{8,24},{12,28},{16,0},{20,4},{24,8},{28,12},{1,17},{... | collective-permute-start | bytes 294920 | tf_op jit(solution)/shard_map/ppermute | solution.py:199
  25.4 6.7 %collective-permute-start.7 = (bf16[1,16,3072]{2,1,0:T(8,128)(2,1)S(1)}, bf16[1,16,3072]{2,1,0:T(8,128)(2,1)S(1)}, u32[]{:S(2)}, u32[]{:S(2)}) collective-permute-start(bf16[1,16,3072]{2,1,0:T(8,128)(2,1)S(1)} %get-tuple-element.31), channel_id=1, source_target_pairs={{0,16},{4,20},{8,24},{12,28},{16,0},{20,4},{24,8},{28,12},{1,17},{... | collective-permute-start | bytes 294920 | tf_op jit(solution)/shard_map/ppermute | solution.py:199
  30.2 4.7 %collective-permute-start.3 = (bf16[1,16,3072]{2,1,0:T(8,128)(2,1)S(1)}, bf16[1,16,3072]{2,1,0:T(8,128)(2,1)S(1)}, u32[]{:S(2)}, u32[]{:S(2)}) collective-permute-start(bf16[1,16,3072]{2,1,0:T(8,128)(2,1)S(1)} %add.37), channel_id=1, source_target_pairs={{0,8},{4,12},{8,0},{12,4},{16,24},{20,28},{24,16},{28,20},{1,9},{5... | collective-permute-start | bytes 294920 | tf_op jit(solution)/shard_map/ppermute | solution.py:199
  32.1 5.2 %collective-permute-start.8 = (bf16[1,16,3072]{2,1,0:T(8,128)(2,1)S(1)}, bf16[1,16,3072]{2,1,0:T(8,128)(2,1)S(1)}, u32[]{:S(2)}, u32[]{:S(2)}) collective-permute-start(bf16[1,16,3072]{2,1,0:T(8,128)(2,1)S(1)} %add.40), channel_id=1, source_target_pairs={{0,4},{4,0},{8,12},{12,8},{16,20},{20,16},{24,28},{28,24},{1,5},{5... | collective-permute-start | bytes 294920 | tf_op jit(solution)/shard_map/ppermute | solution.py:199
  34.9 5.7 %collective-permute-start.4 = (bf16[2,16,3072]{2,1,0:T(8,128)(2,1)S(1)}, bf16[2,16,3072]{2,1,0:T(8,128)(2,1)S(1)}, u32[]{:S(2)}, u32[]{:S(2)}) collective-permute-start(bf16[2,16,3072]{2,1,0:T(8,128)(2,1)S(1)} %pad_maximum_fusion.1), channel_id=1, source_target_pairs={{0,4},{4,0},{8,12},{12,8},{16,20},{20,16},{24,28},{28,24},{1,5},{5... | collective-permute-start | bytes 589832 | tf_op jit(solution)/shard_map/ppermute | solution.py:199
  37.4 5.7 %collective-permute-start.9 = (bf16[2,16,3072]{2,1,0:T(8,128)(2,1)S(1)}, bf16[2,16,3072]{2,1,0:T(8,128)(2,1)S(1)}, u32[]{:S(2)}, u32[]{:S(2)}) collective-permute-start(bf16[2,16,3072]{2,1,0:T(8,128)(2,1)S(1)} %pad_maximum_fusion.2), channel_id=1, source_target_pairs={{0,8},{4,12},{8,0},{12,4},{16,24},{20,28},{24,16},{28,20},{1,9},{5... | collective-permute-start | bytes 589832 | tf_op jit(solution)/shard_map/ppermute | solution.py:199
  43.2 0.7 copy-start.1
  109.5 1.9 %collective-permute-start.11 = (bf16[1960,128]{1,0:T(8,128)(2,1)S(1)}, bf16[1960,128]{1,0:T(8,128)(2,1)S(1)}, u32[]{:S(2)}, u32[]{:S(2)}) collective-permute-start(bf16[1960,128]{1,0:T(8,128)(2,1)S(1)} %get-tuple-element.12), channel_id=1, source_target_pairs={{0,1},{1,0},{2,3},{3,2},{4,5},{5,4},{6,7},{7,6},{8,9},{9,8},{10,11... | collective-permute-start | bytes 1505288 | tf_op jit(solution)/shard_map/ppermute | solution.py:287
  109.5 4.8 %collective-permute-start.10 = (bf16[1960,128]{1,0:T(8,128)(2,1)S(1)}, bf16[1960,128]{1,0:T(8,128)(2,1)S(1)}, u32[]{:S(2)}, u32[]{:S(2)}) collective-permute-start(bf16[1960,128]{1,0:T(8,128)(2,1)S(1)} %get-tuple-element.10), channel_id=1, source_target_pairs={{0,1},{1,0},{2,3},{3,2},{4,5},{5,4},{6,7},{7,6},{8,9},{9,8},{10,11... | collective-permute-start | bytes 1505288 | tf_op jit(solution)/shard_map/ppermute | solution.py:287
  112.7 13.5 %collective-permute-start.12 = (bf16[1960,128]{1,0:T(8,128)(2,1)S(1)}, bf16[1960,128]{1,0:T(8,128)(2,1)S(1)}, u32[]{:S(2)}, u32[]{:S(2)}) collective-permute-start(bf16[1960,128]{1,0:T(8,128)(2,1)S(1)} %add_convert_fusion), channel_id=1, source_target_pairs={{0,2},{1,3},{2,0},{3,1},{4,6},{5,7},{6,4},{7,5},{8,10},{9,11},{10,... | collective-permute-start | bytes 1505288 | tf_op jit(solution)/shard_map/ppermute | solution.py:287

commit v11 on v9

--- a/solution.py
+++ b/solution.py
@@ -14,6 +14,7 @@
 EPSILON = 1e-06
 LANES = 128
 TILES = L // LANES
+ROWS = 64
 COLUMNS = 512
 
 
@@ -54,14 +55,20 @@
     lax.fori_loop(0, seg_count, one, 0)
 
 
-def builders(u_ref, seg, off, a_ref, count):
+def builders(u_refs, seg, off, a_ref, count):
     lane = lanes(count)
     wide = lanes(count * (TILES + 1))
     zero = jnp.zeros((count, LANES), jnp.bfloat16)
     held = []
 
     def start():
-        plain = [u_ref[seg, :, m * LANES : (m + 1) * LANES] for m in range(TILES)]
+        half = u_refs[0].shape[0]
+        pick = lane < jnp.where(seg < half, LANES, 0)
+        low, high = jnp.minimum(seg, half - 1), jnp.maximum(seg - half, 0)
+        plain = []
+        for m in range(TILES):
+            span = slice(m * LANES, (m + 1) * LANES)
+            plain.append(jnp.where(pick, u_refs[0][low, :, span], u_refs[1][high, :, span]))
         turned = [pltpu.roll(tile, lax.rem(off, LANES), 1) for tile in plain]
         early = lane < off
         moved = [
@@ -89,19 +96,22 @@
 
 
 def weigh(x_ref, off, row, size, gain_ref):
-    early = lanes(size) < off
-
-    def square(m):
-        value = x_ref[row : row + size, m * LANES : (m + 1) * LANES]
-        return value * value
-
-    squares = [jnp.where(early, square(TILES), square(0))]
-    squares += [square(m) for m in range(1, TILES)]
-    total = jnp.zeros((size, LANES), jnp.float32)
-    for m in range(0, TILES, 4):
-        four = (squares[m] + squares[m + 1]) + (squares[m + 2] + squares[m + 3])
-        total = total + four.astype(jnp.float32)
-    power = jnp.sum(jnp.transpose(total), axis=0, keepdims=True) / L
+    parts = []
+    for at in range(row, row + size, ROWS):
+        early = lanes(ROWS) < off
+
+        def square(m):
+            value = x_ref[at : at + ROWS, m * LANES : (m + 1) * LANES]
+            return value * value
+
+        total = jnp.zeros((ROWS, LANES), jnp.float32)
+        for m in range(0, TILES, 4):
+            one = square(m) if m else jnp.where(early, square(TILES), square(0))
+            four = (one + square(m + 1)) + (square(m + 2) + square(m + 3))
+            total = total + four.astype(jnp.float32)
+        parts.append(total)
+    across = jnp.concatenate(parts, axis=0)
+    power = jnp.sum(jnp.transpose(across), axis=0, keepdims=True) / L
     gain_ref[:, row : row + size] = lax.rsqrt(power + EPSILON)
 
 
@@ -116,20 +126,21 @@
 
 
 def stack_kernel(
-    blocks, scale, offsets_ref, quality_ref, u_ref, x_ref,
+    blocks, scale, offsets_ref, quality_ref, u0, u1, x_ref,
     keep0, keep1, send0, send1, a0, a1, total, gain_ref,
 ):
     slots = (a0, a1)
+    u_refs = (u0, u1)
     n = pl.program_id(0)
     last = pl.num_programs(0) - 1
     off = offsets_ref[n]
-    count = u_ref.shape[1]
+    count = u0.shape[1]
     groups = total.shape[0]
 
     @pl.when(n == 0)
     def _():
         total[...] = jnp.zeros_like(total)
-        for piece in builders(u_ref, 0, off, a0, count):
+        for piece in builders(u_refs, 0, off, a0, count):
             piece()
 
     def pieces(k, x_ref):
@@ -143,7 +154,7 @@
 
     def segment(parity):
         later = jnp.minimum(n + 1, last)
-        built = builders(u_ref, later, offsets_ref[later], slots[1 - parity], count)
+        built = builders(u_refs, later, offsets_ref[later], slots[1 - parity], count)
         for piece in pieces(0, x_ref):
             piece()
         for k, (start, width) in enumerate(blocks):
@@ -221,7 +232,7 @@
     values = [value[:half], value[half:]]
     for steps in zip(*plans):
         values = [step(v, bit) for v, (step, bit) in zip(values, steps)]
-    return jnp.concatenate(values, axis=0)
+    return values
 
 
 def solution(mesh):
@@ -267,7 +278,7 @@
             functools.partial(stack_kernel, blocks, scale),
             grid=(seg_count,),
             out_shape=(kept, kept, sent, sent),
-            in_specs=[smem, vmem, vmem, pl.BlockSpec((channels, stride), lambda g: (0, g))],
+            in_specs=[smem, vmem, vmem, vmem, pl.BlockSpec((channels, stride), lambda g: (0, g))],
             out_specs=(vmem,) * 4,
             scratch_shapes=[pltpu.VMEM((TILES, rows, LANES), jnp.bfloat16)] * 2
             + [
@@ -281,7 +292,7 @@
                 transcendentals=0,
             ),
             name="stacks",
-        )(offsets, usable.reshape(even, LANES), sources, records)
+        )(offsets, usable.reshape(even, LANES), *sources, records)
 
         def swap(v, bit):
             return lax.ppermute(v, "win", [(d, d ^ bit) for d in range(win)])

time: 127 us -> 126 us (level)
  transfers between devices with their start and end apart: 13 -> 13, of which waited for: 12 -> 11; matrix products, arithmetic and copies ran while one was open for 3% -> 3% of each run, Pallas kernels for 0% -> 0%
where the time goes in v11:
time: 126 us
  Pallas kernels  67.5 us (54%)
  waiting for transfers between devices  34.8 us (28%)
  starting transfers between devices  14.2 us (11%)
  local copies, waits for them, and re-layouts  4.7 us (4%)
  other arithmetic  4.64 us (4%)
    pallas_call x1, Pallas kernels, body(): pl.pallas_call(functools.partial(stack_kernel, blocks, scale), grid=(seg_...  64.4 us
    ppermute x10, waiting for transfers between devices, swap(): return lax.ppermute(v, axis, [(d, d ^ bit) for d in range(size)])  22.8 us
    ppermute x10, starting transfers between devices, swap(): return lax.ppermute(v, axis, [(d, d ^ bit) for d in range(size)])  12.1 us
    ppermute x3, waiting for transfers between devices, swap(): return lax.ppermute(v, 'win', [(d, d ^ bit) for d in range(win)])  12 us
    gather x1, local copies, waits for them, and re-layouts, body(): rows = records.at[lax.rem(flat, channels)].get(mode='promise_in_bounds')  3.23 us
  transfers between devices with their start and end apart: 13, of which 11 were waited for; matrix products, arithmetic and copies ran while one was open for 3% of the time, Pallas kernels for 0%

profile of v11, /device:TPU:0, one launch (start us, length us, event | category | flops | bytes accessed | tf_op | source)
XLA Modules:
  0.0 126.0 jit_solution(11490988483628324621)
XLA Ops:
  0.0 0.8 broadcast_select_fusion.19
  1.0 3.2 %gather_fusion = bf16[16,25600]{1,0:T(8,128)(2,1)S(1)} fusion(bf16[1280,25600]{1,0:T(8,128)(2,1)} %x_ref.1, s32[1024]{0:T(1024)S(1)} %pad_clamp_fusion), kind=kCustom, calls=%fused_computation | custom fusion | bytes 1638464 | tf_op jit(solution)/shard_map/gather | solution.py:254
  4.9 1.9 %sources.1 = bf16[8,16,3072]{2,1,0:T(8,128)(2,1)S(1)} custom-call(s32[8]{0:T(128)S(1)} %copy-done, s32[16]{0:T(128)S(1)} %reshape.34.flat_ref, s32[1]{0:T(128)} %bitcast.1.me_ref, bf16[16,25600]{1,0:T(8,128)(2,1)S(1)} %gather_fusion), custom_call_target="tpu_custom_call" | custom-call | tf_op jit(solution)/shard_map/sources/pallas_call | solution.py:257
  6.9 3.0 %collective-permute-start = (bf16[2,16,3072]{2,1,0:T(8,128)(2,1)S(1)}, bf16[2,16,3072]{2,1,0:T(8,128)(2,1)S(1)}, u32[]{:S(2)}, u32[]{:S(2)}) collective-permute-start(bf16[2,16,3072]{2,1,0:T(8,128)(2,1)S(1)} %get-tuple-element.16), channel_id=1, source_target_pairs={{0,4},{4,0},{8,12},{12,8},{16,20},{20,16},{24,28},{28,24},{1,5},{5... | collective-permute-start | bytes 589832 | tf_op jit(solution)/shard_map/ppermute | solution.py:210
  9.9 1.6 %collective-permute-start.5 = (bf16[2,16,3072]{2,1,0:T(8,128)(2,1)S(1)}, bf16[2,16,3072]{2,1,0:T(8,128)(2,1)S(1)}, u32[]{:S(2)}, u32[]{:S(2)}) collective-permute-start(bf16[2,16,3072]{2,1,0:T(8,128)(2,1)S(1)} %get-tuple-element.15), channel_id=1, source_target_pairs={{0,8},{4,12},{8,0},{12,4},{16,24},{20,28},{24,16},{28,20},{1,9},{5... | collective-permute-start | bytes 589832 | tf_op jit(solution)/shard_map/ppermute | solution.py:210
  11.5 3.3 %collective-permute-done = bf16[2,16,3072]{2,1,0:T(8,128)(2,1)S(1)} collective-permute-done((bf16[2,16,3072]{2,1,0:T(8,128)(2,1)S(1)}, bf16[2,16,3072]{2,1,0:T(8,128)(2,1)S(1)}, u32[]{:S(2)}, u32[]{:S(2)}) %collective-permute-start) | collective-permute-done | bytes 196640 | tf_op jit(solution)/shard_map/ppermute | solution.py:210
  14.8 1.5 %collective-permute-done.5 = bf16[2,16,3072]{2,1,0:T(8,128)(2,1)S(1)} collective-permute-done((bf16[2,16,3072]{2,1,0:T(8,128)(2,1)S(1)}, bf16[2,16,3072]{2,1,0:T(8,128)(2,1)S(1)}, u32[]{:S(2)}, u32[]{:S(2)}) %collective-permute-start.5) | collective-permute-done | bytes 196640 | tf_op jit(solution)/shard_map/ppermute | solution.py:210
  16.3 1.6 %collective-permute-start.1 = (bf16[1,16,3072]{2,1,0:T(8,128)(2,1)S(1)}, bf16[1,16,3072]{2,1,0:T(8,128)(2,1)S(1)}, u32[]{:S(2)}, u32[]{:S(2)}) collective-permute-start(bf16[1,16,3072]{2,1,0:T(8,128)(2,1)S(1)} %broadcast_select_fusion.11), channel_id=1, source_target_pairs={{0,8},{4,12},{8,0},{12,4},{16,24},{20,28},{24,16},{28,20},{1,9},{5... | collective-permute-start | bytes 294920 | tf_op jit(solution)/shard_map/ppermute | solution.py:210
  18.6 2.4 %collective-permute-done.1 = bf16[1,16,3072]{2,1,0:T(8,128)(2,1)S(1)} collective-permute-done((bf16[1,16,3072]{2,1,0:T(8,128)(2,1)S(1)}, bf16[1,16,3072]{2,1,0:T(8,128)(2,1)S(1)}, u32[]{:S(2)}, u32[]{:S(2)}) %collective-permute-start.1) | collective-permute-done | bytes 98336 | tf_op jit(solution)/shard_map/ppermute | solution.py:210
  21.0 1.7 %collective-permute-done.6 = bf16[1,16,3072]{2,1,0:T(8,128)(2,1)S(1)} collective-permute-done((bf16[1,16,3072]{2,1,0:T(8,128)(2,1)S(1)}, bf16[1,16,3072]{2,1,0:T(8,128)(2,1)S(1)}, u32[]{:S(2)}, u32[]{:S(2)}) %collective-permute-start.6) | collective-permute-done | bytes 98336 | tf_op jit(solution)/shard_map/ppermute | solution.py:210
  22.7 2.6 %collective-permute-start.7 = (bf16[1,16,3072]{2,1,0:T(8,128)(2,1)S(1)}, bf16[1,16,3072]{2,1,0:T(8,128)(2,1)S(1)}, u32[]{:S(2)}, u32[]{:S(2)}) collective-permute-start(bf16[1,16,3072]{2,1,0:T(8,128)(2,1)S(1)} %get-tuple-element.31), channel_id=1, source_target_pairs={{0,16},{4,20},{8,24},{12,28},{16,0},{20,4},{24,8},{28,12},{1,17},{... | collective-permute-start | bytes 294920 | tf_op jit(solution)/shard_map/ppermute | solution.py:210
  25.7 5.2 %collective-permute-done.7 = bf16[1,16,3072]{2,1,0:T(8,128)(2,1)S(1)} collective-permute-done((bf16[1,16,3072]{2,1,0:T(8,128)(2,1)S(1)}, bf16[1,16,3072]{2,1,0:T(8,128)(2,1)S(1)}, u32[]{:S(2)}, u32[]{:S(2)}) %collective-permute-start.7) | collective-permute-done | bytes 98336 | tf_op jit(solution)/shard_map/ppermute | solution.py:210
  32.4 3.2 %collective-permute-done.8 = bf16[1,16,3072]{2,1,0:T(8,128)(2,1)S(1)} collective-permute-done((bf16[1,16,3072]{2,1,0:T(8,128)(2,1)S(1)}, bf16[1,16,3072]{2,1,0:T(8,128)(2,1)S(1)}, u32[]{:S(2)}, u32[]{:S(2)}) %collective-permute-start.8) | collective-permute-done | bytes 98336 | tf_op jit(solution)/shard_map/ppermute | solution.py:210
  35.8 1.3 %collective-permute-done.3 = bf16[1,16,3072]{2,1,0:T(8,128)(2,1)S(1)} collective-permute-done((bf16[1,16,3072]{2,1,0:T(8,128)(2,1)S(1)}, bf16[1,16,3072]{2,1,0:T(8,128)(2,1)S(1)}, u32[]{:S(2)}, u32[]{:S(2)}) %collective-permute-start.3) | collective-permute-done | bytes 98336 | tf_op jit(solution)/shard_map/ppermute | solution.py:210
  37.1 1.5 %collective-permute-start.4 = (bf16[2,16,3072]{2,1,0:T(8,128)(2,1)S(1)}, bf16[2,16,3072]{2,1,0:T(8,128)(2,1)S(1)}, u32[]{:S(2)}, u32[]{:S(2)}) collective-permute-start(bf16[2,16,3072]{2,1,0:T(8,128)(2,1)S(1)} %pad_maximum_fusion.2), channel_id=1, source_target_pairs={{0,4},{4,0},{8,12},{12,8},{16,20},{20,16},{24,28},{28,24},{1,5},{5... | collective-permute-start | bytes 589832 | tf_op jit(solution)/shard_map/ppermute | solution.py:210
  38.6 2.8 %collective-permute-done.9 = bf16[2,16,3072]{2,1,0:T(8,128)(2,1)S(1)} collective-permute-done((bf16[2,16,3072]{2,1,0:T(8,128)(2,1)S(1)}, bf16[2,16,3072]{2,1,0:T(8,128)(2,1)S(1)}, u32[]{:S(2)}, u32[]{:S(2)}) %collective-permute-start.9) | collective-permute-done | bytes 196640 | tf_op jit(solution)/shard_map/ppermute | solution.py:210
  41.5 1.3 %collective-permute-done.4 = bf16[2,16,3072]{2,1,0:T(8,128)(2,1)S(1)} collective-permute-done((bf16[2,16,3072]{2,1,0:T(8,128)(2,1)S(1)}, bf16[2,16,3072]{2,1,0:T(8,128)(2,1)S(1)}, u32[]{:S(2)}, u32[]{:S(2)}) %collective-permute-start.4) | collective-permute-done | bytes 196640 | tf_op jit(solution)/shard_map/ppermute | solution.py:210
  43.6 64.4 %stacks.1 = (f32[1960,128]{1,0:T(8,128)}, f32[1960,128]{1,0:T(8,128)}, bf16[1960,128]{1,0:T(8,128)(2,1)S(1)}, bf16[1960,128]{1,0:T(8,128)(2,1)S(1)}) custom-call(s32[8]{0:T(128)S(1)} %copy-done.1, f32[10,128]{1,0:T(8,128)S(1)} %convert_bitcast_fusion.quality_ref, bf16[4,16,3072]{2,1,0:T(8,128)(2,1)S(1)} %pad_maximum_fusion.u0, ...), custom_call_target="tpu_custom_call" | custom-call | flops 49325015040 | bytes 65536000 | tf_op jit(solution)/shard_map/stacks/pallas_call | solution.py:277
  108.5 1.4 %collective-permute-done.11 = bf16[1960,128]{1,0:T(8,128)(2,1)S(1)} collective-permute-done((bf16[1960,128]{1,0:T(8,128)(2,1)S(1)}, bf16[1960,128]{1,0:T(8,128)(2,1)S(1)}, u32[]{:S(2)}, u32[]{:S(2)}) %collective-permute-start.11) | collective-permute-done | bytes 501792 | tf_op jit(solution)/shard_map/ppermute | solution.py:298
  109.8 1.3 %add_convert_fusion = bf16[1960,128]{1,0:T(8,128)(2,1)S(1)} fusion(f32[1960,128]{1,0:T(8,128)} %get-tuple-element.11, bf16[1960,128]{1,0:T(8,128)(2,1)S(1)} %collective-permute-done.11), kind=kLoop, calls=%fused_computation.1 | loop fusion | flops 752640 | bytes 2007040 | tf_op jit(solution)/shard_map/convert_element_type | solution.py:301
  111.2 1.6 %collective-permute-start.12 = (bf16[1960,128]{1,0:T(8,128)(2,1)S(1)}, bf16[1960,128]{1,0:T(8,128)(2,1)S(1)}, u32[]{:S(2)}, u32[]{:S(2)}) collective-permute-start(bf16[1960,128]{1,0:T(8,128)(2,1)S(1)} %add_convert_fusion), channel_id=1, source_target_pairs={{0,2},{1,3},{2,0},{3,1},{4,6},{5,7},{6,4},{7,5},{8,10},{9,11},{10,... | collective-permute-start | bytes 1505288 | tf_op jit(solution)/shard_map/ppermute | solution.py:298
  112.8 1.3 %convert_add_fusion.near_ref = f32[1960,128]{1,0:T(8,128)S(1)} fusion(f32[1960,128]{1,0:T(8,128)} %get-tuple-element.9, bf16[1960,128]{1,0:T(8,128)(2,1)S(1)} %collective-permute-done.10), kind=kLoop, calls=%fused_computation.2 | loop fusion | flops 501760 | bytes 2508800 | tf_op jit(solution)/shard_map/add | solution.py:302
  114.1 10.7 %collective-permute-done.12.chip_ref = bf16[1960,128]{1,0:T(8,128)(2,1)S(1)} collective-permute-done((bf16[1960,128]{1,0:T(8,128)(2,1)S(1)}, bf16[1960,128]{1,0:T(8,128)(2,1)S(1)}, u32[]{:S(2)}, u32[]{:S(2)}) %collective-permute-start.12) | collective-permute-done | bytes 501792 | tf_op jit(solution)/shard_map/ppermute | solution.py:298
  124.7 1.3 %finish.1 = f32[1960,128]{1,0:T(8,128)} custom-call(f32[1960,128]{1,0:T(8,128)S(1)} %convert_add_fusion.near_ref, bf16[1960,128]{1,0:T(8,128)(2,1)S(1)} %collective-permute-done.12.chip_ref), custom_call_target="tpu_custom_call" | custom-call | tf_op jit(solution)/shard_map/finish/pallas_call | solution.py:303
  (34 shorter events, 4.9 us)
Async XLA Ops:
  4.3 0.7 copy-start
  6.9 7.9 %collective-permute-start = (bf16[2,16,3072]{2,1,0:T(8,128)(2,1)S(1)}, bf16[2,16,3072]{2,1,0:T(8,128)(2,1)S(1)}, u32[]{:S(2)}, u32[]{:S(2)}) collective-permute-start(bf16[2,16,3072]{2,1,0:T(8,128)(2,1)S(1)} %get-tuple-element.16), channel_id=1, source_target_pairs={{0,4},{4,0},{8,12},{12,8},{16,20},{20,16},{24,28},{28,24},{1,5},{5... | collective-permute-start | bytes 589832 | tf_op jit(solution)/shard_map/ppermute | solution.py:210
  9.9 6.4 %collective-permute-start.5 = (bf16[2,16,3072]{2,1,0:T(8,128)(2,1)S(1)}, bf16[2,16,3072]{2,1,0:T(8,128)(2,1)S(1)}, u32[]{:S(2)}, u32[]{:S(2)}) collective-permute-start(bf16[2,16,3072]{2,1,0:T(8,128)(2,1)S(1)} %get-tuple-element.15), channel_id=1, source_target_pairs={{0,8},{4,12},{8,0},{12,4},{16,24},{20,28},{24,16},{28,20},{1,9},{5... | collective-permute-start | bytes 589832 | tf_op jit(solution)/shard_map/ppermute | solution.py:210
  16.3 4.7 %collective-permute-start.1 = (bf16[1,16,3072]{2,1,0:T(8,128)(2,1)S(1)}, bf16[1,16,3072]{2,1,0:T(8,128)(2,1)S(1)}, u32[]{:S(2)}, u32[]{:S(2)}) collective-permute-start(bf16[1,16,3072]{2,1,0:T(8,128)(2,1)S(1)} %broadcast_select_fusion.11), channel_id=1, source_target_pairs={{0,8},{4,12},{8,0},{12,4},{16,24},{20,28},{24,16},{28,20},{1,9},{5... | collective-permute-start | bytes 294920 | tf_op jit(solution)/shard_map/ppermute | solution.py:210
  18.0 4.7 %collective-permute-start.6 = (bf16[1,16,3072]{2,1,0:T(8,128)(2,1)S(1)}, bf16[1,16,3072]{2,1,0:T(8,128)(2,1)S(1)}, u32[]{:S(2)}, u32[]{:S(2)}) collective-permute-start(bf16[1,16,3072]{2,1,0:T(8,128)(2,1)S(1)} %broadcast_select_fusion.8), channel_id=1, source_target_pairs={{0,4},{4,0},{8,12},{12,8},{16,20},{20,16},{24,28},{28,24},{1,5},{5... | collective-permute-start | bytes 294920 | tf_op jit(solution)/shard_map/ppermute | solution.py:210
  22.7 8.2 %collective-permute-start.7 = (bf16[1,16,3072]{2,1,0:T(8,128)(2,1)S(1)}, bf16[1,16,3072]{2,1,0:T(8,128)(2,1)S(1)}, u32[]{:S(2)}, u32[]{:S(2)}) collective-permute-start(bf16[1,16,3072]{2,1,0:T(8,128)(2,1)S(1)} %get-tuple-element.31), channel_id=1, source_target_pairs={{0,16},{4,20},{8,24},{12,28},{16,0},{20,4},{24,8},{28,12},{1,17},{... | collective-permute-start | bytes 294920 | tf_op jit(solution)/shard_map/ppermute | solution.py:210
  25.4 7.0 %collective-permute-start.2 = (bf16[1,16,3072]{2,1,0:T(8,128)(2,1)S(1)}, bf16[1,16,3072]{2,1,0:T(8,128)(2,1)S(1)}, u32[]{:S(2)}, u32[]{:S(2)}) collective-permute-start(bf16[1,16,3072]{2,1,0:T(8,128)(2,1)S(1)} %get-tuple-element.32), channel_id=1, source_target_pairs={{0,16},{4,20},{8,24},{12,28},{16,0},{20,4},{24,8},{28,12},{1,17},{... | collective-permute-start | bytes 294920 | tf_op jit(solution)/shard_map/ppermute | solution.py:210
  31.0 4.7 %collective-permute-start.8 = (bf16[1,16,3072]{2,1,0:T(8,128)(2,1)S(1)}, bf16[1,16,3072]{2,1,0:T(8,128)(2,1)S(1)}, u32[]{:S(2)}, u32[]{:S(2)}) collective-permute-start(bf16[1,16,3072]{2,1,0:T(8,128)(2,1)S(1)} %add.40), channel_id=1, source_target_pairs={{0,4},{4,0},{8,12},{12,8},{16,20},{20,16},{24,28},{28,24},{1,5},{5... | collective-permute-start | bytes 294920 | tf_op jit(solution)/shard_map/ppermute | solution.py:210
  32.4 4.7 %collective-permute-start.3 = (bf16[1,16,3072]{2,1,0:T(8,128)(2,1)S(1)}, bf16[1,16,3072]{2,1,0:T(8,128)(2,1)S(1)}, u32[]{:S(2)}, u32[]{:S(2)}) collective-permute-start(bf16[1,16,3072]{2,1,0:T(8,128)(2,1)S(1)} %add.37), channel_id=1, source_target_pairs={{0,8},{4,12},{8,0},{12,4},{16,24},{20,28},{24,16},{28,20},{1,9},{5... | collective-permute-start | bytes 294920 | tf_op jit(solution)/shard_map/ppermute | solution.py:210
  35.7 5.7 %collective-permute-start.9 = (bf16[2,16,3072]{2,1,0:T(8,128)(2,1)S(1)}, bf16[2,16,3072]{2,1,0:T(8,128)(2,1)S(1)}, u32[]{:S(2)}, u32[]{:S(2)}) collective-permute-start(bf16[2,16,3072]{2,1,0:T(8,128)(2,1)S(1)} %pad_maximum_fusion.3), channel_id=1, source_target_pairs={{0,8},{4,12},{8,0},{12,4},{16,24},{20,28},{24,16},{28,20},{1,9},{5... | collective-permute-start | bytes 589832 | tf_op jit(solution)/shard_map/ppermute | solution.py:210
  37.1 5.7 %collective-permute-start.4 = (bf16[2,16,3072]{2,1,0:T(8,128)(2,1)S(1)}, bf16[2,16,3072]{2,1,0:T(8,128)(2,1)S(1)}, u32[]{:S(2)}, u32[]{:S(2)}) collective-permute-start(bf16[2,16,3072]{2,1,0:T(8,128)(2,1)S(1)} %pad_maximum_fusion.2), channel_id=1, source_target_pairs={{0,4},{4,0},{8,12},{12,8},{16,20},{20,16},{24,28},{28,24},{1,5},{5... | collective-permute-start | bytes 589832 | tf_op jit(solution)/shard_map/ppermute | solution.py:210
  42.9 0.7 copy-start.1
  108.0 1.9 %collective-permute-start.11 = (bf16[1960,128]{1,0:T(8,128)(2,1)S(1)}, bf16[1960,128]{1,0:T(8,128)(2,1)S(1)}, u32[]{:S(2)}, u32[]{:S(2)}) collective-permute-start(bf16[1960,128]{1,0:T(8,128)(2,1)S(1)} %get-tuple-element.12), channel_id=1, source_target_pairs={{0,1},{1,0},{2,3},{3,2},{4,5},{5,4},{6,7},{7,6},{8,9},{9,8},{10,11... | collective-permute-start | bytes 1505288 | tf_op jit(solution)/shard_map/ppermute | solution.py:298
  108.0 4.8 %collective-permute-start.10 = (bf16[1960,128]{1,0:T(8,128)(2,1)S(1)}, bf16[1960,128]{1,0:T(8,128)(2,1)S(1)}, u32[]{:S(2)}, u32[]{:S(2)}) collective-permute-start(bf16[1960,128]{1,0:T(8,128)(2,1)S(1)} %get-tuple-element.10), channel_id=1, source_target_pairs={{0,1},{1,0},{2,3},{3,2},{4,5},{5,4},{6,7},{7,6},{8,9},{9,8},{10,11... | collective-permute-start | bytes 1505288 | tf_op jit(solution)/shard_map/ppermute | solution.py:298
  111.2 13.5 %collective-permute-start.12 = (bf16[1960,128]{1,0:T(8,128)(2,1)S(1)}, bf16[1960,128]{1,0:T(8,128)(2,1)S(1)}, u32[]{:S(2)}, u32[]{:S(2)}) collective-permute-start(bf16[1960,128]{1,0:T(8,128)(2,1)S(1)} %add_convert_fusion), channel_id=1, source_target_pairs={{0,2},{1,3},{2,0},{3,1},{4,6},{5,7},{6,4},{7,5},{8,10},{9,11},{10,... | collective-permute-start | bytes 1505288 | tf_op jit(solution)/shard_map/ppermute | solution.py:298
